TPU v7x, 32 devices: a whole 2x2x4 slice. The times are simulated.
32 devices in a mesh: rows: 4 (over z), cols: 8 (over y, x, core).
Axes of the slice: x: 2, y: 2, z: 4, core: 2. Of those that a mesh axis runs over, the one named last changes fastest.
Arguments:
- blocks: bfloat16 [4, 8, 32, 256, 256], P('rows', 'cols'), may hold values from -600 to 600
- block_row: int32 [4, 8, 32], P('rows', 'cols'), may hold values from 0 to 15, as said below
- block_col: int32 [4, 8, 32], P('rows', 'cols'), may hold values from 0 to 15, as said below
- objective: float32 [32768, 48], P(('cols', 'rows')), may hold values from -3600 to 3600
- demand: float32 [16384, 48], P(('rows', 'cols')), may hold values from -2560 to 2560
- capacity: float32 [32768, 48], P(('cols', 'rows')), may hold values from 0.02 to 0.5
- step_size: float32 [3, 48], replicated, may hold values from 0.0055242716 to 0.011048543
- restart: int32 [3, 48], replicated, may hold values from 0 to 1
- primal_weight: float32 [48], replicated, may hold values from 0.5 to 2
Outputs:
- primal_flow: float32 [32768, 48], P(('cols', 'rows'))
- dual_prices: float32 [16384, 48], P(('rows', 'cols'))
- final_weight: float32 [48], replicated
Inputs may be any that keep to these rules, and one draw needn't show every extreme that they name: `block_row`: on each device the 32 blocks sit in distinct slots (block row, block column), listed in increasing order of block row * 16 + block column; every block row of a row group and every block column of a column group holds a block on every device. `block_col`: goes with block_row, as described there.
All inputs are finite; a program needn't handle non-finite values.
Results may differ from a plain program's by a relative error of at most 0.00097.
Values may be sent and summed in bfloat16 or wider, within the bound.
No kernel may reach another device: no remote copies, remote signals or barrier semaphores. Data moves between devices by JAX's collectives and lax.ppermute only.
A program may use at most 64 MiB of HBM per device.

v0:
```python
import jax
import jax.numpy as jnp
from jax import lax
from jax.sharding import PartitionSpec as P

BLK = 256
RB = 16
CB = 16
PASSES = 3
ITERS = 3


epsilon = 1e-06


def scale_blocks(matrix, row_factor, col_factor):
    return matrix.astype(jnp.float32) * row_factor[:, :, None] * col_factor[:, None, :]


def extreme_parts(scaled, rows_of, cols_of):
    magnitude = jnp.abs(scaled)
    row_hot = rows_of[:, None] == jnp.arange(RB)[None, :]
    col_hot = cols_of[:, None] == jnp.arange(CB)[None, :]
    row_part = jnp.max(
        jnp.where(row_hot[:, :, None], jnp.max(magnitude, axis=2)[:, None, :], 0.0), axis=0
    )
    col_part = jnp.max(
        jnp.where(col_hot[:, :, None], jnp.max(magnitude, axis=1)[:, None, :], 0.0), axis=0
    )
    return (row_part.reshape(RB * BLK), col_part.reshape(CB * BLK))


def on_device(
    blocks, block_row, block_col, objective, demand, capacity, step_size, restart, primal_weight
):
    highest = lax.Precision.HIGHEST
    matrix = blocks[0, 0]
    rows_of = block_row[0, 0]
    cols_of = block_col[0, 0]
    row_count = lax.axis_size("rows")
    col_count = lax.axis_size("cols")
    row_place = lax.axis_index("rows")
    col_place = lax.axis_index("cols")
    scenarios = objective.shape[1]
    row_scale = jnp.ones((RB * BLK,), jnp.float32)
    col_scale = jnp.ones((CB * BLK,), jnp.float32)
    for sweep in range(PASSES):
        scaled = scale_blocks(
            matrix, row_scale.reshape(RB, BLK)[rows_of], col_scale.reshape(CB, BLK)[cols_of]
        )
        row_part, col_part = extreme_parts(scaled, rows_of, cols_of)
        row_max = lax.pmax(row_part, "cols")
        col_max = lax.pmax(col_part, "rows")
        row_scale = row_scale / jnp.sqrt(row_max + epsilon)
        col_scale = col_scale / jnp.sqrt(col_max + epsilon)
    final_matrix = scale_blocks(
        matrix, row_scale.reshape(RB, BLK)[rows_of], col_scale.reshape(CB, BLK)[cols_of]
    ).astype(jnp.bfloat16)
    row_onehot = (rows_of[:, None] == jnp.arange(RB)[None, :]).astype(jnp.float32)
    col_onehot = (cols_of[:, None] == jnp.arange(CB)[None, :]).astype(jnp.float32)
    primal_rows = CB * BLK // row_count
    dual_rows = RB * BLK // col_count
    col_piece = lax.dynamic_slice_in_dim(col_scale, row_place * primal_rows, primal_rows, 0)
    row_piece = lax.dynamic_slice_in_dim(row_scale, col_place * dual_rows, dual_rows, 0)
    scaled_cost = objective * col_piece[:, None]
    scaled_demand = demand * row_piece[:, None]
    upper = capacity / col_piece[:, None]
    primal = jnp.zeros((primal_rows, scenarios), jnp.float32)
    dual = jnp.zeros((dual_rows, scenarios), jnp.float32)
    anchor_primal = primal
    anchor_dual = dual
    sum_primal = primal
    sum_dual = dual
    weight_total = jnp.zeros((scenarios,), jnp.float32)
    weight = primal_weight
    for iteration in range(ITERS):
        stride = step_size[iteration]
        primal_step = stride / weight
        dual_step = stride * weight
        if iteration == 0:
            gradient = scaled_cost
        else:
            gathered = lax.all_gather(dual.astype(jnp.bfloat16), "cols", axis=0, tiled=True)
            picked = gathered.reshape(RB, BLK, scenarios)[rows_of]
            products = jnp.einsum(
                "nij,nis->njs", final_matrix, picked, preferred_element_type=jnp.float32
            )
            partial_sum = jnp.einsum(
                "nc,njs->cjs", col_onehot, products, precision=highest
            ).reshape(CB * BLK, scenarios)
            gradient = scaled_cost - lax.psum_scatter(
                partial_sum, "rows", scatter_dimension=0, tiled=True
            )
        new_primal = jnp.clip(primal - primal_step[None, :] * gradient, 0.0, upper)
        extrapolated = (2.0 * new_primal - primal).astype(jnp.bfloat16)
        forward_gathered = lax.all_gather(extrapolated, "rows", axis=0, tiled=True)
        forward_picked = forward_gathered.reshape(CB, BLK, scenarios)[cols_of]
        forward_products = jnp.einsum(
            "nij,njs->nis", final_matrix, forward_picked, preferred_element_type=jnp.float32
        )
        forward_partial_sum = jnp.einsum(
            "nr,nis->ris", row_onehot, forward_products, precision=highest
        ).reshape(RB * BLK, scenarios)
        summed = lax.psum(forward_partial_sum, "cols")
        image = lax.dynamic_slice_in_dim(summed, col_place * dual_rows, dual_rows, 0)
        dual = dual + dual_step[None, :] * (scaled_demand - image)
        primal = new_primal
        sum_primal = sum_primal + stride[None, :] * primal
        sum_dual = sum_dual + stride[None, :] * dual
        weight_total = weight_total + stride
        mean_primal = sum_primal / weight_total[None, :]
        mean_dual = sum_dual / weight_total[None, :]
        primal_move = mean_primal - anchor_primal
        dual_move = mean_dual - anchor_dual
        drift_primal, drift_dual = lax.psum(
            (jnp.sum(primal_move * primal_move, axis=0), jnp.sum(dual_move * dual_move, axis=0)),
            ("rows", "cols"),
        )
        candidate = jnp.sqrt(weight * jnp.sqrt((drift_dual + epsilon) / (drift_primal + epsilon)))
        restart_now = restart[iteration] == 1
        weight = jnp.where(restart_now, candidate, weight)
        primal = jnp.where(restart_now[None, :], mean_primal, primal)
        dual = jnp.where(restart_now[None, :], mean_dual, dual)
        anchor_primal = jnp.where(restart_now[None, :], mean_primal, anchor_primal)
        anchor_dual = jnp.where(restart_now[None, :], mean_dual, anchor_dual)
        sum_primal = jnp.where(restart_now[None, :], 0.0, sum_primal)
        sum_dual = jnp.where(restart_now[None, :], 0.0, sum_dual)
        weight_total = jnp.where(restart_now, 0.0, weight_total)
    return (primal, dual, weight)


def solution(mesh):
    in_specs = (
        P("rows", "cols", None, None, None),
        P("rows", "cols", None),
        P("rows", "cols", None),
        P(("cols", "rows"), None),
        P(("rows", "cols"), None),
        P(("cols", "rows"), None),
        P(),
        P(),
        P(),
    )
    out_specs = (P(("cols", "rows"), None), P(("rows", "cols"), None), P())
    return jax.shard_map(
        on_device, mesh=mesh, in_specs=in_specs, out_specs=out_specs, check_vma=False
    )
```

profile of v0, /device:TPU:0, one launch (start us, length us, event | category | flops | bytes accessed | tf_op | source)
XLA Modules:
  0.0 553.9 jit_solution(6566551448365022617)
XLA Ops:
  12.2 5.4 fusion.2
  17.7 25.5 %pmax.43 = f32[4096]{0:T(1024)S(1)} all-reduce(f32[4096]{0:T(1024)S(1)} %bitcast.151), channel_id=1, replica_groups=mesh['rows'=4,'cols'=8] {'cols'}, use_global_device_ids=true, to_apply=%region_5.6 | all-reduce | flops 4096 | bytes 32768 | tf_op jit(solution)/shard_map/pmax | solution.py:52
  44.0 19.0 %pmax.42 = f32[4096]{0:T(1024)S(1)} all-reduce(f32[4096]{0:T(1024)S(1)} %bitcast.153), channel_id=1, replica_groups=mesh['rows'=4,'cols'=8] {'rows'}, use_global_device_ids=true, to_apply=%region_2.3 | all-reduce | flops 4096 | bytes 32768 | tf_op jit(solution)/shard_map/pmax | solution.py:53
  63.6 5.4 fusion.6
  69.2 22.3 %pmax.45 = f32[4096]{0:T(1024)S(1)} all-reduce(f32[4096]{0:T(1024)S(1)} %bitcast.155), channel_id=1, replica_groups=mesh['rows'=4,'cols'=8] {'cols'}, use_global_device_ids=true, to_apply=%region_11.12 | all-reduce | flops 4096 | bytes 32768 | tf_op jit(solution)/shard_map/pmax | solution.py:52
  92.3 15.5 %pmax.44 = f32[4096]{0:T(1024)S(1)} all-reduce(f32[4096]{0:T(1024)S(1)} %bitcast.157), channel_id=1, replica_groups=mesh['rows'=4,'cols'=8] {'rows'}, use_global_device_ids=true, to_apply=%region_8.9 | all-reduce | flops 4096 | bytes 32768 | tf_op jit(solution)/shard_map/pmax | solution.py:53
  108.5 5.4 fusion.10
  114.0 22.3 %pmax.47 = f32[4096]{0:T(1024)S(1)} all-reduce(f32[4096]{0:T(1024)S(1)} %bitcast.158), channel_id=1, replica_groups=mesh['rows'=4,'cols'=8] {'cols'}, use_global_device_ids=true, to_apply=%region_17.18 | all-reduce | flops 4096 | bytes 32768 | tf_op jit(solution)/shard_map/pmax | solution.py:52
  136.5 16.3 %pmax.46 = f32[4096]{0:T(1024)S(1)} all-reduce(f32[4096]{0:T(1024)S(1)} %bitcast.159), channel_id=1, replica_groups=mesh['rows'=4,'cols'=8] {'rows'}, use_global_device_ids=true, to_apply=%region_14.15 | all-reduce | flops 4096 | bytes 32768 | tf_op jit(solution)/shard_map/pmax | solution.py:53
  154.3 14.5 %all_gather.15 = bf16[4096,48]{0,1:T(8,128)(2,1)S(1)} all-gather(bf16[1024,48]{0,1:T(8,128)(2,1)S(1)} %multiply_convert_fusion), channel_id=1, replica_groups=mesh['rows'=4,'cols'=8] {'rows'}, dimensions={0}, use_global_device_ids=true | all-gather | bytes 491520 | tf_op jit(solution)/shard_map/all_gather | solution.py:96
  169.5 4.0 fusion.32
  176.6 52.0 %all-reduce.7.cloned.1.call-done = f32[4096,48]{0,1:T(8,128)} async-done(((f32[4096,48]{0,1:T(8,128)}), f32[4096,48]{0,1:T(8,128)}) %all-reduce.7.cloned.1.call-update) | async-done | bytes 786448 | tf_op jit(solution)/shard_map/psum | solution.py:104
  229.8 8.8 %all_gather.16 = bf16[4096,48]{0,1:T(8,128)(2,1)S(1)} all-gather(bf16[512,48]{0,1:T(8,128)(2,1)S(1)} %fusion.34), channel_id=1, replica_groups=mesh['rows'=4,'cols'=8] {'cols'}, dimensions={0}, use_global_device_ids=true | all-gather | bytes 442368 | tf_op jit(solution)/shard_map/all_gather | solution.py:83
  239.3 4.0 fusion.26
  246.2 40.1 %all-reduce.2 = (f32[48]{0:T(128)S(1)}, f32[48]{0:T(128)S(1)}) all-reduce(f32[48]{0:T(128)S(1)} %get-tuple-element.35, f32[48]{0:T(128)S(1)} %get-tuple-element.33), channel_id=1, replica_groups=mesh['rows'=4,'cols'=8] {'rows','cols'}, use_global_device_ids=true, to_apply=%region_22.23 | all-reduce | flops 96 | bytes 768 | tf_op jit(solution)/shard_map/psum | solution.py:115
  287.7 15.0 %all_gather.17 = bf16[4096,48]{0,1:T(8,128)(2,1)S(1)} all-gather(bf16[1024,48]{0,1:T(8,128)(2,1)S(1)} %subtract_convert_fusion.1), channel_id=1, replica_groups=mesh['rows'=4,'cols'=8] {'rows'}, dimensions={0}, use_global_device_ids=true | all-gather | bytes 491520 | tf_op jit(solution)/shard_map/all_gather | solution.py:96
  303.3 4.0 fusion.28
  310.3 56.3 %all-reduce.9.cloned.1.call-done = f32[4096,48]{0,1:T(8,128)} async-done(((f32[4096,48]{0,1:T(8,128)}), f32[4096,48]{0,1:T(8,128)}) %all-reduce.9.cloned.1.call-update) | async-done | bytes 786448 | tf_op jit(solution)/shard_map/psum | solution.py:104
  367.8 9.0 %all_gather.18 = bf16[4096,48]{0,1:T(8,128)(2,1)S(1)} all-gather(bf16[512,48]{0,1:T(8,128)(2,1)S(1)} %fusion.35), channel_id=1, replica_groups=mesh['rows'=4,'cols'=8] {'cols'}, dimensions={0}, use_global_device_ids=true | all-gather | bytes 442368 | tf_op jit(solution)/shard_map/all_gather | solution.py:83
  384.4 40.3 %all-reduce.1 = (f32[48]{0:T(128)S(1)}, f32[48]{0:T(128)S(1)}) all-reduce(f32[48]{0:T(128)S(1)} %get-tuple-element.28, f32[48]{0:T(128)S(1)} %get-tuple-element.25), channel_id=1, replica_groups=mesh['rows'=4,'cols'=8] {'rows','cols'}, use_global_device_ids=true, to_apply=%region_28.29 | all-reduce | flops 96 | bytes 768 | tf_op jit(solution)/shard_map/psum | solution.py:115
  426.8 14.9 %all_gather.19 = bf16[4096,48]{0,1:T(8,128)(2,1)S(1)} all-gather(bf16[1024,48]{0,1:T(8,128)(2,1)S(1)} %get-tuple-element.37), channel_id=1, replica_groups=mesh['rows'=4,'cols'=8] {'rows'}, dimensions={0}, use_global_device_ids=true | all-gather | bytes 491520 | tf_op jit(solution)/shard_map/all_gather | solution.py:96
  442.3 4.0 fusion.24
  449.3 56.5 %all-reduce.11.cloned.1.call-done = f32[4096,48]{0,1:T(8,128)} async-done(((f32[4096,48]{0,1:T(8,128)}), f32[4096,48]{0,1:T(8,128)}) %all-reduce.11.cloned.1.call-update) | async-done | bytes 786448 | tf_op jit(solution)/shard_map/psum | solution.py:104
  507.0 39.2 %all-reduce = (f32[48]{0:T(128)S(1)}, f32[48]{0:T(128)S(1)}) all-reduce(f32[48]{0:T(128)S(1)} %get-tuple-element.18, f32[48]{0:T(128)S(1)} %get-tuple-element.15), channel_id=1, replica_groups=mesh['rows'=4,'cols'=8] {'rows','cols'}, use_global_device_ids=true, to_apply=%region_34.35 | all-reduce | flops 96 | bytes 768 | tf_op jit(solution)/shard_map/psum | solution.py:115
  (111 shorter events, 40.0 us)
Async XLA Ops:
  7.2 221.5 %all-reduce.7.cloned.1.call-start = ((), (), s32[]{:S(2)}) async-start(), calls=%async_computation.2 | async-start | bytes 1572864 | tf_op jit(solution)/shard_map/psum | solution.py:104
  69.0 85.1 %copy-start = (f32[1024,48]{0,1:T(8,128)S(1)}, f32[1024,48]{0,1:T(8,128)}, u32[]{:S(2)}) copy-start(f32[1024,48]{0,1:T(8,128)} %param.12) | copy-start | bytes 589828
  69.0 85.1 %copy-start.1 = (f32[1024,48]{0,1:T(8,128)S(1)}, f32[1024,48]{0,1:T(8,128)}, u32[]{:S(2)}) copy-start(f32[1024,48]{0,1:T(8,128)} %param.14) | copy-start | bytes 589828
  169.5 4.0 copy-start.3
  173.5 3.1 copy-start.5
  173.5 55.1 %copy-start.2 = (f32[512,48]{0,1:T(8,128)S(1)}, f32[512,48]{0,1:T(8,128)}, u32[]{:S(2)}) copy-start(f32[512,48]{0,1:T(8,128)} %param.13) | copy-start | bytes 294916
  176.5 109.9 %reduce-scatter.3.cloned.1.call-start = ((), (), s32[]{:S(2)}) async-start(), calls=%async_computation.3 | async-start | bytes 983040 | tf_op jit(solution)/shard_map/reduce_scatter | solution.py:91
  239.2 4.0 copy-start.4
  243.2 43.1 %copy-start.6 = (f32[3,48]{1,0:T(4,128)S(1)}, f32[3,48]{1,0:T(4,128)}, u32[]{:S(2)}) copy-start(f32[3,48]{1,0:T(4,128)} %param.15) | copy-start | bytes 1732
  243.2 43.1 %copy-start.7 = (f32[48]{0:T(128)S(1)}, f32[48]{0:T(128)}, u32[]{:S(2)}) copy-start(f32[48]{0:T(128)} %param.17) | copy-start | bytes 580
  246.1 120.5 %all-reduce.9.cloned.1.call-start = ((), (), s32[]{:S(2)}) async-start(), calls=%async_computation.4 | async-start | bytes 1572864 | tf_op jit(solution)/shard_map/psum | solution.py:104
  310.3 114.4 %reduce-scatter.5.cloned.1.call-start = ((), (), s32[]{:S(2)}) async-start(), calls=%async_computation.5 | async-start | bytes 983040 | tf_op jit(solution)/shard_map/reduce_scatter | solution.py:91
  384.3 121.5 %all-reduce.11.cloned.1.call-start = ((), (), s32[]{:S(2)}) async-start(), calls=%async_computation.6 | async-start | bytes 1572864 | tf_op jit(solution)/shard_map/psum | solution.py:104
Sparse Core Ops, SparseCore 0:
  176.6 51.9 all-reduce.6
  246.3 23.5 reduce-scatter.2
  310.4 56.1 all-reduce.8
  384.5 23.5 reduce-scatter.4
  449.4 56.3 all-reduce.10
where the time goes:
time: 555 us; the launch traced here: 554 us
  blocking collectives  303 us (55%)
  waiting for transfers between devices  165 us (30%)
  other arithmetic  29 us (5%)
  matrix products  27.6 us (5%)
  local copies, waits for them, and re-layouts  15.1 us (3%)
  between operations  14.3 us (3%)
    psum x3, waiting for transfers between devices, on_device(): summed = lax.psum(forward_partial_sum, 'cols')  165 us
    psum x3, blocking collectives, on_device(): lax.psum((jnp.sum(primal_move * primal_move, axis=0), jnp.sum(dual_move *...  120 us
    pmax x3, blocking collectives, on_device(): row_max = lax.pmax(row_part, 'cols')  70.1 us
    pmax x3, blocking collectives, on_device(): col_max = lax.pmax(col_part, 'rows')  50.8 us
    all_gather x3, blocking collectives, on_device(): forward_gathered = lax.all_gather(extrapolated, 'rows', axis=0, tiled=True)  44.4 us
    all_gather x2, blocking collectives, on_device(): lax.all_gather(dual.astype(jnp.bfloat16), 'cols', axis=0, tiled=True)  17.8 us
    reduce_max x3, other arithmetic, extreme_parts(): jnp.max(magnitude, axis=2)[:, None, :]  16.1 us
    dot_general x3, matrix products, on_device(): jnp.einsum('nij,njs->nis', final_matrix, forward_picked, preferred_elemen...  12.1 us
  transfers between devices with their start and end apart: 5, of which 3 were waited for; matrix products, arithmetic and copies ran while one was open for 0% of the time, Pallas kernels for 0%

commit v1 on v0

v1 whole, which is shorter than its diff:
```python
import functools

import jax
import jax.numpy as jnp
from jax import lax
from jax.experimental import pallas as pl
from jax.experimental.pallas import tpu as pltpu
from jax.sharding import PartitionSpec as P

BLK = 256
RB = 16
CB = 16
PASSES = 3
ITERS = 3
LANES = 128
CHUNKS = 8

epsilon = 1e-06
F32 = jnp.float32
BF16 = jnp.bfloat16
VMEM = pl.BlockSpec(memory_space=pltpu.VMEM)
SMEM = pl.BlockSpec(memory_space=pltpu.SMEM)
ANY = pl.BlockSpec(memory_space=pl.ANY)
PARAMS = pltpu.CompilerParams(vmem_limit_bytes=32 * 1024 * 1024)


def swap(value, axis, offset):
    count = lax.axis_size(axis)
    return lax.ppermute(value, axis, [(i, i ^ offset) for i in range(count)])


def start_loads(hbm_ref, vmem_ref, sems):
    size = hbm_ref.shape[0] // CHUNKS
    copies = []
    for chunk in range(CHUNKS):
        part = pl.ds(chunk * size, size)
        copy = pltpu.make_async_copy(hbm_ref.at[part], vmem_ref.at[part], sems.at[chunk])
        copy.start()
        copies.append(copy)
    return copies


def for_each_block(copies, count, body):
    size = count // CHUNKS
    for chunk in range(CHUNKS):
        copies[chunk].wait()

        @pl.loop(chunk * size, (chunk + 1) * size)
        def _(n):
            body(n)


def unit_row(ref, unit):
    row = ref[pl.ds(unit // 2, 1), :]
    return jnp.where(unit % 2 == 0, row[:, :LANES], row[:, LANES:])


def lane_sum(tile):
    return jnp.broadcast_to(jnp.sum(tile, axis=1, keepdims=True), tile.shape)


def pack_pair(first, second):
    lane = lax.broadcasted_iota(jnp.int32, first.shape, 1)
    out = jnp.zeros_like(first)
    for place, rest in ((0, first), (3, second)):
        for part in range(3):
            rounded = rest.astype(BF16).astype(F32)
            out = jnp.where(lane == place + part, rounded, out)
            rest = rest - rounded
    return out.astype(BF16)


def unpack_pair(total):
    lane = lax.broadcasted_iota(jnp.int32, total.shape, 1)
    first = lane_sum(jnp.where(lane < 3, total, 0.0))
    second = lane_sum(jnp.where((lane >= 3) & (lane < 6), total, 0.0))
    return first, second


def next_weight(weight, restart, drift_dual, drift_primal):
    candidate = jnp.sqrt(
        weight * jnp.sqrt((drift_dual + epsilon) / (drift_primal + epsilon))
    )
    return jnp.where(restart == 1, candidate, weight)


def first_max_kernel(rows_ref, cols_ref, a_hbm, row_out, col_out, a, sems, racc, cacc):
    copies = start_loads(a_hbm, a, sems)
    racc[...] = jnp.zeros_like(racc)
    cacc[...] = jnp.zeros_like(cacc)

    def block(n):
        r, c = rows_ref[n], cols_ref[n]
        col = cacc[c]
        for t in range(BLK // 32):
            part = pl.ds(t * 32, 32)
            mag = jnp.abs(a[n, part, :])
            col = jnp.maximum(col, jnp.maximum(mag[:16], mag[16:]))
            racc[r, part, :] = jnp.maximum(
                racc[r, part, :], jnp.maximum(mag[:, :LANES], mag[:, LANES:])
            )
        cacc[c] = col

    for_each_block(copies, a.shape[0], block)
    for b in range(RB):
        flipped = racc[b].astype(F32).T
        row_out[b : b + 1, :] = jnp.max(flipped, axis=0, keepdims=True)
        col_out[b : b + 1, :] = jnp.max(cacc[b].astype(F32), axis=0, keepdims=True)


def max_kernel(
    rows_ref, cols_ref, a_hbm, r_ref, c_ref, row_out, col_out, a, sems, rb, racc, cacc
):
    copies = start_loads(a_hbm, a, sems)
    racc[...] = jnp.zeros_like(racc)
    cacc[...] = jnp.zeros_like(cacc)
    spread_rows(r_ref, rb)

    def block(n):
        r, c = rows_ref[n], cols_ref[n]
        factor = c_ref[pl.ds(c, 1), :]
        col = cacc[c]
        for t in range(BLK // 32):
            part = pl.ds(t * 32, 32)
            mag = jnp.abs(a[n, part, :].astype(F32))
            tall = rb[r, part, :]
            by_row = jnp.concatenate([mag[:, :LANES] * tall, mag[:, LANES:] * tall], 1)
            by_col = mag * factor
            for q in range(4):
                col = jnp.maximum(col, by_row[8 * q : 8 * q + 8])
            racc[r, part, :] = jnp.maximum(
                racc[r, part, :], jnp.maximum(by_col[:, :LANES], by_col[:, LANES:])
            )
        cacc[c] = col

    for_each_block(copies, a.shape[0], block)
    for b in range(RB):
        row_out[b : b + 1, :] = (
            jnp.max(racc[b].T, axis=0, keepdims=True) * r_ref[b : b + 1, :]
        )
        col_out[b : b + 1, :] = (
            jnp.max(cacc[b], axis=0, keepdims=True) * c_ref[b : b + 1, :]
        )


def spread_rows(r_ref, rb):
    for b in range(RB):
        rb[b] = jnp.broadcast_to(r_ref[b : b + 1, :], (LANES, BLK)).T


def row_col_max(rows_of, cols_of, matrix, row_scale, col_scale):
    count = matrix.shape[0]
    first = row_scale is None
    kind = BF16 if first else F32
    scratch = [
        pltpu.VMEM(matrix.shape, BF16),
        pltpu.SemaphoreType.DMA((CHUNKS,)),
    ]
    if not first:
        scratch.append(pltpu.VMEM((RB, BLK, LANES), F32))
    scratch += [
        pltpu.VMEM((RB, BLK, LANES), kind),
        pltpu.VMEM((CB, 16 if first else 8, BLK), kind),
    ]
    operands = (rows_of, cols_of, matrix) + (() if first else (row_scale, col_scale))
    return pl.pallas_call(
        first_max_kernel if first else max_kernel,
        out_shape=(
            jax.ShapeDtypeStruct((RB, BLK), F32),
            jax.ShapeDtypeStruct((CB, BLK), F32),
        ),
        in_specs=[SMEM, SMEM, ANY] + ([] if first else [VMEM, VMEM]),
        out_specs=(VMEM, VMEM),
        scratch_shapes=scratch,
        compiler_params=PARAMS,
        name="first_max" if first else "row_col_max",
    )(*operands)


def exchange_max(row_part, col_part):
    row_step, col_step = 1, 1
    while row_step < lax.axis_size("cols") or col_step < lax.axis_size("rows"):
        row_next = col_next = None
        if row_step < lax.axis_size("cols"):
            row_next = swap(row_part, "cols", row_step)
        if col_step < lax.axis_size("rows"):
            col_next = swap(col_part, "rows", col_step)
        if row_next is not None:
            row_part = jnp.maximum(row_part, row_next)
        if col_next is not None:
            col_part = jnp.maximum(col_part, col_next)
        row_step, col_step = 2 * row_step, 2 * col_step
    return row_part, col_part


def place_pieces(pieces, owners, out):
    for piece, owner in zip(pieces, owners):
        units = piece.shape[1] // LANES
        for k in range(units):
            out[owner * units + k] = piece[:, k * LANES : (k + 1) * LANES]


def fetch_units(ref, first, count):
    return jnp.concatenate([ref[first + k] for k in range(count)], axis=1)


def forward_kernel(scaling, pieces, *refs):
    rows_ref, cols_ref, m_hbm = refs[:3]
    refs = refs[3:]
    if scaling:
        r_ref, c_ref = refs[:2]
        refs = refs[2:]
    piece_refs, refs = refs[:pieces], refs[pieces:]
    if scaling:
        keep, send, m_out, m, sems, x, acc, rb, out_sems = refs
    else:
        keep, send, m, sems, x, acc = refs
    copies = start_loads(m_hbm, m, sems)
    me = lax.axis_index("rows")
    place_pieces(
        [ref[...] for ref in piece_refs], [me ^ o for o in range(pieces)], x
    )
    acc[...] = jnp.zeros_like(acc)
    if scaling:
        spread_rows(r_ref, rb)

    def block(n):
        r, c = rows_ref[n], cols_ref[n]
        if scaling:
            factor = c_ref[pl.ds(c, 1), :]
            for t in range(BLK // 32):
                part = pl.ds(t * 32, 32)
                raw = m[n, part, :].astype(F32)
                tall = rb[r, part, :]
                scaled = jnp.concatenate([raw[:, :LANES] * tall, raw[:, LANES:] * tall], 1)
                m[n, part, :] = (scaled * factor).astype(BF16)
        product = lax.dot_general(
            fetch_units(x, 2 * c, 2),
            m[n],
            (((1,), (1,)), ((), ())),
            preferred_element_type=F32,
        )
        acc[2 * r] += product[:, :LANES]
        acc[2 * r + 1] += product[:, LANES:]

    for_each_block(copies, m.shape[0], block)
    outs = []
    if scaling:
        size = m.shape[0] // CHUNKS
        for chunk in range(CHUNKS):
            part = pl.ds(chunk * size, size)
            copy = pltpu.make_async_copy(m.at[part], m_out.at[part], out_sems.at[chunk])
            copy.start()
            outs.append(copy)
    place = lax.axis_index("cols")
    chip, core = place // 2, place % 2
    units = keep.shape[2] // LANES
    for o in range(keep.shape[0]):
        shard = 2 * (chip ^ o)
        for k in range(units):
            span = pl.ds(k * LANES, LANES)
            keep[o, :, span] = acc[(shard + core) * units + k]
            send[o, :, span] = acc[(shard + 1 - core) * units + k].astype(BF16)
    for copy in outs:
        copy.wait()


def forward(rows_of, cols_of, matrix, pieces, scales=None):
    scenarios = pieces[0].shape[0]
    chips = lax.axis_size("cols") // 2
    width = RB * BLK // lax.axis_size("cols")
    scaling = scales is not None
    out_shape = [
        jax.ShapeDtypeStruct((chips, scenarios, width), F32),
        jax.ShapeDtypeStruct((chips, scenarios, width), BF16),
    ]
    out_specs = [VMEM, VMEM]
    scratch = [
        pltpu.VMEM(matrix.shape, BF16),
        pltpu.SemaphoreType.DMA((CHUNKS,)),
        pltpu.VMEM((CB * BLK // LANES, scenarios, LANES), BF16),
        pltpu.VMEM((RB * BLK // LANES, scenarios, LANES), F32),
    ]
    if scaling:
        out_shape.append(jax.ShapeDtypeStruct(matrix.shape, BF16))
        out_specs.append(ANY)
        scratch += [
            pltpu.VMEM((RB, BLK, LANES), F32),
            pltpu.SemaphoreType.DMA((CHUNKS,)),
        ]
    return pl.pallas_call(
        functools.partial(forward_kernel, scaling, len(pieces)),
        out_shape=out_shape,
        in_specs=[SMEM, SMEM, ANY] + [VMEM] * (len(pieces) + 2 * scaling),
        out_specs=out_specs,
        scratch_shapes=scratch,
        compiler_params=PARAMS,
        name="scale_and_forward" if scaling else "forward",
    )(rows_of, cols_of, matrix, *(scales or ()), *pieces)


def backward_kernel(pieces, *refs):
    rows_ref, cols_ref, m_hbm = refs[:3]
    piece_refs, refs = refs[3 : 3 + pieces], refs[3 + pieces :]
    keep, sends, (m, sems, y, acc) = refs[0], refs[1:-4], refs[-4:]
    copies = start_loads(m_hbm, m, sems)
    place = lax.axis_index("cols")
    chip, core = place // 2, place % 2
    width = RB * BLK // lax.axis_size("cols")
    total = None
    for o, ref in enumerate(piece_refs):
        for half in range(2):
            owner = 2 * (chip ^ o) + (core ^ half)
            place_pieces([ref[half, :, :width]], [owner], y)
            tail = ref[half, :, width:].astype(F32)
            total = tail if total is None else total + tail
    acc[...] = jnp.zeros_like(acc)

    def block(n):
        r, c = rows_ref[n], cols_ref[n]
        product = lax.dot_general(
            fetch_units(y, 2 * r, 2),
            m[n],
            (((1,), (0,)), ((), ())),
            preferred_element_type=F32,
        )
        acc[2 * c] += product[:, :LANES]
        acc[2 * c + 1] += product[:, LANES:]

    for_each_block(copies, m.shape[0], block)
    me = lax.axis_index("rows")
    units = keep.shape[1] // LANES - 1
    tail = pack_pair(*unpack_pair(total))
    for o, out in enumerate((keep,) + tuple(sends)):
        for k in range(units):
            out[:, pl.ds(k * LANES, LANES)] = acc[(me ^ o) * units + k].astype(out.dtype)
        out[:, pl.ds(units * LANES, LANES)] = tail.astype(out.dtype)


def backward(rows_of, cols_of, matrix, pieces):
    scenarios = pieces[0].shape[1]
    width = CB * BLK // lax.axis_size("rows") + LANES
    shape = (scenarios, width)
    others = lax.axis_size("rows") - 1
    return pl.pallas_call(
        functools.partial(backward_kernel, len(pieces)),
        out_shape=[jax.ShapeDtypeStruct(shape, F32)]
        + [jax.ShapeDtypeStruct(shape, BF16)] * others,
        in_specs=[SMEM, SMEM, ANY] + [VMEM] * len(pieces),
        out_specs=[VMEM] * (1 + others),
        scratch_shapes=[
            pltpu.VMEM(matrix.shape, BF16),
            pltpu.SemaphoreType.DMA((CHUNKS,)),
            pltpu.VMEM((RB * BLK // LANES, scenarios, LANES), BF16),
            pltpu.VMEM((CB * BLK // LANES, scenarios, LANES), F32),
        ],
        compiler_params=PARAMS,
        name="backward",
    )(rows_of, cols_of, matrix, *pieces)


def settle(again, stride, totals, new, total, anchor):
    total = total + stride * new
    mean = total / totals
    move = mean - anchor
    return (
        jnp.where(again, mean, new),
        jnp.where(again, 0.0, total),
        jnp.where(again, mean, anchor),
        move * move,
    )


def primal_kernel(first, terms, *refs):
    obj, cap, c_ref, stride_ref, again_ref, weight_ref = refs[:6]
    refs = refs[6:]
    if not first:
        before_ref, wt_ref, state, sums, anchors = refs[:5]
        term_refs = refs[5 : 5 + terms]
        refs = refs[5 + terms :]
    state_out, sums_out, anchors_out, ext, drift, weight_out = refs
    width = obj.shape[1]
    weight = weight_ref[...]
    stride = stride_ref[...]
    again = again_ref[...] == 1
    totals = stride
    if not first:
        totals = wt_ref[...] + stride
        tail = sum(ref[:, width:].astype(F32) for ref in term_refs)
        weight = next_weight(weight, before_ref[...], *unpack_pair(tail))
    weight_out[...] = weight
    step = stride / weight
    place = lax.axis_index("rows")
    units = width // LANES
    moved = jnp.zeros_like(weight)
    for k in range(units):
        span = pl.ds(k * LANES, LANES)
        scale = unit_row(c_ref, place * units + k)
        gradient = obj[:, span] * scale
        upper = cap[:, span] / scale
        if first:
            old = total = anchor = jnp.zeros_like(gradient)
        else:
            old, total, anchor = state[:, span], sums[:, span], anchors[:, span]
            product = sum(ref[:, span].astype(F32) for ref in term_refs)
            gradient = gradient - product
        new = jnp.minimum(jnp.maximum(old - step * gradient, 0.0), upper)
        ext[:, span] = (2.0 * new - old).astype(BF16)
        new, total, anchor, square = settle(again, stride, totals, new, total, anchor)
        state_out[:, span] = new
        sums_out[:, span] = total
        anchors_out[:, span] = anchor
        moved = moved + square
    drift[...] = moved


def primal_update(obj, cap, col_scale, stride, again, weight, rest=None, terms=()):
    shape = obj.shape
    tile = jax.ShapeDtypeStruct((shape[0], LANES), F32)
    whole = jax.ShapeDtypeStruct(shape, F32)
    operands = (obj, cap, col_scale, stride, again, weight) + tuple(rest or ()) + tuple(terms)
    return pl.pallas_call(
        functools.partial(primal_kernel, rest is None, len(terms)),
        out_shape=[whole, whole, whole, jax.ShapeDtypeStruct(shape, BF16), tile, tile],
        in_specs=[VMEM] * len(operands),
        out_specs=[VMEM] * 6,
        compiler_params=PARAMS,
        name="primal_update",
    )(*operands)


def dual_kernel(first, last, terms, *refs):
    demand, r_ref, stride_ref, again_ref, weight_ref, drift_ref = refs[:6]
    refs = refs[6:]
    if not first:
        wt_ref, state, sums, anchors = refs[:4]
        refs = refs[4:]
    term_refs, refs = refs[:terms], refs[terms:]
    state_out, refs = refs[0], refs[1:]
    if last:
        (packed,) = refs
    else:
        sums_out, anchors_out, wt_out, packed = refs
    width = demand.shape[1]
    stride = stride_ref[...]
    again = again_ref[...] == 1
    totals = stride if first else wt_ref[...] + stride
    step = stride * weight_ref[...]
    place = lax.axis_index("cols")
    units = width // LANES
    moved = jnp.zeros_like(step)
    for k in range(units):
        span = pl.ds(k * LANES, LANES)
        scale = unit_row(r_ref, place * units + k)
        image = sum(ref[:, span].astype(F32) for ref in term_refs)
        if first:
            old = total = anchor = jnp.zeros_like(image)
        else:
            old, total, anchor = state[:, span], sums[:, span], anchors[:, span]
        new = old + step * (demand[:, span] * scale - image)
        new, total, anchor, square = settle(again, stride, totals, new, total, anchor)
        state_out[:, span] = new
        if not last:
            sums_out[:, span] = total
            anchors_out[:, span] = anchor
            packed[:, span] = new.astype(BF16)
        moved = moved + square
    dual, primal = lane_sum(moved), lane_sum(drift_ref[...])
    if last:
        lane = lax.broadcasted_iota(jnp.int32, dual.shape, 1)
        packed[...] = jnp.where(lane == 0, dual, jnp.where(lane == 1, primal, 0.0))
    else:
        wt_out[...] = jnp.where(again, 0.0, totals)
        packed[:, width:] = pack_pair(dual, primal)


def dual_update(demand, row_scale, stride, again, weight, drift, rest, terms, last):
    shape = demand.shape
    tile = jax.ShapeDtypeStruct((shape[0], LANES), F32)
    whole = jax.ShapeDtypeStruct(shape, F32)
    operands = (demand, row_scale, stride, again, weight, drift)
    operands += tuple(rest or ()) + tuple(terms)
    if last:
        out_shape = [whole, tile]
    else:
        joined = jax.ShapeDtypeStruct((shape[0], shape[1] + LANES), BF16)
        out_shape = [whole, whole, whole, tile, joined]
    return pl.pallas_call(
        functools.partial(dual_kernel, rest is None, last, len(terms)),
        out_shape=out_shape,
        in_specs=[VMEM] * len(operands),
        out_specs=[VMEM] * len(out_shape),
        compiler_params=PARAMS,
        name="dual_update",
    )(*operands)


def sum_columns(keep, send):
    chips = keep.shape[0]
    near = swap(send, "cols", 1)
    joined = keep + near.astype(F32)
    far = [swap(joined[o].astype(BF16), "cols", 2 * o) for o in range(1, chips)]
    return [joined[0]] + far


def on_device(
    blocks, block_row, block_col, objective, demand, capacity, step_size, restart, primal_weight
):
    matrix = blocks[0, 0]
    rows_of = block_row[0, 0]
    cols_of = block_col[0, 0]
    chips = lax.axis_size("cols") // 2
    row_groups = lax.axis_size("rows")
    scenarios = objective.shape[1]
    obj, cap, need = objective.T, capacity.T, demand.T
    strides = jnp.broadcast_to(step_size[:, :, None], (ITERS, scenarios, LANES))
    agains = jnp.broadcast_to(restart[:, :, None], (ITERS, scenarios, LANES))
    weight = jnp.broadcast_to(primal_weight[:, None], (scenarios, LANES))

    row_scale = col_scale = None
    for _ in range(PASSES):
        row_max, col_max = row_col_max(rows_of, cols_of, matrix, row_scale, col_scale)
        row_max, col_max = exchange_max(row_max, col_max)
        row_scale = (1.0 if row_scale is None else row_scale) / jnp.sqrt(row_max + epsilon)
        col_scale = (1.0 if col_scale is None else col_scale) / jnp.sqrt(col_max + epsilon)

    primal_rest = dual_rest = None
    terms = ()
    for k in range(ITERS):
        state, sums, anchors, ext, drift, weight = primal_update(
            obj, cap, col_scale, strides[k], agains[k], weight, primal_rest, terms
        )
        primal = state
        pieces = [ext] + [swap(ext, "rows", o) for o in range(1, row_groups)]
        if k == 0:
            keep, send, matrix = forward(
                rows_of, cols_of, matrix, pieces, (row_scale, col_scale)
            )
        else:
            keep, send = forward(rows_of, cols_of, matrix, pieces)
        terms = sum_columns(keep, send)
        last = k == ITERS - 1
        outs = dual_update(
            need, row_scale, strides[k], agains[k], weight, drift, dual_rest, terms, last
        )
        if last:
            dual, packed = outs
            break
        dual, dual_sums, dual_anchors, totals, packed = outs
        primal_rest = (agains[k], totals, state, sums, anchors)
        dual_rest = (totals, dual, dual_sums, dual_anchors)
        pair = jnp.stack([packed, swap(packed, "cols", 1)])
        pieces = [pair] + [swap(pair, "cols", 2 * o) for o in range(1, chips)]
        sent = backward(rows_of, cols_of, matrix, pieces)
        terms = [sent[0]] + [swap(sent[o], "rows", o) for o in range(1, row_groups)]

    total = packed + swap(packed, "cols", 1)
    total = total + sum(swap(total, "cols", 2 * o) for o in range(1, chips))
    total = total + sum(swap(total, "rows", o) for o in range(1, row_groups))
    final = next_weight(weight[:, 0], restart[-1], total[:, 0], total[:, 1])
    return (primal.T, dual.T, final)


def solution(mesh):
    in_specs = (
        P("rows", "cols", None, None, None),
        P("rows", "cols", None),
        P("rows", "cols", None),
        P(("cols", "rows"), None),
        P(("rows", "cols"), None),
        P(("cols", "rows"), None),
        P(),
        P(),
        P(),
    )
    out_specs = (P(("cols", "rows"), None), P(("rows", "cols"), None), P())
    return jax.shard_map(
        on_device, mesh=mesh, in_specs=in_specs, out_specs=out_specs, check_vma=False
    )
```

time: 555 us -> 203 us (0.37)
  blocking collectives: 303 us -> 0 us
  waiting for transfers between devices: 165 us -> 79.1 us
  starting transfers between devices: 0.21 us -> 70 us
  Pallas kernels: 0 us -> 47.7 us
  other arithmetic: 29 us -> 1.03 us
  matrix products: 27.6 us -> 0 us
  between operations: 14.3 us -> 1.04 us
  local copies, waits for them, and re-layouts: 15.1 us -> 4.21 us
    psum x3 -> x0, waiting for transfers between devices: 165 us -> none  [on_device(): summed = lax.psum(forward_partial_sum, 'cols')]
    pmax x6 -> x0, blocking collectives: 121 us -> none  [the longest x3 70.1 us: on_device(): row_max = lax.pmax(row_part, 'cols')]
    psum x3 -> x0, blocking collectives: 120 us -> none  [on_device(): lax.psum((jnp.sum(primal_move * primal_move, axis=0), jnp.sum(dual_move *...]
    ppermute x0 -> x57, waiting for transfers between devices: none -> 79.1 us  [swap(): return lax.ppermute(value, axis, [(i, i ^ offset) for i in range(count)])]
    ppermute x0 -> x57, starting transfers between devices: none -> 70 us  [swap(): return lax.ppermute(value, axis, [(i, i ^ offset) for i in range(count)])]
    all_gather x5 -> x0, blocking collectives: 62.2 us -> none  [the longest x3 44.4 us: on_device(): forward_gathered = lax.all_gather(extrapolated, 'rows', axis=0, tiled=True)]
    pallas_call x0 -> x14, Pallas kernels: none -> 47.7 us  [the longest x3 22.5 us: forward(): pl.pallas_call(functools.partial(forward_kernel, scaling, len(pieces)), o...]
    dot_general x10 -> x0, matrix products: 27.6 us -> none  [the longest x3 12.1 us: on_device(): jnp.einsum('nij,njs->nis', final_matrix, forward_picked, preferred_elemen...]
  transfers between devices with their start and end apart: 5 -> 57, of which waited for: 3 -> 45; matrix products, arithmetic and copies ran while one was open for 0% -> 0% of each run, Pallas kernels for 0% -> 0%
where the time goes in v1:
time: 203 us
  waiting for transfers between devices  79.1 us (39%)
  starting transfers between devices  70 us (34%)
  Pallas kernels  47.7 us (23%)
  local copies, waits for them, and re-layouts  4.21 us (2%)
    ppermute x57, waiting for transfers between devices, swap(): return lax.ppermute(value, axis, [(i, i ^ offset) for i in range(count)])  79.1 us
    ppermute x57, starting transfers between devices, swap(): return lax.ppermute(value, axis, [(i, i ^ offset) for i in range(count)])  70 us
    pallas_call x3, Pallas kernels, forward(): pl.pallas_call(functools.partial(forward_kernel, scaling, len(pieces)), o...  22.5 us
    pallas_call x2, Pallas kernels, backward(): pl.pallas_call(functools.partial(backward_kernel, len(pieces)), out_shape...  12.2 us
    pallas_call x3, Pallas kernels, row_col_max(): pl.pallas_call(first_max_kernel if first else max_kernel, out_shape=(jax....  10.5 us
  transfers between devices with their start and end apart: 57, of which 45 were waited for; matrix products, arithmetic and copies ran while one was open for 0% of the time, Pallas kernels for 0%

profile of v1, /device:TPU:0, one launch (start us, length us, event | category | flops | bytes accessed | tf_op | source)
XLA Modules:
  0.0 203.1 jit_solution(13942066854766017696)
XLA Ops:
  0.6 2.2 %copy-done = bf16[1,1,32,256,256]{4,3,2,1,0:T(8,128)(2,1)S(1)} copy-done((bf16[1,1,32,256,256]{4,3,2,1,0:T(8,128)(2,1)S(1)}, bf16[1,1,32,256,256]{4,3,2,1,0:T(8,128)(2,1)}, u32[]{:S(2)}) %copy-start) | copy-done | bytes 4194328
  4.1 2.4 %first_max.1 = (f32[16,256]{1,0:T(8,128)S(1)}, f32[16,256]{1,0:T(8,128)S(1)}) custom-call(s32[32]{0:T(128)S(1)} %bitcast.65, s32[32]{0:T(128)S(1)} %bitcast.73, bf16[32,256,256]{2,1,0:T(8,128)(2,1)S(1)} %bitcast.50), custom_call_target="tpu_custom_call" | custom-call | tf_op jit(solution)/shard_map/first_max/pallas_call | solution.py:166
  7.0 2.6 %collective-permute-start = (f32[16,256]{1,0:T(8,128)S(1)}, f32[16,256]{1,0:T(8,128)S(1)}, u32[]{:S(2)}, u32[]{:S(2)}) collective-permute-start(f32[16,256]{1,0:T(8,128)S(1)} %get-tuple-element.52), channel_id=1, source_target_pairs={{0,8},{8,0},{16,24},{24,16},{1,9},{9,1},{17,25},{25,17},{2,10},{10... | collective-permute-start | bytes 49160 | tf_op jit(solution)/shard_map/ppermute | solution.py:29
  11.4 3.0 %collective-permute-start.1 = (f32[16,256]{1,0:T(8,128)S(1)}, f32[16,256]{1,0:T(8,128)S(1)}, u32[]{:S(2)}, u32[]{:S(2)}) collective-permute-start(f32[16,256]{1,0:T(8,128)S(1)} %max.45), channel_id=1, source_target_pairs={{0,16},{8,24},{16,0},{24,8},{1,17},{9,25},{17,1},{25,9},{2,18},{10... | collective-permute-start | bytes 49160 | tf_op jit(solution)/shard_map/ppermute | solution.py:29
  18.4 4.0 %row_col_max.2 = (f32[16,256]{1,0:T(8,128)S(1)}, f32[16,256]{1,0:T(8,128)S(1)}) custom-call(s32[32]{0:T(128)S(1)} %bitcast.66, s32[32]{0:T(128)S(1)} %bitcast.74, bf16[32,256,256]{2,1,0:T(8,128)(2,1)S(1)} %bitcast.51, f32[16,256]{1,0:T(8,128)S(1)} %add_rsqrt_fusion.r_ref, f32[16,256]{1,0:T(8,128)S(1)} %add_rsqrt_fusion.1.c_ref), custom_call_target="tpu_custom_call" | custom-call | tf_op jit(solution)/shard_map/row_col_max/pallas_call | solution.py:166
  31.7 4.0 %row_col_max.3 = (f32[16,256]{1,0:T(8,128)S(1)}, f32[16,256]{1,0:T(8,128)S(1)}) custom-call(s32[32]{0:T(128)S(1)} %bitcast.67, s32[32]{0:T(128)S(1)} %bitcast.75, bf16[32,256,256]{2,1,0:T(8,128)(2,1)S(1)} %bitcast.52, f32[16,256]{1,0:T(8,128)S(1)} %rsqrt_multiply_fusion.2.r_ref, f32[16,256]{1,0:T(8,128)S(1)} %rsqrt_multiply_fusion.3.c_ref), custom_call_target="tpu_custom_call" | custom-call | tf_op jit(solution)/shard_map/row_col_max/pallas_call | solution.py:166
  49.9 4.6 %collective-permute-done.16.refs_7_ = bf16[48,1024]{1,0:T(8,128)(2,1)S(1)} collective-permute-done((bf16[48,1024]{1,0:T(8,128)(2,1)S(1)}, bf16[48,1024]{1,0:T(8,128)(2,1)S(1)}, u32[]{:S(2)}, u32[]{:S(2)}) %collective-permute-start.16) | collective-permute-done | bytes 98336 | tf_op jit(solution)/shard_map/ppermute | solution.py:29
  54.5 8.3 %scale_and_forward.1 = (f32[4,48,512]{2,1,0:T(8,128)S(1)}, bf16[4,48,512]{2,1,0:T(8,128)(2,1)S(1)}, bf16[32,256,256]{2,1,0:T(8,128)(2,1)S(1)}) custom-call(s32[32]{0:T(128)S(1)} %bitcast.68, s32[32]{0:T(128)S(1)} %bitcast.76, bf16[32,256,256]{2,1,0:T(8,128)(2,1)S(1)} %bitcast.53, f32[16,256]{1,0:T(8,128)S(1)} %rsqrt_multiply_fusion.refs_3_.refs_1_, ...), custom_call_target="tpu_custom_call" | custom-call | tf_op jit(solution)/shard_map/scale_and_forward/pallas_call | solution.py:291
  70.1 2.4 %collective-permute-done.21.refs_9_ = bf16[48,512]{1,0:T(8,128)(2,1)S(1)} collective-permute-done((bf16[48,512]{1,0:T(8,128)(2,1)S(1)}, bf16[48,512]{1,0:T(8,128)(2,1)S(1)}, u32[]{:S(2)}, u32[]{:S(2)}) %collective-permute-start.21) | collective-permute-done | bytes 49184 | tf_op jit(solution)/shard_map/ppermute | solution.py:29
  75.1 2.4 %collective-permute-start.25 = (bf16[2,48,640]{2,1,0:T(8,128)(2,1)S(1)}, bf16[2,48,640]{2,1,0:T(8,128)(2,1)S(1)}, u32[]{:S(2)}, u32[]{:S(2)}) collective-permute-start(bf16[2,48,640]{2,1,0:T(8,128)(2,1)S(1)} %pad_maximum_fusion.refs_3_), channel_id=1, source_target_pairs={{0,6},{1,7},{2,4},{3,5},{4,2},{5,3},{6,0},{7,1},{8,14},{9,15},{10,... | collective-permute-start | bytes 368648 | tf_op jit(solution)/shard_map/ppermute | solution.py:29
  77.6 2.7 %collective-permute-done.23.refs_4_ = bf16[2,48,640]{2,1,0:T(8,128)(2,1)S(1)} collective-permute-done((bf16[2,48,640]{2,1,0:T(8,128)(2,1)S(1)}, bf16[2,48,640]{2,1,0:T(8,128)(2,1)S(1)}, u32[]{:S(2)}, u32[]{:S(2)}) %collective-permute-start.23) | collective-permute-done | bytes 122912 | tf_op jit(solution)/shard_map/ppermute | solution.py:29
  82.3 6.0 %backward.2 = (f32[48,1152]{1,0:T(8,128)S(1)}, bf16[48,1152]{1,0:T(8,128)(2,1)S(1)}, bf16[48,1152]{1,0:T(8,128)(2,1)S(1)}, bf16[48,1152]{1,0:T(8,128)(2,1)S(1)}) custom-call(s32[32]{0:T(128)S(1)} %bitcast.69, s32[32]{0:T(128)S(1)} %bitcast.77, bf16[32,256,256]{2,1,0:T(8,128)(2,1)S(1)} %get-tuple-element.67.refs_2_, ...), custom_call_target="tpu_custom_call" | custom-call | tf_op jit(solution)/shard_map/backward/pallas_call | solution.py:345
  93.6 6.7 %collective-permute-done.27.refs_13_ = bf16[48,1152]{1,0:T(8,128)(2,1)S(1)} collective-permute-done((bf16[48,1152]{1,0:T(8,128)(2,1)S(1)}, bf16[48,1152]{1,0:T(8,128)(2,1)S(1)}, u32[]{:S(2)}, u32[]{:S(2)}) %collective-permute-start.27) | collective-permute-done | bytes 110624 | tf_op jit(solution)/shard_map/ppermute | solution.py:29
  106.1 6.1 %collective-permute-done.30.refs_5_ = bf16[48,1024]{1,0:T(8,128)(2,1)S(1)} collective-permute-done((bf16[48,1024]{1,0:T(8,128)(2,1)S(1)}, bf16[48,1024]{1,0:T(8,128)(2,1)S(1)}, u32[]{:S(2)}, u32[]{:S(2)}) %collective-permute-start.30) | collective-permute-done | bytes 98336 | tf_op jit(solution)/shard_map/ppermute | solution.py:29
  112.2 7.1 %forward.2 = (f32[4,48,512]{2,1,0:T(8,128)S(1)}, bf16[4,48,512]{2,1,0:T(8,128)(2,1)S(1)}) custom-call(s32[32]{0:T(128)S(1)} %bitcast.70, s32[32]{0:T(128)S(1)} %bitcast.78, bf16[32,256,256]{2,1,0:T(8,128)(2,1)S(1)} %get-tuple-element.67.refs_2_, bf16[48,1024]{1,0:T(8,128)(2,1)S(1)} %get-tuple-element.78.refs_3_, ...), custom_call_target="tpu_custom_call" | custom-call | tf_op jit(solution)/shard_map/forward/pallas_call | solution.py:291
  134.8 2.2 %collective-permute-done.38.refs_5_ = bf16[2,48,640]{2,1,0:T(8,128)(2,1)S(1)} collective-permute-done((bf16[2,48,640]{2,1,0:T(8,128)(2,1)S(1)}, bf16[2,48,640]{2,1,0:T(8,128)(2,1)S(1)}, u32[]{:S(2)}, u32[]{:S(2)}) %collective-permute-start.38) | collective-permute-done | bytes 122912 | tf_op jit(solution)/shard_map/ppermute | solution.py:29
  138.8 6.1 %backward.3 = (f32[48,1152]{1,0:T(8,128)S(1)}, bf16[48,1152]{1,0:T(8,128)(2,1)S(1)}, bf16[48,1152]{1,0:T(8,128)(2,1)S(1)}, bf16[48,1152]{1,0:T(8,128)(2,1)S(1)}) custom-call(s32[32]{0:T(128)S(1)} %bitcast.71, s32[32]{0:T(128)S(1)} %bitcast.79, bf16[32,256,256]{2,1,0:T(8,128)(2,1)S(1)} %get-tuple-element.67.refs_2_, ...), custom_call_target="tpu_custom_call" | custom-call | tf_op jit(solution)/shard_map/backward/pallas_call | solution.py:345
  150.6 6.4 %collective-permute-done.41.refs_13_ = bf16[48,1152]{1,0:T(8,128)(2,1)S(1)} collective-permute-done((bf16[48,1152]{1,0:T(8,128)(2,1)S(1)}, bf16[48,1152]{1,0:T(8,128)(2,1)S(1)}, u32[]{:S(2)}, u32[]{:S(2)}) %collective-permute-start.41) | collective-permute-done | bytes 110624 | tf_op jit(solution)/shard_map/ppermute | solution.py:29
  158.2 2.2 %collective-permute-start.43 = (bf16[48,1024]{1,0:T(8,128)(2,1)S(1)}, bf16[48,1024]{1,0:T(8,128)(2,1)S(1)}, u32[]{:S(2)}, u32[]{:S(2)}) collective-permute-start(bf16[48,1024]{1,0:T(8,128)(2,1)S(1)} %get-tuple-element.96.refs_3_), channel_id=1, source_target_pairs={{0,8},{8,0},{16,24},{24,16},{1,9},{9,1},{17,25},{25,17},{2,10},{10... | collective-permute-start | bytes 294920 | tf_op jit(solution)/shard_map/ppermute | solution.py:29
  163.7 6.2 %collective-permute-done.44.refs_5_ = bf16[48,1024]{1,0:T(8,128)(2,1)S(1)} collective-permute-done((bf16[48,1024]{1,0:T(8,128)(2,1)S(1)}, bf16[48,1024]{1,0:T(8,128)(2,1)S(1)}, u32[]{:S(2)}, u32[]{:S(2)}) %collective-permute-start.44) | collective-permute-done | bytes 98336 | tf_op jit(solution)/shard_map/ppermute | solution.py:29
  169.9 7.1 %forward.3 = (f32[4,48,512]{2,1,0:T(8,128)S(1)}, bf16[4,48,512]{2,1,0:T(8,128)(2,1)S(1)}) custom-call(s32[32]{0:T(128)S(1)} %bitcast.72, s32[32]{0:T(128)S(1)} %bitcast.80, bf16[32,256,256]{2,1,0:T(8,128)(2,1)S(1)} %get-tuple-element.67.refs_2_, bf16[48,1024]{1,0:T(8,128)(2,1)S(1)} %get-tuple-element.96.refs_3_, ...), custom_call_target="tpu_custom_call" | custom-call | tf_op jit(solution)/shard_map/forward/pallas_call | solution.py:291
  183.1 2.5 %collective-permute-done.49.refs_13_ = bf16[48,512]{1,0:T(8,128)(2,1)S(1)} collective-permute-done((bf16[48,512]{1,0:T(8,128)(2,1)S(1)}, bf16[48,512]{1,0:T(8,128)(2,1)S(1)}, u32[]{:S(2)}, u32[]{:S(2)}) %collective-permute-start.49) | collective-permute-done | bytes 49184 | tf_op jit(solution)/shard_map/ppermute | solution.py:29
  191.5 2.9 %collective-permute-done.53 = f32[48,128]{1,0:T(8,128)S(1)} collective-permute-done((f32[48,128]{1,0:T(8,128)S(1)}, f32[48,128]{1,0:T(8,128)S(1)}, u32[]{:S(2)}, u32[]{:S(2)}) %collective-permute-start.53) | collective-permute-done | bytes 24608 | tf_op jit(solution)/shard_map/ppermute | solution.py:29
  196.7 2.1 %collective-permute-start.56 = (f32[48,128]{1,0:T(8,128)S(1)}, f32[48,128]{1,0:T(8,128)S(1)}, u32[]{:S(2)}, u32[]{:S(2)}) collective-permute-start(f32[48,128]{1,0:T(8,128)S(1)} %add_add_fusion.1), channel_id=1, source_target_pairs={{0,24},{8,16},{16,8},{24,0},{1,25},{9,17},{17,9},{25,1},{2,26},{10... | collective-permute-start | bytes 73736 | tf_op jit(solution)/shard_map/ppermute | solution.py:29
  (169 shorter events, 99.5 us)
Async XLA Ops:
  41.0 8.1 %collective-permute-start.14 = (f32[16,256]{1,0:T(8,128)S(1)}, f32[16,256]{1,0:T(8,128)S(1)}, u32[]{:S(2)}, u32[]{:S(2)}) collective-permute-start(f32[16,256]{1,0:T(8,128)S(1)} %max.58), channel_id=1, source_target_pairs={{0,4},{1,5},{2,6},{3,7},{4,0},{5,1},{6,2},{7,3},{8,12},{9,13},{10,... | collective-permute-start | bytes 49160 | tf_op jit(solution)/shard_map/ppermute | solution.py:29
  44.7 5.2 %collective-permute-start.15 = (bf16[48,1024]{1,0:T(8,128)(2,1)S(1)}, bf16[48,1024]{1,0:T(8,128)(2,1)S(1)}, u32[]{:S(2)}, u32[]{:S(2)}) collective-permute-start(bf16[48,1024]{1,0:T(8,128)(2,1)S(1)} %get-tuple-element.60.refs_5_), channel_id=1, source_target_pairs={{0,8},{8,0},{16,24},{24,16},{1,9},{9,1},{17,25},{25,17},{2,10},{10... | collective-permute-start | bytes 294920 | tf_op jit(solution)/shard_map/ppermute | solution.py:29
  45.8 8.7 %collective-permute-start.16 = (bf16[48,1024]{1,0:T(8,128)(2,1)S(1)}, bf16[48,1024]{1,0:T(8,128)(2,1)S(1)}, u32[]{:S(2)}, u32[]{:S(2)}) collective-permute-start(bf16[48,1024]{1,0:T(8,128)(2,1)S(1)} %get-tuple-element.60.refs_5_), channel_id=1, source_target_pairs={{0,16},{8,24},{16,0},{24,8},{1,17},{9,25},{17,1},{25,9},{2,18},{10... | collective-permute-start | bytes 294920 | tf_op jit(solution)/shard_map/ppermute | solution.py:29
  47.7 6.8 %collective-permute-start.17 = (bf16[48,1024]{1,0:T(8,128)(2,1)S(1)}, bf16[48,1024]{1,0:T(8,128)(2,1)S(1)}, u32[]{:S(2)}, u32[]{:S(2)}) collective-permute-start(bf16[48,1024]{1,0:T(8,128)(2,1)S(1)} %get-tuple-element.60.refs_5_), channel_id=1, source_target_pairs={{0,24},{8,16},{16,8},{24,0},{1,25},{9,17},{17,9},{25,1},{2,26},{10... | collective-permute-start | bytes 294920 | tf_op jit(solution)/shard_map/ppermute | solution.py:29
  67.5 5.0 %collective-permute-start.21 = (bf16[48,512]{1,0:T(8,128)(2,1)S(1)}, bf16[48,512]{1,0:T(8,128)(2,1)S(1)}, u32[]{:S(2)}, u32[]{:S(2)}) collective-permute-start(bf16[48,512]{1,0:T(8,128)(2,1)S(1)} %get-tuple-element.113), channel_id=1, source_target_pairs={{0,6},{1,7},{2,4},{3,5},{4,2},{5,3},{6,0},{7,1},{8,14},{9,15},{10,... | collective-permute-start | bytes 147464 | tf_op jit(solution)/shard_map/ppermute | solution.py:29
  74.0 6.2 %collective-permute-start.23 = (bf16[2,48,640]{2,1,0:T(8,128)(2,1)S(1)}, bf16[2,48,640]{2,1,0:T(8,128)(2,1)S(1)}, u32[]{:S(2)}, u32[]{:S(2)}) collective-permute-start(bf16[2,48,640]{2,1,0:T(8,128)(2,1)S(1)} %pad_maximum_fusion.refs_3_), channel_id=1, source_target_pairs={{0,2},{1,3},{2,0},{3,1},{4,6},{5,7},{6,4},{7,5},{8,10},{9,11},{10,... | collective-permute-start | bytes 368648 | tf_op jit(solution)/shard_map/ppermute | solution.py:29
  74.6 7.7 %collective-permute-start.24 = (bf16[2,48,640]{2,1,0:T(8,128)(2,1)S(1)}, bf16[2,48,640]{2,1,0:T(8,128)(2,1)S(1)}, u32[]{:S(2)}, u32[]{:S(2)}) collective-permute-start(bf16[2,48,640]{2,1,0:T(8,128)(2,1)S(1)} %pad_maximum_fusion.refs_3_), channel_id=1, source_target_pairs={{0,4},{1,5},{2,6},{3,7},{4,0},{5,1},{6,2},{7,3},{8,12},{9,13},{10,... | collective-permute-start | bytes 368648 | tf_op jit(solution)/shard_map/ppermute | solution.py:29
  75.1 7.2 %collective-permute-start.25 = (bf16[2,48,640]{2,1,0:T(8,128)(2,1)S(1)}, bf16[2,48,640]{2,1,0:T(8,128)(2,1)S(1)}, u32[]{:S(2)}, u32[]{:S(2)}) collective-permute-start(bf16[2,48,640]{2,1,0:T(8,128)(2,1)S(1)} %pad_maximum_fusion.refs_3_), channel_id=1, source_target_pairs={{0,6},{1,7},{2,4},{3,5},{4,2},{5,3},{6,0},{7,1},{8,14},{9,15},{10,... | collective-permute-start | bytes 368648 | tf_op jit(solution)/shard_map/ppermute | solution.py:29
  88.4 5.2 %collective-permute-start.26 = (bf16[48,1152]{1,0:T(8,128)(2,1)S(1)}, bf16[48,1152]{1,0:T(8,128)(2,1)S(1)}, u32[]{:S(2)}, u32[]{:S(2)}) collective-permute-start(bf16[48,1152]{1,0:T(8,128)(2,1)S(1)} %get-tuple-element.70), channel_id=1, source_target_pairs={{0,8},{8,0},{16,24},{24,16},{1,9},{9,1},{17,25},{25,17},{2,10},{10... | collective-permute-start | bytes 331784 | tf_op jit(solution)/shard_map/ppermute | solution.py:29
  90.1 10.3 %collective-permute-start.27 = (bf16[48,1152]{1,0:T(8,128)(2,1)S(1)}, bf16[48,1152]{1,0:T(8,128)(2,1)S(1)}, u32[]{:S(2)}, u32[]{:S(2)}) collective-permute-start(bf16[48,1152]{1,0:T(8,128)(2,1)S(1)} %get-tuple-element.71), channel_id=1, source_target_pairs={{0,16},{8,24},{16,0},{24,8},{1,17},{9,25},{17,1},{25,9},{2,18},{10... | collective-permute-start | bytes 331784 | tf_op jit(solution)/shard_map/ppermute | solution.py:29
  90.9 9.5 %collective-permute-start.28 = (bf16[48,1152]{1,0:T(8,128)(2,1)S(1)}, bf16[48,1152]{1,0:T(8,128)(2,1)S(1)}, u32[]{:S(2)}, u32[]{:S(2)}) collective-permute-start(bf16[48,1152]{1,0:T(8,128)(2,1)S(1)} %get-tuple-element.72), channel_id=1, source_target_pairs={{0,24},{8,16},{16,8},{24,0},{1,25},{9,17},{17,9},{25,1},{2,26},{10... | collective-permute-start | bytes 331784 | tf_op jit(solution)/shard_map/ppermute | solution.py:29
  100.8 5.4 %collective-permute-start.29 = (bf16[48,1024]{1,0:T(8,128)(2,1)S(1)}, bf16[48,1024]{1,0:T(8,128)(2,1)S(1)}, u32[]{:S(2)}, u32[]{:S(2)}) collective-permute-start(bf16[48,1024]{1,0:T(8,128)(2,1)S(1)} %get-tuple-element.78.refs_3_), channel_id=1, source_target_pairs={{0,8},{8,0},{16,24},{24,16},{1,9},{9,1},{17,25},{25,17},{2,10},{10... | collective-permute-start | bytes 294920 | tf_op jit(solution)/shard_map/ppermute | solution.py:29
  102.9 9.3 %collective-permute-start.30 = (bf16[48,1024]{1,0:T(8,128)(2,1)S(1)}, bf16[48,1024]{1,0:T(8,128)(2,1)S(1)}, u32[]{:S(2)}, u32[]{:S(2)}) collective-permute-start(bf16[48,1024]{1,0:T(8,128)(2,1)S(1)} %get-tuple-element.78.refs_3_), channel_id=1, source_target_pairs={{0,16},{8,24},{16,0},{24,8},{1,17},{9,25},{17,1},{25,9},{2,18},{10... | collective-permute-start | bytes 294920 | tf_op jit(solution)/shard_map/ppermute | solution.py:29
  103.4 8.8 %collective-permute-start.31 = (bf16[48,1024]{1,0:T(8,128)(2,1)S(1)}, bf16[48,1024]{1,0:T(8,128)(2,1)S(1)}, u32[]{:S(2)}, u32[]{:S(2)}) collective-permute-start(bf16[48,1024]{1,0:T(8,128)(2,1)S(1)} %get-tuple-element.78.refs_3_), channel_id=1, source_target_pairs={{0,24},{8,16},{16,8},{24,0},{1,25},{9,17},{17,9},{25,1},{2,26},{10... | collective-permute-start | bytes 294920 | tf_op jit(solution)/shard_map/ppermute | solution.py:29
  129.4 5.5 %collective-permute-start.37 = (bf16[2,48,640]{2,1,0:T(8,128)(2,1)S(1)}, bf16[2,48,640]{2,1,0:T(8,128)(2,1)S(1)}, u32[]{:S(2)}, u32[]{:S(2)}) collective-permute-start(bf16[2,48,640]{2,1,0:T(8,128)(2,1)S(1)} %pad_maximum_fusion.1.refs_3_), channel_id=1, source_target_pairs={{0,2},{1,3},{2,0},{3,1},{4,6},{5,7},{6,4},{7,5},{8,10},{9,11},{10,... | collective-permute-start | bytes 368648 | tf_op jit(solution)/shard_map/ppermute | solution.py:29
  131.1 5.9 %collective-permute-start.38 = (bf16[2,48,640]{2,1,0:T(8,128)(2,1)S(1)}, bf16[2,48,640]{2,1,0:T(8,128)(2,1)S(1)}, u32[]{:S(2)}, u32[]{:S(2)}) collective-permute-start(bf16[2,48,640]{2,1,0:T(8,128)(2,1)S(1)} %pad_maximum_fusion.1.refs_3_), channel_id=1, source_target_pairs={{0,4},{1,5},{2,6},{3,7},{4,0},{5,1},{6,2},{7,3},{8,12},{9,13},{10,... | collective-permute-start | bytes 368648 | tf_op jit(solution)/shard_map/ppermute | solution.py:29
  131.6 7.2 %collective-permute-start.39 = (bf16[2,48,640]{2,1,0:T(8,128)(2,1)S(1)}, bf16[2,48,640]{2,1,0:T(8,128)(2,1)S(1)}, u32[]{:S(2)}, u32[]{:S(2)}) collective-permute-start(bf16[2,48,640]{2,1,0:T(8,128)(2,1)S(1)} %pad_maximum_fusion.1.refs_3_), channel_id=1, source_target_pairs={{0,6},{1,7},{2,4},{3,5},{4,2},{5,3},{6,0},{7,1},{8,14},{9,15},{10,... | collective-permute-start | bytes 368648 | tf_op jit(solution)/shard_map/ppermute | solution.py:29
  145.0 5.6 %collective-permute-start.40 = (bf16[48,1152]{1,0:T(8,128)(2,1)S(1)}, bf16[48,1152]{1,0:T(8,128)(2,1)S(1)}, u32[]{:S(2)}, u32[]{:S(2)}) collective-permute-start(bf16[48,1152]{1,0:T(8,128)(2,1)S(1)} %get-tuple-element.87), channel_id=1, source_target_pairs={{0,8},{8,0},{16,24},{24,16},{1,9},{9,1},{17,25},{25,17},{2,10},{10... | collective-permute-start | bytes 331784 | tf_op jit(solution)/shard_map/ppermute | solution.py:29
  147.1 9.9 %collective-permute-start.41 = (bf16[48,1152]{1,0:T(8,128)(2,1)S(1)}, bf16[48,1152]{1,0:T(8,128)(2,1)S(1)}, u32[]{:S(2)}, u32[]{:S(2)}) collective-permute-start(bf16[48,1152]{1,0:T(8,128)(2,1)S(1)} %get-tuple-element.88), channel_id=1, source_target_pairs={{0,16},{8,24},{16,0},{24,8},{1,17},{9,25},{17,1},{25,9},{2,18},{10... | collective-permute-start | bytes 331784 | tf_op jit(solution)/shard_map/ppermute | solution.py:29
  147.6 9.4 %collective-permute-start.42 = (bf16[48,1152]{1,0:T(8,128)(2,1)S(1)}, bf16[48,1152]{1,0:T(8,128)(2,1)S(1)}, u32[]{:S(2)}, u32[]{:S(2)}) collective-permute-start(bf16[48,1152]{1,0:T(8,128)(2,1)S(1)} %get-tuple-element.89), channel_id=1, source_target_pairs={{0,24},{8,16},{16,8},{24,0},{1,25},{9,17},{17,9},{25,1},{2,26},{10... | collective-permute-start | bytes 331784 | tf_op jit(solution)/shard_map/ppermute | solution.py:29
  158.2 5.5 %collective-permute-start.43 = (bf16[48,1024]{1,0:T(8,128)(2,1)S(1)}, bf16[48,1024]{1,0:T(8,128)(2,1)S(1)}, u32[]{:S(2)}, u32[]{:S(2)}) collective-permute-start(bf16[48,1024]{1,0:T(8,128)(2,1)S(1)} %get-tuple-element.96.refs_3_), channel_id=1, source_target_pairs={{0,8},{8,0},{16,24},{24,16},{1,9},{9,1},{17,25},{25,17},{2,10},{10... | collective-permute-start | bytes 294920 | tf_op jit(solution)/shard_map/ppermute | solution.py:29
  160.4 9.5 %collective-permute-start.44 = (bf16[48,1024]{1,0:T(8,128)(2,1)S(1)}, bf16[48,1024]{1,0:T(8,128)(2,1)S(1)}, u32[]{:S(2)}, u32[]{:S(2)}) collective-permute-start(bf16[48,1024]{1,0:T(8,128)(2,1)S(1)} %get-tuple-element.96.refs_3_), channel_id=1, source_target_pairs={{0,16},{8,24},{16,0},{24,8},{1,17},{9,25},{17,1},{25,9},{2,18},{10... | collective-permute-start | bytes 294920 | tf_op jit(solution)/shard_map/ppermute | solution.py:29
  160.7 9.2 %collective-permute-start.45 = (bf16[48,1024]{1,0:T(8,128)(2,1)S(1)}, bf16[48,1024]{1,0:T(8,128)(2,1)S(1)}, u32[]{:S(2)}, u32[]{:S(2)}) collective-permute-start(bf16[48,1024]{1,0:T(8,128)(2,1)S(1)} %get-tuple-element.96.refs_3_), channel_id=1, source_target_pairs={{0,24},{8,16},{16,8},{24,0},{1,25},{9,17},{17,9},{25,1},{2,26},{10... | collective-permute-start | bytes 294920 | tf_op jit(solution)/shard_map/ppermute | solution.py:29
  196.7 5.6 %collective-permute-start.56 = (f32[48,128]{1,0:T(8,128)S(1)}, f32[48,128]{1,0:T(8,128)S(1)}, u32[]{:S(2)}, u32[]{:S(2)}) collective-permute-start(f32[48,128]{1,0:T(8,128)S(1)} %add_add_fusion.1), channel_id=1, source_target_pairs={{0,24},{8,16},{16,8},{24,0},{1,25},{9,17},{17,9},{25,1},{2,26},{10... | collective-permute-start | bytes 73736 | tf_op jit(solution)/shard_map/ppermute | solution.py:29
  (45 other events, 386.1 us)

commit v2 on v1

v2 whole, which is shorter than its diff:
```python
import functools

import jax
import jax.numpy as jnp
from jax import lax
from jax.experimental import pallas as pl
from jax.experimental.pallas import tpu as pltpu
from jax.sharding import PartitionSpec as P

BLK = 256
RB = 16
CB = 16
PASSES = 3
ITERS = 3
LANES = 128

epsilon = 1e-06
F32 = jnp.float32
BF16 = jnp.bfloat16
VMEM = pl.BlockSpec(memory_space=pltpu.VMEM)
SMEM = pl.BlockSpec(memory_space=pltpu.SMEM)
PARAMS = pltpu.CompilerParams(vmem_limit_bytes=32 * 1024 * 1024)


def swap(value, axis, offset):
    count = lax.axis_size(axis)
    return lax.ppermute(value, axis, [(i, i ^ offset) for i in range(count)])


def for_each_block(count, group, body):
    if count == group:
        body(range(count))
    else:

        @pl.loop(0, count // group)
        def _(step):
            body([step * group + k for k in range(group)])


def unit_row(ref, unit):
    row = ref[pl.ds(unit // 2, 1), :]
    return jnp.where(unit % 2 == 0, row[:, :LANES], row[:, LANES:])


def lane_sum(tile):
    return jnp.broadcast_to(jnp.sum(tile, axis=1, keepdims=True), tile.shape)


def split_parts(value):
    parts = []
    for _ in range(3):
        rounded = value.astype(BF16).astype(F32)
        parts.append(rounded)
        value = value - rounded
    return parts


def tail_rows():
    return -(-3 * (lax.axis_size("cols") // 2) // 16) * 16


def to_tail(values, half=0):
    scenarios = values[0][1].shape[0]
    lane = lax.broadcasted_iota(jnp.int32, (scenarios, LANES), 1)
    tile = jnp.zeros((scenarios, LANES), F32)
    for place, value in values:
        for k, part in enumerate(split_parts(value)):
            tile = jnp.where(lane == place + k, part, tile)
    gap = jnp.zeros((LANES // 2 - scenarios, LANES), F32)
    pieces = [jnp.where(half == 0, tile, 0.0), gap, jnp.where(half == 0, 0.0, tile), gap]
    return jnp.concatenate(pieces, axis=0).T[: tail_rows()]


def from_tail(tail, scenarios, first=0, last=LANES):
    rest = jnp.zeros((LANES - tail.shape[0], LANES), F32)
    square = jnp.concatenate([tail, rest], axis=0).T
    tile = square[:scenarios] + square[LANES // 2 : LANES // 2 + scenarios]
    lane = lax.broadcasted_iota(jnp.int32, tile.shape, 1)
    return lane_sum(jnp.where((lane >= first) & (lane < last), tile, 0.0))


def next_weight(weight, restart, drift_dual, drift_primal):
    candidate = jnp.sqrt(
        weight * jnp.sqrt((drift_dual + epsilon) / (drift_primal + epsilon))
    )
    return jnp.where(restart == 1, candidate, weight)


def first_max_kernel(
    places_vmem, a, row_out, col_out, places_ref, sem, racc, cacc
):
    places = pltpu.make_async_copy(places_vmem, places_ref, sem)
    places.start()
    racc[...] = jnp.zeros_like(racc)
    cacc[...] = jnp.zeros_like(cacc)

    def block(n):
        r, c = places_ref[0, n], places_ref[1, n]
        col = cacc[c]
        for t in range(BLK // 32):
            part = pl.ds(t * 32, 32)
            mag = jnp.abs(a[n, part, :])
            col = jnp.maximum(col, jnp.maximum(mag[:16], mag[16:]))
            racc[r, part, :] = jnp.maximum(
                racc[r, part, :], jnp.maximum(mag[:, :LANES], mag[:, LANES:])
            )
        cacc[c] = col

    places.wait()
    for_each_block(a.shape[0], 4, lambda ns: [block(n) for n in ns])
    for b in range(RB):
        flipped = racc[b].astype(F32).T
        row_out[b : b + 1, :] = jnp.max(flipped, axis=0, keepdims=True)
        col_out[b : b + 1, :] = jnp.max(cacc[b].astype(F32), axis=0, keepdims=True)


def max_kernel(
    rows_ref, cols_ref, a, r_ref, c_ref, row_out, col_out, rb, racc, cacc
):
    racc[...] = jnp.zeros_like(racc)
    cacc[...] = jnp.zeros_like(cacc)
    spread_rows(r_ref, rb)

    def block(n):
        r, c = rows_ref[n], cols_ref[n]
        factor = c_ref[pl.ds(c, 1), :]
        col = cacc[c]
        for t in range(BLK // 32):
            part = pl.ds(t * 32, 32)
            mag = jnp.abs(a[n, part, :].astype(F32))
            tall = rb[r, part, :]
            by_row = jnp.concatenate([mag[:, :LANES] * tall, mag[:, LANES:] * tall], 1)
            by_col = mag * factor
            for q in range(4):
                col = jnp.maximum(col, by_row[8 * q : 8 * q + 8])
            racc[r, part, :] = jnp.maximum(
                racc[r, part, :], jnp.maximum(by_col[:, :LANES], by_col[:, LANES:])
            )
        cacc[c] = col

    for_each_block(a.shape[0], 2, lambda ns: [block(n) for n in ns])
    for b in range(RB):
        row_out[b : b + 1, :] = (
            jnp.max(racc[b].T, axis=0, keepdims=True) * r_ref[b : b + 1, :]
        )
        col_out[b : b + 1, :] = (
            jnp.max(cacc[b], axis=0, keepdims=True) * c_ref[b : b + 1, :]
        )


def spread_rows(r_ref, rb):
    for b in range(RB):
        rb[b] = jnp.broadcast_to(r_ref[b : b + 1, :], (LANES, BLK)).T


def first_max(places, matrix):
    count = matrix.shape[0]
    return pl.pallas_call(
        first_max_kernel,
        out_shape=(
            jax.ShapeDtypeStruct((RB, BLK), F32),
            jax.ShapeDtypeStruct((CB, BLK), F32),
        ),
        in_specs=[VMEM, VMEM],
        out_specs=(VMEM, VMEM),
        scratch_shapes=[
            pltpu.SMEM((2, count), jnp.int32),
            pltpu.SemaphoreType.DMA,
            pltpu.VMEM((RB, BLK, LANES), BF16),
            pltpu.VMEM((CB, 16, BLK), BF16),
        ],
        compiler_params=PARAMS,
        name="first_max",
    )(places, matrix)


def row_col_max(rows_of, cols_of, matrix, row_scale, col_scale):
    return pl.pallas_call(
        max_kernel,
        out_shape=(
            jax.ShapeDtypeStruct((RB, BLK), F32),
            jax.ShapeDtypeStruct((CB, BLK), F32),
        ),
        in_specs=[SMEM, SMEM, VMEM, VMEM, VMEM],
        out_specs=(VMEM, VMEM),
        scratch_shapes=[
            pltpu.VMEM((RB, BLK, LANES), F32),
            pltpu.VMEM((RB, BLK, LANES), F32),
            pltpu.VMEM((CB, 8, BLK), F32),
        ],
        compiler_params=PARAMS,
        name="row_col_max",
    )(rows_of, cols_of, matrix, row_scale, col_scale)


def exchange_max(row_part, col_part, last=False):
    row_step, col_step = 1, 1
    while row_step < lax.axis_size("cols") or col_step < lax.axis_size("rows"):
        row_next = col_next = None
        if row_step < lax.axis_size("cols"):
            row_next = swap(row_part, "cols", row_step)
        if col_step < lax.axis_size("rows"):
            col_next = swap(col_part, "rows", col_step)
        if row_next is not None:
            row_part = jnp.maximum(row_part, row_next)
        if col_next is not None:
            col_part = jnp.maximum(col_part, col_next)
        if last and col_step * 2 == lax.axis_size("rows"):
            row_part, col_part = lax.optimization_barrier((row_part, col_part))
        row_step, col_step = 2 * row_step, 2 * col_step
    return row_part, col_part


def fetch_units(ref, first, count):
    return jnp.concatenate([ref[first + k] for k in range(count)], axis=1)


def scale_kernel(rows_ref, cols_ref, a, r_ref, c_ref, m, rb):
    spread_rows(r_ref, rb)

    def block(n):
        r, c = rows_ref[n], cols_ref[n]
        factor = c_ref[pl.ds(c, 1), :]
        for t in range(BLK // 32):
            part = pl.ds(t * 32, 32)
            raw = a[n, part, :].astype(F32)
            tall = rb[r, part, :]
            for half in range(2):
                lanes = slice(half * LANES, (half + 1) * LANES)
                scaled = raw[:, lanes] * tall * factor[:, lanes]
                m[n, part, pl.ds(half * LANES, LANES)] = scaled.astype(BF16)

    for_each_block(m.shape[0], 2, lambda ns: [block(n) for n in ns])


def scale_matrix(rows_of, cols_of, matrix, row_scale, col_scale):
    return pl.pallas_call(
        scale_kernel,
        out_shape=jax.ShapeDtypeStruct(matrix.shape, BF16),
        in_specs=[SMEM, SMEM, VMEM, VMEM, VMEM],
        out_specs=VMEM,
        scratch_shapes=[pltpu.VMEM((RB, BLK, LANES), F32)],
        compiler_params=PARAMS,
        name="scale_matrix",
    )(rows_of, cols_of, matrix, row_scale, col_scale)


def product_scratch(scenarios):
    return [
        pltpu.VMEM((CB * BLK // LANES, scenarios, LANES), BF16),
        pltpu.VMEM((RB * BLK // LANES, scenarios, LANES), F32),
    ]


def block_products(ns, sources, targets, x, m, acc, dims):
    products = [
        lax.dot_general(
            fetch_units(x, 2 * sources[n], 2), m[n], dims, preferred_element_type=F32
        )
        for n in ns
    ]
    for n, product in zip(ns, products):
        unit = 2 * targets[n]
        acc[unit] += product[:, :LANES]
        acc[unit + 1] += product[:, LANES:]


def forward_kernel(pieces, *refs):
    rows_ref, cols_ref, m, drift = refs[:4]
    piece_refs = refs[4 : 4 + pieces]
    keep, send, x, acc = refs[4 + pieces :]
    scenarios = x.shape[1]
    me = lax.axis_index("rows")
    units = x.shape[0] // pieces
    for o, piece in enumerate(piece_refs):
        for k in range(units):
            x[(me ^ o) * units + k] = piece[k * scenarios : (k + 1) * scenarios, :]
    acc[...] = jnp.zeros_like(acc)
    count = m.shape[0]
    dims = (((1,), (1,)), ((), ()))
    for_each_block(
        count, count, lambda ns: block_products(ns, cols_ref, rows_ref, x, m, acc, dims)
    )
    me, core = lax.axis_index("cols") // 2, lax.axis_index("cols") % 2
    shards = lax.axis_size("cols")
    units = acc.shape[0] // shards
    for chip in range(shards // 2):
        for k in range(units):
            rows = pl.ds((chip * units + k) * scenarios, scenarios)
            keep[rows, :] = acc[(2 * chip + core) * units + k]
            send[rows, :] = acc[(2 * chip + 1 - core) * units + k].astype(BF16)
    tail = to_tail([(3 * me, lane_sum(drift[...]))], core)
    rows = pl.ds(keep.shape[0] - tail_rows(), tail_rows())
    keep[rows, :] = tail
    send[rows, :] = tail.astype(BF16)


def half_rows(scenarios):
    return RB * BLK // 2 // LANES * scenarios + tail_rows()


def forward(rows_of, cols_of, matrix, drift, pieces):
    scenarios = drift.shape[0]
    rows = half_rows(scenarios)
    return pl.pallas_call(
        functools.partial(forward_kernel, len(pieces)),
        out_shape=[
            jax.ShapeDtypeStruct((rows, LANES), F32),
            jax.ShapeDtypeStruct((rows, LANES), BF16),
        ],
        in_specs=[SMEM, SMEM, VMEM, VMEM] + [VMEM] * len(pieces),
        out_specs=[VMEM] * 2,
        scratch_shapes=product_scratch(scenarios),
        compiler_params=PARAMS,
        name="forward",
    )(rows_of, cols_of, matrix, drift, *pieces)


def backward_kernel(*refs):
    rows_ref, cols_ref, m, own, other, drift, keep = refs[:7]
    sends, (y, acc) = refs[7:-2], refs[-2:]
    scenarios = y.shape[1]
    core = lax.axis_index("cols") % 2
    shards = lax.axis_size("cols")
    units = y.shape[0] // shards
    for half, ref in ((core, own), (1 - core, other)):
        for chip in range(shards // 2):
            for k in range(units):
                start = (chip * units + k) * scenarios
                y[(2 * chip + half) * units + k] = ref[start : start + scenarios, :]
    acc[...] = jnp.zeros_like(acc)
    count = m.shape[0]
    dims = (((1,), (0,)), ((), ()))
    for_each_block(
        count, count, lambda ns: block_products(ns, rows_ref, cols_ref, y, m, acc, dims)
    )
    tail = own[own.shape[0] - tail_rows() :, :].astype(F32)
    tail = tail + other[other.shape[0] - tail_rows() :, :].astype(F32)
    tail = to_tail([(0, from_tail(tail, scenarios)), (3, drift[...])])
    me = lax.axis_index("rows")
    units = acc.shape[0] // (1 + len(sends))
    for o, out in enumerate((keep,) + tuple(sends)):
        for k in range(units):
            out[pl.ds(k * scenarios, scenarios), :] = acc[(me ^ o) * units + k].astype(
                out.dtype
            )
        out[pl.ds(units * scenarios, tail_rows()), :] = tail.astype(out.dtype)


def backward(rows_of, cols_of, matrix, own, other, drift):
    scenarios = drift.shape[0]
    groups = lax.axis_size("rows")
    shape = (CB * BLK // groups // LANES * scenarios + tail_rows(), LANES)
    return pl.pallas_call(
        backward_kernel,
        out_shape=[jax.ShapeDtypeStruct(shape, F32)]
        + [jax.ShapeDtypeStruct(shape, BF16)] * (groups - 1),
        in_specs=[SMEM, SMEM, VMEM, VMEM, VMEM, VMEM],
        out_specs=[VMEM] * groups,
        scratch_shapes=product_scratch(scenarios),
        compiler_params=PARAMS,
        name="backward",
    )(rows_of, cols_of, matrix, own, other, drift)


def settle(again, stride, totals, new, total, anchor):
    total = total + stride * new
    mean = total / totals
    move = mean - anchor
    return (
        jnp.where(again, mean, new),
        jnp.where(again, 0.0, total),
        jnp.where(again, mean, anchor),
        move * move,
    )


def primal_kernel(first, last, terms, *refs):
    obj, cap, c_ref, stride_ref, again_ref, weight_ref = refs[:6]
    refs = refs[6:]
    if not first:
        before_ref, wt_ref, state, sums, anchors = refs[:5]
        term_refs = refs[5 : 5 + terms]
        refs = refs[5 + terms :]
    state_out, ext, drift, weight_out = refs[:4]
    width = obj.shape[1]
    weight = weight_ref[...]
    stride = stride_ref[...]
    again = again_ref[...] == 1
    totals = stride
    if not first:
        totals = wt_ref[...] + stride
        scenarios = weight.shape[0]
        tail = sum(ref[ref.shape[0] - tail_rows() :, :].astype(F32) for ref in term_refs)
        drift_dual = from_tail(tail, scenarios, 0, 3)
        drift_primal = from_tail(tail, scenarios, 3, 6)
        weight = next_weight(weight, before_ref[...], drift_dual, drift_primal)
    weight_out[...] = weight
    step = stride / weight
    place = lax.axis_index("rows")
    units = width // LANES
    moved = jnp.zeros_like(weight)
    for k in range(units):
        span = pl.ds(k * LANES, LANES)
        scale = unit_row(c_ref, place * units + k)
        gradient = obj[:, span] * scale
        upper = cap[:, span] / scale
        if first:
            old = total = anchor = jnp.zeros_like(gradient)
        else:
            old, total, anchor = state[:, span], sums[:, span], anchors[:, span]
            rows = pl.ds(k * obj.shape[0], obj.shape[0])
            product = sum(ref[rows, :].astype(F32) for ref in term_refs)
            gradient = gradient - product
        new = jnp.minimum(jnp.maximum(old - step * gradient, 0.0), upper)
        ext[pl.ds(k * obj.shape[0], obj.shape[0]), :] = (2.0 * new - old).astype(BF16)
        new, total, anchor, square = settle(again, stride, totals, new, total, anchor)
        state_out[:, span] = new
        if not last:
            sums_out, anchors_out = refs[4:]
            sums_out[:, span] = total
            anchors_out[:, span] = anchor
        moved = moved + square
    drift[...] = moved


def primal_update(obj, cap, col_scale, stride, again, weight, rest, terms, last):
    shape = obj.shape
    tile = jax.ShapeDtypeStruct((shape[0], LANES), F32)
    whole = jax.ShapeDtypeStruct(shape, F32)
    ext = jax.ShapeDtypeStruct((shape[1] // LANES * shape[0], LANES), BF16)
    operands = (obj, cap, col_scale, stride, again, weight) + tuple(rest or ()) + tuple(terms)
    return pl.pallas_call(
        functools.partial(primal_kernel, rest is None, last, len(terms)),
        out_shape=[whole, ext, tile, tile] + [whole] * (0 if last else 2),
        in_specs=[VMEM] * len(operands),
        out_specs=[VMEM] * (4 if last else 6),
        compiler_params=PARAMS,
        name="primal_update",
    )(*operands)


def dual_kernel(first, last, chips, *refs):
    stride_ref, again_ref, weight_ref = refs[:3]
    refs = refs[3:]
    if first:
        r_ref, refs = refs[0], refs[1:]
        demands, refs = refs[:chips], refs[chips:]
    else:
        need, wt_ref, state, sums, anchors = refs[:5]
        refs = refs[5:]
    parts, refs = (refs[:2], refs[2:4]), refs[4:]
    if last:
        out, drifts, state_out = refs
    else:
        if first:
            need, refs = refs[0], refs[1:]
        state_out, sums_out, anchors_out, wt_out, packed, drift_out = refs
    stride = stride_ref[...]
    scenarios = stride.shape[0]
    again = again_ref[...] == 1
    totals = stride if first else wt_ref[...] + stride
    step = stride * weight_ref[...]
    place = lax.axis_index("cols")
    me, core = place // 2, place % 2
    count = state_out.shape[0] // scenarios
    units = count // chips
    if first:
        for o, demand in enumerate(demands):
            for k in range(units):
                scale = unit_row(r_ref, (2 * (me ^ o) + core) * units + k)
                start = pl.multiple_of(((me ^ o) * units + k) * scenarios, 8)
                need[pl.ds(start, scenarios), :] = (
                    demand[:, k * LANES : (k + 1) * LANES] * scale
                )
    moved = jnp.zeros_like(step)
    for k in range(count):
        span = pl.ds(k * scenarios, scenarios)
        part, place = divmod(k, count // 2)
        rows = pl.ds(place * scenarios, scenarios)
        image = sum(ref[rows, :].astype(F32) for ref in parts[part])
        if first:
            old = total = anchor = jnp.zeros_like(image)
        else:
            old, total, anchor = state[span, :], sums[span, :], anchors[span, :]
        new = old + step * (need[span, :] - image)
        new, total, anchor, square = settle(again, stride, totals, new, total, anchor)
        state_out[span, :] = new
        if not last:
            sums_out[span, :] = total
            anchors_out[span, :] = anchor
            packed[span, :] = new.astype(BF16)
        moved = moved + square
    start = count // 2 * scenarios
    tail = sum(ref[start:, :].astype(F32) for ref in parts[1])
    dual, primal = lane_sum(moved), from_tail(tail, scenarios)
    if last:
        lane = lax.broadcasted_iota(jnp.int32, dual.shape, 1)
        drifts[...] = jnp.where(lane == 0, dual, jnp.where(lane == 1, primal, 0.0))
        for k in range(units):
            start = pl.multiple_of((me * units + k) * scenarios, 8)
            out[:, k * LANES : (k + 1) * LANES] = state_out[pl.ds(start, scenarios), :]
    else:
        wt_out[...] = jnp.where(again, 0.0, totals)
        packed[pl.ds(count * scenarios, tail_rows()), :] = to_tail([(0, dual)], core).astype(BF16)
        drift_out[...] = primal


def dual_update(stride, again, weight, rest, terms, width, row_scale=None, last=False):
    first = row_scale is not None
    chips = lax.axis_size("cols") // 2
    scenarios = stride.shape[0]
    rows = half_rows(scenarios)
    tile = jax.ShapeDtypeStruct((scenarios, LANES), F32)
    half = jax.ShapeDtypeStruct((rows - tail_rows(), LANES), F32)
    operands = (stride, again, weight) + ((row_scale,) if first else ())
    operands += tuple(rest) + tuple(terms)
    scratch = []
    if last:
        out_shape = [jax.ShapeDtypeStruct((scenarios, width), F32), tile]
        scratch = [pltpu.VMEM(half.shape, F32)]
    else:
        packed = jax.ShapeDtypeStruct((rows, LANES), BF16)
        out_shape = [half] * (3 + first) + [tile, packed, tile]
    return pl.pallas_call(
        functools.partial(dual_kernel, first, last, chips),
        out_shape=out_shape,
        in_specs=[VMEM] * len(operands),
        out_specs=[VMEM] * len(out_shape),
        scratch_shapes=scratch,
        compiler_params=PARAMS,
        name="dual_update",
    )(*operands)


def sum_columns(keep, send):
    chips = lax.axis_size("cols") // 2
    joined = keep + swap(send, "cols", 1).astype(F32)
    middle = (joined.shape[0] - tail_rows()) // 2
    parts = [joined[:middle], joined[middle:]]
    steps = [1 << k for k in range(chips.bit_length() - 1)]
    for k in range(len(steps)):
        got = [
            swap(part.astype(BF16), "cols", 2 * order[k])
            for part, order in zip(parts, (steps, steps[::-1]))
        ]
        if k == len(steps) - 1:
            return [parts[0], got[0], parts[1], got[1]]
        parts = [part + more.astype(F32) for part, more in zip(parts, got)]


def on_device(
    blocks, block_row, block_col, objective, demand, capacity, step_size, restart, primal_weight
):
    rows_of = block_row[0, 0]
    cols_of = block_col[0, 0]
    chips = lax.axis_size("cols") // 2
    row_groups = lax.axis_size("rows")
    scenarios = objective.shape[1]
    obj, cap, need = objective.T, capacity.T, demand.T
    strides = jnp.broadcast_to(step_size[:, :, None], (ITERS, scenarios, LANES))
    agains = jnp.broadcast_to(restart[:, :, None], (ITERS, scenarios, LANES))
    weight = jnp.broadcast_to(primal_weight[:, None], (scenarios, LANES))

    matrix = blocks[0, 0]
    row_top, col_top = first_max(jnp.stack([rows_of, cols_of]), matrix)
    row_top, col_top = exchange_max(row_top, col_top)
    row_scale = 1.0 / jnp.sqrt(row_top + epsilon)
    col_scale = 1.0 / jnp.sqrt(col_top + epsilon)
    for sweep in range(1, PASSES):
        row_top, col_top = row_col_max(rows_of, cols_of, matrix, row_scale, col_scale)
        row_top, col_top = exchange_max(row_top, col_top, sweep == PASSES - 1)
        row_scale = row_scale / jnp.sqrt(row_top + epsilon)
        col_scale = col_scale / jnp.sqrt(col_top + epsilon)

    primal_rest = dual_rest = None
    terms = ()
    for k in range(ITERS):
        last = k == ITERS - 1
        primal, ext, drift, weight, *more = primal_update(
            obj, cap, col_scale, strides[k], agains[k], weight, primal_rest, terms, last
        )
        if k == 0:
            row_scale, need = lax.optimization_barrier((row_scale, need))
        pieces = [ext] + [swap(ext, "rows", o) for o in range(1, row_groups)]
        if k == 0:
            matrix = scale_matrix(rows_of, cols_of, matrix, row_scale, col_scale)
            dual_rest = [need] + [swap(need, "cols", 2 * o) for o in range(1, chips)]
            pieces, dual_rest = lax.optimization_barrier((pieces, dual_rest))
        keep, send = forward(rows_of, cols_of, matrix, drift, pieces)
        terms = sum_columns(keep, send)
        outs = dual_update(
            strides[k],
            agains[k],
            weight,
            dual_rest,
            terms,
            need.shape[1],
            row_scale=row_scale if k == 0 else None,
            last=last,
        )
        if last:
            dual, packed = outs
            break
        if k == 0:
            demands, outs = outs[0], outs[1:]
        dual, dual_sums, dual_anchors, totals, packed, drift = outs
        primal_rest = (agains[k], totals, primal, *more)
        dual_rest = (demands, totals, dual, dual_sums, dual_anchors)
        sent = backward(rows_of, cols_of, matrix, packed, swap(packed, "cols", 1), drift)
        terms = [sent[0]] + [swap(sent[o], "rows", o) for o in range(1, row_groups)]

    other = swap(packed, "cols", 1)
    lane = lax.broadcasted_iota(jnp.int32, packed.shape, 1)
    total = packed + jnp.where(lane == 0, other, 0.0)
    step = 1
    while step < row_groups:
        total = total + swap(total, "rows", step)
        step *= 2
    final = next_weight(weight[:, 0], restart[-1], total[:, 0], total[:, 1])
    return (primal.T, dual.T, final)


def solution(mesh):
    in_specs = (
        P("rows", "cols", None, None, None),
        P("rows", "cols", None),
        P("rows", "cols", None),
        P(("cols", "rows"), None),
        P(("rows", "cols"), None),
        P(("cols", "rows"), None),
        P(),
        P(),
        P(),
    )
    out_specs = (P(("cols", "rows"), None), P(("rows", "cols"), None), P())
    return jax.shard_map(
        on_device, mesh=mesh, in_specs=in_specs, out_specs=out_specs, check_vma=False
    )
```

time: 203 us -> 167 us (0.82)
  Pallas kernels: 47.7 us -> 23.5 us
  starting transfers between devices: 70 us -> 64.3 us
  waiting for transfers between devices: 79.1 us -> 73.4 us
    pallas_call x14 -> x15, Pallas kernels: 47.7 us -> 23.5 us  [the longest x2 7.03 us: row_col_max(): pl.pallas_call(max_kernel, out_shape=(jax.ShapeDtypeStruct((RB, BLK), F32...]
    ppermute x57 -> x53, waiting for transfers between devices: 79.1 us -> 73.4 us  [swap(): return lax.ppermute(value, axis, [(i, i ^ offset) for i in range(count)])]
    ppermute x57 -> x53, starting transfers between devices: 70 us -> 64.3 us  [swap(): return lax.ppermute(value, axis, [(i, i ^ offset) for i in range(count)])]
  transfers between devices with their start and end apart: 57 -> 53, of which waited for: 45 -> 35; matrix products, arithmetic and copies ran while one was open for 0% -> 0% of each run, Pallas kernels for 0% -> 2%
where the time goes in v2:
time: 167 us
  waiting for transfers between devices  73.4 us (44%)
  starting transfers between devices  64.3 us (39%)
  Pallas kernels  23.5 us (14%)
  local copies, waits for them, and re-layouts  2.91 us (2%)
  other arithmetic  1.87 us (1%)
    ppermute x53, waiting for transfers between devices, swap(): return lax.ppermute(value, axis, [(i, i ^ offset) for i in range(count)])  73.4 us
    ppermute x53, starting transfers between devices, swap(): return lax.ppermute(value, axis, [(i, i ^ offset) for i in range(count)])  64.3 us
    pallas_call x2, Pallas kernels, row_col_max(): pl.pallas_call(max_kernel, out_shape=(jax.ShapeDtypeStruct((RB, BLK), F32...  7.03 us
    pallas_call x3, Pallas kernels, forward(): pl.pallas_call(functools.partial(forward_kernel, len(pieces)), out_shape=...  5.99 us
  transfers between devices with their start and end apart: 53, of which 35 were waited for; matrix products, arithmetic and copies ran while one was open for 0% of the time, Pallas kernels for 2%

profile of v2, /device:TPU:0, one launch (start us, length us, event | category | flops | bytes accessed | tf_op | source)
XLA Modules:
  0.0 167.0 jit_solution(472404457387015206)
XLA Ops:
  1.4 2.2 %copy-done = bf16[1,1,32,256,256]{4,3,2,1,0:T(8,128)(2,1)S(1)} copy-done((bf16[1,1,32,256,256]{4,3,2,1,0:T(8,128)(2,1)S(1)}, bf16[1,1,32,256,256]{4,3,2,1,0:T(8,128)(2,1)}, u32[]{:S(2)}) %copy-start) | copy-done | bytes 4194328
  5.9 2.6 %collective-permute-start = (f32[16,256]{1,0:T(8,128)S(1)}, f32[16,256]{1,0:T(8,128)S(1)}, u32[]{:S(2)}, u32[]{:S(2)}) collective-permute-start(f32[16,256]{1,0:T(8,128)S(1)} %get-tuple-element.66), channel_id=1, source_target_pairs={{0,8},{8,0},{16,24},{24,16},{1,9},{9,1},{17,25},{25,17},{2,10},{10... | collective-permute-start | bytes 49160 | tf_op jit(solution)/shard_map/ppermute | solution.py:27
  10.3 3.0 %collective-permute-start.1 = (f32[16,256]{1,0:T(8,128)S(1)}, f32[16,256]{1,0:T(8,128)S(1)}, u32[]{:S(2)}, u32[]{:S(2)}) collective-permute-start(f32[16,256]{1,0:T(8,128)S(1)} %max.45), channel_id=1, source_target_pairs={{0,16},{8,24},{16,0},{24,8},{1,17},{9,25},{17,1},{25,9},{2,18},{10... | collective-permute-start | bytes 49160 | tf_op jit(solution)/shard_map/ppermute | solution.py:27
  15.0 2.1 %collective-permute-done.4 = f32[16,256]{1,0:T(8,128)S(1)} collective-permute-done((f32[16,256]{1,0:T(8,128)S(1)}, f32[16,256]{1,0:T(8,128)S(1)}, u32[]{:S(2)}, u32[]{:S(2)}) %collective-permute-start.4) | collective-permute-done | bytes 16416 | tf_op jit(solution)/shard_map/ppermute | solution.py:27
  17.2 3.5 %row_col_max.2 = (f32[16,256]{1,0:T(8,128)S(1)}, f32[16,256]{1,0:T(8,128)S(1)}) custom-call(s32[32]{0:T(128)S(1)} %bitcast.48, s32[32]{0:T(128)S(1)} %bitcast.39, bf16[32,256,256]{2,1,0:T(8,128)(2,1)S(1)} %bitcast.25, f32[16,256]{1,0:T(8,128)S(1)} %add_rsqrt_fusion.r_ref, f32[16,256]{1,0:T(8,128)S(1)} %add_rsqrt_fusion.1.c_ref), custom_call_target="tpu_custom_call" | custom-call | tf_op jit(solution)/shard_map/row_col_max/pallas_call | solution.py:178
  30.0 3.5 %row_col_max.3 = (f32[16,256]{1,0:T(8,128)S(1)}, f32[16,256]{1,0:T(8,128)S(1)}) custom-call(s32[32]{0:T(128)S(1)} %bitcast.49, s32[32]{0:T(128)S(1)} %bitcast.40, bf16[32,256,256]{2,1,0:T(8,128)(2,1)S(1)} %bitcast.26, f32[16,256]{1,0:T(8,128)S(1)} %rsqrt_multiply_fusion.2.r_ref, f32[16,256]{1,0:T(8,128)S(1)} %rsqrt_multiply_fusion.3.c_ref), custom_call_target="tpu_custom_call" | custom-call | tf_op jit(solution)/shard_map/row_col_max/pallas_call | solution.py:178
  34.7 2.7 %collective-permute-done.12 = f32[16,256]{1,0:T(8,128)S(1)} collective-permute-done((f32[16,256]{1,0:T(8,128)S(1)}, f32[16,256]{1,0:T(8,128)S(1)}, u32[]{:S(2)}, u32[]{:S(2)}) %collective-permute-start.12) | collective-permute-done | bytes 16416 | tf_op jit(solution)/shard_map/ppermute | solution.py:27
  52.4 2.5 %scale_matrix.1.refs_2_ = bf16[32,256,256]{2,1,0:T(8,128)(2,1)S(1)} custom-call(s32[32]{0:T(128)S(1)} %bitcast.50, s32[32]{0:T(128)S(1)} %bitcast.41, bf16[32,256,256]{2,1,0:T(8,128)(2,1)S(1)} %bitcast.27, f32[16,256]{1,0:T(8,128)S(1)} %rsqrt_multiply_fusion.r_ref.refs_3_, f32[16,256]{1,0:T(8,128)S(1)} %rsqrt_multiply_fusion.1.refs_2_.c_ref), custom_call_target="tpu_custom_call" | custom-call | tf_op jit(solution)/shard_map/scale_matrix/pallas_call | solution.py:237
  62.2 2.8 %collective-permute-done.24 = bf16[400,128]{1,0:T(8,128)(2,1)S(1)} collective-permute-done((bf16[400,128]{1,0:T(8,128)(2,1)S(1)}, bf16[400,128]{1,0:T(8,128)(2,1)S(1)}, u32[]{:S(2)}, u32[]{:S(2)}) %collective-permute-start.24) | collective-permute-done | bytes 102432 | tf_op jit(solution)/shard_map/ppermute | solution.py:27
  67.3 3.8 %collective-permute-done.23.refs_9_ = bf16[384,128]{1,0:T(8,128)(2,1)S(1)} collective-permute-done((bf16[384,128]{1,0:T(8,128)(2,1)S(1)}, bf16[384,128]{1,0:T(8,128)(2,1)S(1)}, u32[]{:S(2)}, u32[]{:S(2)}) %collective-permute-start.23) | collective-permute-done | bytes 98336 | tf_op jit(solution)/shard_map/ppermute | solution.py:27
  80.8 5.4 %collective-permute-done.28.refs_13_ = bf16[400,128]{1,0:T(8,128)(2,1)S(1)} collective-permute-done((bf16[400,128]{1,0:T(8,128)(2,1)S(1)}, bf16[400,128]{1,0:T(8,128)(2,1)S(1)}, u32[]{:S(2)}, u32[]{:S(2)}) %collective-permute-start.28) | collective-permute-done | bytes 102432 | tf_op jit(solution)/shard_map/ppermute | solution.py:27
  89.0 2.2 %collective-permute-start.32 = (bf16[384,128]{1,0:T(8,128)(2,1)S(1)}, bf16[384,128]{1,0:T(8,128)(2,1)S(1)}, u32[]{:S(2)}, u32[]{:S(2)}) collective-permute-start(bf16[384,128]{1,0:T(8,128)(2,1)S(1)} %get-tuple-element.105.refs_4_), channel_id=1, source_target_pairs={{0,24},{8,16},{16,8},{24,0},{1,25},{9,17},{17,9},{25,1},{2,26},{10... | collective-permute-start | bytes 294920 | tf_op jit(solution)/shard_map/ppermute | solution.py:27
  91.8 6.4 %collective-permute-done.31.refs_6_ = bf16[384,128]{1,0:T(8,128)(2,1)S(1)} collective-permute-done((bf16[384,128]{1,0:T(8,128)(2,1)S(1)}, bf16[384,128]{1,0:T(8,128)(2,1)S(1)}, u32[]{:S(2)}, u32[]{:S(2)}) %collective-permute-start.31) | collective-permute-done | bytes 98336 | tf_op jit(solution)/shard_map/ppermute | solution.py:27
  104.3 2.5 %collective-permute-done.36 = bf16[400,128]{1,0:T(8,128)(2,1)S(1)} collective-permute-done((bf16[400,128]{1,0:T(8,128)(2,1)S(1)}, bf16[400,128]{1,0:T(8,128)(2,1)S(1)}, u32[]{:S(2)}, u32[]{:S(2)}) %collective-permute-start.36) | collective-permute-done | bytes 102432 | tf_op jit(solution)/shard_map/ppermute | solution.py:27
  109.3 3.1 %collective-permute-done.35.refs_9_ = bf16[384,128]{1,0:T(8,128)(2,1)S(1)} collective-permute-done((bf16[384,128]{1,0:T(8,128)(2,1)S(1)}, bf16[384,128]{1,0:T(8,128)(2,1)S(1)}, u32[]{:S(2)}, u32[]{:S(2)}) %collective-permute-start.35) | collective-permute-done | bytes 98336 | tf_op jit(solution)/shard_map/ppermute | solution.py:27
  118.2 2.1 %collective-permute-start.41 = (bf16[400,128]{1,0:T(8,128)(2,1)S(1)}, bf16[400,128]{1,0:T(8,128)(2,1)S(1)}, u32[]{:S(2)}, u32[]{:S(2)}) collective-permute-start(bf16[400,128]{1,0:T(8,128)(2,1)S(1)} %get-tuple-element.117), channel_id=1, source_target_pairs={{0,24},{8,16},{16,8},{24,0},{1,25},{9,17},{17,9},{25,1},{2,26},{10... | collective-permute-start | bytes 307208 | tf_op jit(solution)/shard_map/ppermute | solution.py:27
  120.9 7.6 %collective-permute-done.40.refs_13_ = bf16[400,128]{1,0:T(8,128)(2,1)S(1)} collective-permute-done((bf16[400,128]{1,0:T(8,128)(2,1)S(1)}, bf16[400,128]{1,0:T(8,128)(2,1)S(1)}, u32[]{:S(2)}, u32[]{:S(2)}) %collective-permute-start.40) | collective-permute-done | bytes 102432 | tf_op jit(solution)/shard_map/ppermute | solution.py:27
  134.7 6.4 %collective-permute-done.43.refs_6_ = bf16[384,128]{1,0:T(8,128)(2,1)S(1)} collective-permute-done((bf16[384,128]{1,0:T(8,128)(2,1)S(1)}, bf16[384,128]{1,0:T(8,128)(2,1)S(1)}, u32[]{:S(2)}, u32[]{:S(2)}) %collective-permute-start.43) | collective-permute-done | bytes 98336 | tf_op jit(solution)/shard_map/ppermute | solution.py:27
  141.1 2.0 %forward.5 = (f32[784,128]{1,0:T(8,128)S(1)}, bf16[784,128]{1,0:T(8,128)(2,1)S(1)}) custom-call(s32[32]{0:T(128)S(1)} %bitcast.55, s32[32]{0:T(128)S(1)} %bitcast.46, bf16[32,256,256]{2,1,0:T(8,128)(2,1)S(1)} %scale_matrix.1.refs_2_, f32[48,128]{1,0:T(8,128)S(1)} %get-tuple-element.123.refs_3_, bf16[384,128]{1,0:T(8,128)(2,1)S(1)} %get-tuple-element.124.refs_4_, ...), custom_call_target="tpu_custom_call" | custom-call | tf_op jit(solution)/shard_map/forward/pallas_call | solution.py:305
  146.9 2.8 %collective-permute-done.48 = bf16[400,128]{1,0:T(8,128)(2,1)S(1)} collective-permute-done((bf16[400,128]{1,0:T(8,128)(2,1)S(1)}, bf16[400,128]{1,0:T(8,128)(2,1)S(1)}, u32[]{:S(2)}, u32[]{:S(2)}) %collective-permute-start.48) | collective-permute-done | bytes 102432 | tf_op jit(solution)/shard_map/ppermute | solution.py:27
  151.9 3.8 %collective-permute-done.47.refs_9_ = bf16[384,128]{1,0:T(8,128)(2,1)S(1)} collective-permute-done((bf16[384,128]{1,0:T(8,128)(2,1)S(1)}, bf16[384,128]{1,0:T(8,128)(2,1)S(1)}, u32[]{:S(2)}, u32[]{:S(2)}) %collective-permute-start.47) | collective-permute-done | bytes 98336 | tf_op jit(solution)/shard_map/ppermute | solution.py:27
  159.5 2.0 %collective-permute-done.51 = f32[48,128]{1,0:T(8,128)S(1)} collective-permute-done((f32[48,128]{1,0:T(8,128)S(1)}, f32[48,128]{1,0:T(8,128)S(1)}, u32[]{:S(2)}, u32[]{:S(2)}) %collective-permute-start.51) | collective-permute-done | bytes 24608 | tf_op jit(solution)/shard_map/ppermute | solution.py:27
  161.6 2.3 %collective-permute-start.52 = (f32[48,128]{1,0:T(8,128)S(1)}, f32[48,128]{1,0:T(8,128)S(1)}, u32[]{:S(2)}, u32[]{:S(2)}) collective-permute-start(f32[48,128]{1,0:T(8,128)S(1)} %add.78), channel_id=1, source_target_pairs={{0,16},{8,24},{16,0},{24,8},{1,17},{9,25},{17,1},{25,9},{2,18},{10... | collective-permute-start | bytes 73736 | tf_op jit(solution)/shard_map/ppermute | solution.py:27
  164.0 2.4 %collective-permute-done.52 = f32[48,128]{1,0:T(8,128)S(1)} collective-permute-done((f32[48,128]{1,0:T(8,128)S(1)}, f32[48,128]{1,0:T(8,128)S(1)}, u32[]{:S(2)}, u32[]{:S(2)}) %collective-permute-start.52) | collective-permute-done | bytes 24608 | tf_op jit(solution)/shard_map/ppermute | solution.py:27
  (165 shorter events, 86.4 us)
Async XLA Ops:
  42.5 6.4 %collective-permute-start.14 = (f32[16,256]{1,0:T(8,128)S(1)}, f32[16,256]{1,0:T(8,128)S(1)}, u32[]{:S(2)}, u32[]{:S(2)}) collective-permute-start(f32[16,256]{1,0:T(8,128)S(1)} %max.56), channel_id=1, source_target_pairs={{0,4},{1,5},{2,6},{3,7},{4,0},{5,1},{6,2},{7,3},{8,12},{9,13},{10,... | collective-permute-start | bytes 49160 | tf_op jit(solution)/shard_map/ppermute | solution.py:27
  44.4 6.5 %collective-permute-start.15 = (bf16[384,128]{1,0:T(8,128)(2,1)S(1)}, bf16[384,128]{1,0:T(8,128)(2,1)S(1)}, u32[]{:S(2)}, u32[]{:S(2)}) collective-permute-start(bf16[384,128]{1,0:T(8,128)(2,1)S(1)} %get-tuple-element.83.refs_4_), channel_id=1, source_target_pairs={{0,8},{8,0},{16,24},{24,16},{1,9},{9,1},{17,25},{25,17},{2,10},{10... | collective-permute-start | bytes 294920 | tf_op jit(solution)/shard_map/ppermute | solution.py:27
  46.1 8.9 %collective-permute-start.16 = (bf16[384,128]{1,0:T(8,128)(2,1)S(1)}, bf16[384,128]{1,0:T(8,128)(2,1)S(1)}, u32[]{:S(2)}, u32[]{:S(2)}) collective-permute-start(bf16[384,128]{1,0:T(8,128)(2,1)S(1)} %get-tuple-element.83.refs_4_), channel_id=1, source_target_pairs={{0,16},{8,24},{16,0},{24,8},{1,17},{9,25},{17,1},{25,9},{2,18},{10... | collective-permute-start | bytes 294920 | tf_op jit(solution)/shard_map/ppermute | solution.py:27
  47.1 7.9 %collective-permute-start.17 = (bf16[384,128]{1,0:T(8,128)(2,1)S(1)}, bf16[384,128]{1,0:T(8,128)(2,1)S(1)}, u32[]{:S(2)}, u32[]{:S(2)}) collective-permute-start(bf16[384,128]{1,0:T(8,128)(2,1)S(1)} %get-tuple-element.83.refs_4_), channel_id=1, source_target_pairs={{0,24},{8,16},{16,8},{24,0},{1,25},{9,17},{17,9},{25,1},{2,26},{10... | collective-permute-start | bytes 294920 | tf_op jit(solution)/shard_map/ppermute | solution.py:27
  48.9 6.1 %collective-permute-start.18 = (f32[48,512]{1,0:T(8,128)S(1)}, f32[48,512]{1,0:T(8,128)S(1)}, u32[]{:S(2)}, u32[]{:S(2)}) collective-permute-start(f32[48,512]{1,0:T(8,128)S(1)} %bitcast.34), channel_id=1, source_target_pairs={{0,2},{1,3},{2,0},{3,1},{4,6},{5,7},{6,4},{7,5},{8,10},{9,11},{10,... | collective-permute-start | bytes 294920 | tf_op jit(solution)/shard_map/ppermute | solution.py:27
  51.0 5.5 %collective-permute-start.20 = (f32[48,512]{1,0:T(8,128)S(1)}, f32[48,512]{1,0:T(8,128)S(1)}, u32[]{:S(2)}, u32[]{:S(2)}) collective-permute-start(f32[48,512]{1,0:T(8,128)S(1)} %bitcast.36), channel_id=1, source_target_pairs={{0,6},{1,7},{2,4},{3,5},{4,2},{5,3},{6,0},{7,1},{8,14},{9,15},{10,... | collective-permute-start | bytes 294920 | tf_op jit(solution)/shard_map/ppermute | solution.py:27
  60.1 5.0 %collective-permute-start.24 = (bf16[400,128]{1,0:T(8,128)(2,1)S(1)}, bf16[400,128]{1,0:T(8,128)(2,1)S(1)}, u32[]{:S(2)}, u32[]{:S(2)}) collective-permute-start(bf16[400,128]{1,0:T(8,128)(2,1)S(1)} %slice.120), channel_id=1, source_target_pairs={{0,4},{1,5},{2,6},{3,7},{4,0},{5,1},{6,2},{7,3},{8,12},{9,13},{10,... | collective-permute-start | bytes 307208 | tf_op jit(solution)/shard_map/ppermute | solution.py:27
  65.1 6.0 %collective-permute-start.25 = (bf16[400,128]{1,0:T(8,128)(2,1)S(1)}, bf16[400,128]{1,0:T(8,128)(2,1)S(1)}, u32[]{:S(2)}, u32[]{:S(2)}) collective-permute-start(bf16[400,128]{1,0:T(8,128)(2,1)S(1)} %get-tuple-element.137), channel_id=1, source_target_pairs={{0,2},{1,3},{2,0},{3,1},{4,6},{5,7},{6,4},{7,5},{8,10},{9,11},{10,... | collective-permute-start | bytes 307208 | tf_op jit(solution)/shard_map/ppermute | solution.py:27
  74.5 6.3 %collective-permute-start.27 = (bf16[400,128]{1,0:T(8,128)(2,1)S(1)}, bf16[400,128]{1,0:T(8,128)(2,1)S(1)}, u32[]{:S(2)}, u32[]{:S(2)}) collective-permute-start(bf16[400,128]{1,0:T(8,128)(2,1)S(1)} %get-tuple-element.96), channel_id=1, source_target_pairs={{0,8},{8,0},{16,24},{24,16},{1,9},{9,1},{17,25},{25,17},{2,10},{10... | collective-permute-start | bytes 307208 | tf_op jit(solution)/shard_map/ppermute | solution.py:27
  75.3 10.9 %collective-permute-start.28 = (bf16[400,128]{1,0:T(8,128)(2,1)S(1)}, bf16[400,128]{1,0:T(8,128)(2,1)S(1)}, u32[]{:S(2)}, u32[]{:S(2)}) collective-permute-start(bf16[400,128]{1,0:T(8,128)(2,1)S(1)} %get-tuple-element.97), channel_id=1, source_target_pairs={{0,16},{8,24},{16,0},{24,8},{1,17},{9,25},{17,1},{25,9},{2,18},{10... | collective-permute-start | bytes 307208 | tf_op jit(solution)/shard_map/ppermute | solution.py:27
  77.2 9.0 %collective-permute-start.29 = (bf16[400,128]{1,0:T(8,128)(2,1)S(1)}, bf16[400,128]{1,0:T(8,128)(2,1)S(1)}, u32[]{:S(2)}, u32[]{:S(2)}) collective-permute-start(bf16[400,128]{1,0:T(8,128)(2,1)S(1)} %get-tuple-element.98), channel_id=1, source_target_pairs={{0,24},{8,16},{16,8},{24,0},{1,25},{9,17},{17,9},{25,1},{2,26},{10... | collective-permute-start | bytes 307208 | tf_op jit(solution)/shard_map/ppermute | solution.py:27
  86.7 5.1 %collective-permute-start.30 = (bf16[384,128]{1,0:T(8,128)(2,1)S(1)}, bf16[384,128]{1,0:T(8,128)(2,1)S(1)}, u32[]{:S(2)}, u32[]{:S(2)}) collective-permute-start(bf16[384,128]{1,0:T(8,128)(2,1)S(1)} %get-tuple-element.105.refs_4_), channel_id=1, source_target_pairs={{0,8},{8,0},{16,24},{24,16},{1,9},{9,1},{17,25},{25,17},{2,10},{10... | collective-permute-start | bytes 294920 | tf_op jit(solution)/shard_map/ppermute | solution.py:27
  88.6 9.6 %collective-permute-start.31 = (bf16[384,128]{1,0:T(8,128)(2,1)S(1)}, bf16[384,128]{1,0:T(8,128)(2,1)S(1)}, u32[]{:S(2)}, u32[]{:S(2)}) collective-permute-start(bf16[384,128]{1,0:T(8,128)(2,1)S(1)} %get-tuple-element.105.refs_4_), channel_id=1, source_target_pairs={{0,16},{8,24},{16,0},{24,8},{1,17},{9,25},{17,1},{25,9},{2,18},{10... | collective-permute-start | bytes 294920 | tf_op jit(solution)/shard_map/ppermute | solution.py:27
  89.0 9.2 %collective-permute-start.32 = (bf16[384,128]{1,0:T(8,128)(2,1)S(1)}, bf16[384,128]{1,0:T(8,128)(2,1)S(1)}, u32[]{:S(2)}, u32[]{:S(2)}) collective-permute-start(bf16[384,128]{1,0:T(8,128)(2,1)S(1)} %get-tuple-element.105.refs_4_), channel_id=1, source_target_pairs={{0,24},{8,16},{16,8},{24,0},{1,25},{9,17},{17,9},{25,1},{2,26},{10... | collective-permute-start | bytes 294920 | tf_op jit(solution)/shard_map/ppermute | solution.py:27
  102.7 5.0 %collective-permute-start.34 = (bf16[384,128]{1,0:T(8,128)(2,1)S(1)}, bf16[384,128]{1,0:T(8,128)(2,1)S(1)}, u32[]{:S(2)}, u32[]{:S(2)}) collective-permute-start(bf16[384,128]{1,0:T(8,128)(2,1)S(1)} %slice.122), channel_id=1, source_target_pairs={{0,2},{1,3},{2,0},{3,1},{4,6},{5,7},{6,4},{7,5},{8,10},{9,11},{10,... | collective-permute-start | bytes 294920 | tf_op jit(solution)/shard_map/ppermute | solution.py:27
  106.8 5.6 %collective-permute-start.37 = (bf16[400,128]{1,0:T(8,128)(2,1)S(1)}, bf16[400,128]{1,0:T(8,128)(2,1)S(1)}, u32[]{:S(2)}, u32[]{:S(2)}) collective-permute-start(bf16[400,128]{1,0:T(8,128)(2,1)S(1)} %get-tuple-element.133), channel_id=1, source_target_pairs={{0,2},{1,3},{2,0},{3,1},{4,6},{5,7},{6,4},{7,5},{8,10},{9,11},{10,... | collective-permute-start | bytes 307208 | tf_op jit(solution)/shard_map/ppermute | solution.py:27
  115.8 5.0 %collective-permute-start.39 = (bf16[400,128]{1,0:T(8,128)(2,1)S(1)}, bf16[400,128]{1,0:T(8,128)(2,1)S(1)}, u32[]{:S(2)}, u32[]{:S(2)}) collective-permute-start(bf16[400,128]{1,0:T(8,128)(2,1)S(1)} %get-tuple-element.115), channel_id=1, source_target_pairs={{0,8},{8,0},{16,24},{24,16},{1,9},{9,1},{17,25},{25,17},{2,10},{10... | collective-permute-start | bytes 307208 | tf_op jit(solution)/shard_map/ppermute | solution.py:27
  117.6 10.8 %collective-permute-start.40 = (bf16[400,128]{1,0:T(8,128)(2,1)S(1)}, bf16[400,128]{1,0:T(8,128)(2,1)S(1)}, u32[]{:S(2)}, u32[]{:S(2)}) collective-permute-start(bf16[400,128]{1,0:T(8,128)(2,1)S(1)} %get-tuple-element.116), channel_id=1, source_target_pairs={{0,16},{8,24},{16,0},{24,8},{1,17},{9,25},{17,1},{25,9},{2,18},{10... | collective-permute-start | bytes 307208 | tf_op jit(solution)/shard_map/ppermute | solution.py:27
  118.2 10.2 %collective-permute-start.41 = (bf16[400,128]{1,0:T(8,128)(2,1)S(1)}, bf16[400,128]{1,0:T(8,128)(2,1)S(1)}, u32[]{:S(2)}, u32[]{:S(2)}) collective-permute-start(bf16[400,128]{1,0:T(8,128)(2,1)S(1)} %get-tuple-element.117), channel_id=1, source_target_pairs={{0,24},{8,16},{16,8},{24,0},{1,25},{9,17},{17,9},{25,1},{2,26},{10... | collective-permute-start | bytes 307208 | tf_op jit(solution)/shard_map/ppermute | solution.py:27
  129.6 5.1 %collective-permute-start.42 = (bf16[384,128]{1,0:T(8,128)(2,1)S(1)}, bf16[384,128]{1,0:T(8,128)(2,1)S(1)}, u32[]{:S(2)}, u32[]{:S(2)}) collective-permute-start(bf16[384,128]{1,0:T(8,128)(2,1)S(1)} %get-tuple-element.124.refs_4_), channel_id=1, source_target_pairs={{0,8},{8,0},{16,24},{24,16},{1,9},{9,1},{17,25},{25,17},{2,10},{10... | collective-permute-start | bytes 294920 | tf_op jit(solution)/shard_map/ppermute | solution.py:27
  131.5 9.6 %collective-permute-start.43 = (bf16[384,128]{1,0:T(8,128)(2,1)S(1)}, bf16[384,128]{1,0:T(8,128)(2,1)S(1)}, u32[]{:S(2)}, u32[]{:S(2)}) collective-permute-start(bf16[384,128]{1,0:T(8,128)(2,1)S(1)} %get-tuple-element.124.refs_4_), channel_id=1, source_target_pairs={{0,16},{8,24},{16,0},{24,8},{1,17},{9,25},{17,1},{25,9},{2,18},{10... | collective-permute-start | bytes 294920 | tf_op jit(solution)/shard_map/ppermute | solution.py:27
  132.1 9.0 %collective-permute-start.44 = (bf16[384,128]{1,0:T(8,128)(2,1)S(1)}, bf16[384,128]{1,0:T(8,128)(2,1)S(1)}, u32[]{:S(2)}, u32[]{:S(2)}) collective-permute-start(bf16[384,128]{1,0:T(8,128)(2,1)S(1)} %get-tuple-element.124.refs_4_), channel_id=1, source_target_pairs={{0,24},{8,16},{16,8},{24,0},{1,25},{9,17},{17,9},{25,1},{2,26},{10... | collective-permute-start | bytes 294920 | tf_op jit(solution)/shard_map/ppermute | solution.py:27
  144.7 5.0 %collective-permute-start.48 = (bf16[400,128]{1,0:T(8,128)(2,1)S(1)}, bf16[400,128]{1,0:T(8,128)(2,1)S(1)}, u32[]{:S(2)}, u32[]{:S(2)}) collective-permute-start(bf16[400,128]{1,0:T(8,128)(2,1)S(1)} %slice.118), channel_id=1, source_target_pairs={{0,4},{1,5},{2,6},{3,7},{4,0},{5,1},{6,2},{7,3},{8,12},{9,13},{10,... | collective-permute-start | bytes 307208 | tf_op jit(solution)/shard_map/ppermute | solution.py:27
  149.7 6.0 %collective-permute-start.49 = (bf16[400,128]{1,0:T(8,128)(2,1)S(1)}, bf16[400,128]{1,0:T(8,128)(2,1)S(1)}, u32[]{:S(2)}, u32[]{:S(2)}) collective-permute-start(bf16[400,128]{1,0:T(8,128)(2,1)S(1)} %get-tuple-element.129), channel_id=1, source_target_pairs={{0,2},{1,3},{2,0},{3,1},{4,6},{5,7},{6,4},{7,5},{8,10},{9,11},{10,... | collective-permute-start | bytes 307208 | tf_op jit(solution)/shard_map/ppermute | solution.py:27
  (39 other events, 307.4 us)

commit v3 on v2

--- a/solution.py
+++ b/solution.py
@@ -22,7 +22,13 @@
 PARAMS = pltpu.CompilerParams(vmem_limit_bytes=32 * 1024 * 1024)
 
 
+def offsets(groups):
+    return [0] + [o ^ 3 if o < 3 else o for o in range(1, groups)]
+
+
 def swap(value, axis, offset):
+    if offset == 0:
+        return value
     count = lax.axis_size(axis)
     return lax.ppermute(value, axis, [(i, i ^ offset) for i in range(count)])
 
@@ -71,6 +77,16 @@
     return jnp.concatenate(pieces, axis=0).T[: tail_rows()]
 
 
+def to_rows(values):
+    scenarios = values[0].shape[0]
+    lane = lax.broadcasted_iota(jnp.int32, values[0].shape, 1)
+    tile = jnp.zeros(values[0].shape, F32)
+    for place, value in enumerate(values):
+        tile = jnp.where(lane == place, value, tile)
+    rest = jnp.zeros((LANES - scenarios, LANES), F32)
+    return jnp.concatenate([tile, rest], axis=0).T[:8]
+
+
 def from_tail(tail, scenarios, first=0, last=LANES):
     rest = jnp.zeros((LANES - tail.shape[0], LANES), F32)
     square = jnp.concatenate([tail, rest], axis=0).T
@@ -87,8 +103,9 @@
 
 
 def first_max_kernel(
-    places_vmem, a, row_out, col_out, places_ref, sem, racc, cacc
+    places_vmem, a, row_out, col_out, same, places_ref, sem, racc, cacc
 ):
+    del same
     places = pltpu.make_async_copy(places_vmem, places_ref, sem)
     places.start()
     racc[...] = jnp.zeros_like(racc)
@@ -160,9 +177,11 @@
         out_shape=(
             jax.ShapeDtypeStruct((RB, BLK), F32),
             jax.ShapeDtypeStruct((CB, BLK), F32),
+            jax.ShapeDtypeStruct(matrix.shape, BF16),
         ),
         in_specs=[VMEM, VMEM],
-        out_specs=(VMEM, VMEM),
+        out_specs=(VMEM, VMEM, VMEM),
+        input_output_aliases={1: 2},
         scratch_shapes=[
             pltpu.SMEM((2, count), jnp.int32),
             pltpu.SemaphoreType.DMA,
@@ -272,7 +291,7 @@
     scenarios = x.shape[1]
     me = lax.axis_index("rows")
     units = x.shape[0] // pieces
-    for o, piece in enumerate(piece_refs):
+    for o, piece in zip(offsets(pieces), piece_refs):
         for k in range(units):
             x[(me ^ o) * units + k] = piece[k * scenarios : (k + 1) * scenarios, :]
     acc[...] = jnp.zeros_like(acc)
@@ -339,7 +358,7 @@
     tail = to_tail([(0, from_tail(tail, scenarios)), (3, drift[...])])
     me = lax.axis_index("rows")
     units = acc.shape[0] // (1 + len(sends))
-    for o, out in enumerate((keep,) + tuple(sends)):
+    for o, out in zip(offsets(1 + len(sends)), (keep,) + tuple(sends)):
         for k in range(units):
             out[pl.ds(k * scenarios, scenarios), :] = acc[(me ^ o) * units + k].astype(
                 out.dtype
@@ -375,45 +394,50 @@
     )
 
 
-def primal_kernel(first, last, terms, *refs):
-    obj, cap, c_ref, stride_ref, again_ref, weight_ref = refs[:6]
-    refs = refs[6:]
+def column(ref, lane):
+    return jnp.broadcast_to(ref[:, lane : lane + 1], (ref.shape[0], LANES))
+
+
+def primal_kernel(k, terms, *refs):
+    first, last = k == 0, k == ITERS - 1
+    obj, cap, c_ref, plan = refs[:4]
+    refs = refs[4:]
     if not first:
-        before_ref, wt_ref, state, sums, anchors = refs[:5]
+        weight_ref, wt_ref, state, sums, anchors = refs[:5]
         term_refs = refs[5 : 5 + terms]
         refs = refs[5 + terms :]
     state_out, ext, drift, weight_out = refs[:4]
     width = obj.shape[1]
-    weight = weight_ref[...]
-    stride = stride_ref[...]
-    again = again_ref[...] == 1
-    totals = stride
-    if not first:
-        totals = wt_ref[...] + stride
+    stride = column(plan, k)
+    again = column(plan, ITERS + k) == 1
+    if first:
+        totals, weight = stride, column(plan, 2 * ITERS)
+    else:
+        totals, weight = wt_ref[...] + stride, weight_ref[...]
         scenarios = weight.shape[0]
         tail = sum(ref[ref.shape[0] - tail_rows() :, :].astype(F32) for ref in term_refs)
         drift_dual = from_tail(tail, scenarios, 0, 3)
         drift_primal = from_tail(tail, scenarios, 3, 6)
-        weight = next_weight(weight, before_ref[...], drift_dual, drift_primal)
+        weight = next_weight(weight, column(plan, ITERS + k - 1), drift_dual, drift_primal)
     weight_out[...] = weight
     step = stride / weight
     place = lax.axis_index("rows")
     units = width // LANES
     moved = jnp.zeros_like(weight)
-    for k in range(units):
-        span = pl.ds(k * LANES, LANES)
-        scale = unit_row(c_ref, place * units + k)
+    for u in range(units):
+        span = pl.ds(u * LANES, LANES)
+        scale = unit_row(c_ref, place * units + u)
         gradient = obj[:, span] * scale
         upper = cap[:, span] / scale
         if first:
             old = total = anchor = jnp.zeros_like(gradient)
         else:
             old, total, anchor = state[:, span], sums[:, span], anchors[:, span]
-            rows = pl.ds(k * obj.shape[0], obj.shape[0])
+            rows = pl.ds(u * obj.shape[0], obj.shape[0])
             product = sum(ref[rows, :].astype(F32) for ref in term_refs)
             gradient = gradient - product
         new = jnp.minimum(jnp.maximum(old - step * gradient, 0.0), upper)
-        ext[pl.ds(k * obj.shape[0], obj.shape[0]), :] = (2.0 * new - old).astype(BF16)
+        ext[pl.ds(u * obj.shape[0], obj.shape[0]), :] = (2.0 * new - old).astype(BF16)
         new, total, anchor, square = settle(again, stride, totals, new, total, anchor)
         state_out[:, span] = new
         if not last:
@@ -424,14 +448,15 @@
     drift[...] = moved
 
 
-def primal_update(obj, cap, col_scale, stride, again, weight, rest, terms, last):
+def primal_update(k, obj, cap, col_scale, plan, rest, terms):
     shape = obj.shape
     tile = jax.ShapeDtypeStruct((shape[0], LANES), F32)
     whole = jax.ShapeDtypeStruct(shape, F32)
     ext = jax.ShapeDtypeStruct((shape[1] // LANES * shape[0], LANES), BF16)
-    operands = (obj, cap, col_scale, stride, again, weight) + tuple(rest or ()) + tuple(terms)
-    return pl.pallas_call(
-        functools.partial(primal_kernel, rest is None, last, len(terms)),
+    operands = (obj, cap, col_scale, plan) + tuple(rest) + tuple(terms)
+    last = k == ITERS - 1
+    return pl.pallas_call(
+        functools.partial(primal_kernel, k, len(terms)),
         out_shape=[whole, ext, tile, tile] + [whole] * (0 if last else 2),
         in_specs=[VMEM] * len(operands),
         out_specs=[VMEM] * (4 if last else 6),
@@ -440,9 +465,10 @@
     )(*operands)
 
 
-def dual_kernel(first, last, chips, *refs):
-    stride_ref, again_ref, weight_ref = refs[:3]
-    refs = refs[3:]
+def dual_kernel(iteration, chips, *refs):
+    first, last = iteration == 0, iteration == ITERS - 1
+    plan, weight_ref = refs[:2]
+    refs = refs[2:]
     if first:
         r_ref, refs = refs[0], refs[1:]
         demands, refs = refs[:chips], refs[chips:]
@@ -451,14 +477,14 @@
         refs = refs[5:]
     parts, refs = (refs[:2], refs[2:4]), refs[4:]
     if last:
-        out, drifts, state_out = refs
+        out, drifts, weights, state_out = refs
     else:
         if first:
             need, refs = refs[0], refs[1:]
         state_out, sums_out, anchors_out, wt_out, packed, drift_out = refs
-    stride = stride_ref[...]
+    stride = column(plan, iteration)
     scenarios = stride.shape[0]
-    again = again_ref[...] == 1
+    again = column(plan, ITERS + iteration) == 1
     totals = stride if first else wt_ref[...] + stride
     step = stride * weight_ref[...]
     place = lax.axis_index("cols")
@@ -495,8 +521,8 @@
     tail = sum(ref[start:, :].astype(F32) for ref in parts[1])
     dual, primal = lane_sum(moved), from_tail(tail, scenarios)
     if last:
-        lane = lax.broadcasted_iota(jnp.int32, dual.shape, 1)
-        drifts[...] = jnp.where(lane == 0, dual, jnp.where(lane == 1, primal, 0.0))
+        drifts[...] = to_rows([dual, primal])
+        weights[...] = to_rows([weight_ref[...]])
         for k in range(units):
             start = pl.multiple_of((me * units + k) * scenarios, 8)
             out[:, k * LANES : (k + 1) * LANES] = state_out[pl.ds(start, scenarios), :]
@@ -506,24 +532,24 @@
         drift_out[...] = primal
 
 
-def dual_update(stride, again, weight, rest, terms, width, row_scale=None, last=False):
-    first = row_scale is not None
+def dual_update(iteration, plan, weight, rest, terms, width):
+    first, last = iteration == 0, iteration == ITERS - 1
     chips = lax.axis_size("cols") // 2
-    scenarios = stride.shape[0]
+    scenarios = plan.shape[0]
     rows = half_rows(scenarios)
     tile = jax.ShapeDtypeStruct((scenarios, LANES), F32)
     half = jax.ShapeDtypeStruct((rows - tail_rows(), LANES), F32)
-    operands = (stride, again, weight) + ((row_scale,) if first else ())
-    operands += tuple(rest) + tuple(terms)
+    operands = (plan, weight) + tuple(rest) + tuple(terms)
     scratch = []
     if last:
-        out_shape = [jax.ShapeDtypeStruct((scenarios, width), F32), tile]
+        rows = jax.ShapeDtypeStruct((8, LANES), F32)
+        out_shape = [jax.ShapeDtypeStruct((scenarios, width), F32), rows, rows]
         scratch = [pltpu.VMEM(half.shape, F32)]
     else:
         packed = jax.ShapeDtypeStruct((rows, LANES), BF16)
         out_shape = [half] * (3 + first) + [tile, packed, tile]
     return pl.pallas_call(
-        functools.partial(dual_kernel, first, last, chips),
+        functools.partial(dual_kernel, iteration, chips),
         out_shape=out_shape,
         in_specs=[VMEM] * len(operands),
         out_specs=[VMEM] * len(out_shape),
@@ -531,6 +557,21 @@
         compiler_params=PARAMS,
         name="dual_update",
     )(*operands)
+
+
+def copy_kernel(source, out):
+    out[...] = source[...]
+
+
+def hand_over(value):
+    return pl.pallas_call(
+        copy_kernel,
+        out_shape=jax.ShapeDtypeStruct(value.shape, value.dtype),
+        in_specs=[VMEM],
+        out_specs=VMEM,
+        compiler_params=PARAMS,
+        name="hand_over",
+    )(value)
 
 
 def sum_columns(keep, send):
@@ -558,67 +599,60 @@
     row_groups = lax.axis_size("rows")
     scenarios = objective.shape[1]
     obj, cap, need = objective.T, capacity.T, demand.T
-    strides = jnp.broadcast_to(step_size[:, :, None], (ITERS, scenarios, LANES))
-    agains = jnp.broadcast_to(restart[:, :, None], (ITERS, scenarios, LANES))
-    weight = jnp.broadcast_to(primal_weight[:, None], (scenarios, LANES))
+    plan = jnp.concatenate([step_size, restart.astype(F32), primal_weight[None]]).T
+    plan = jnp.pad(plan, ((0, 0), (0, LANES - plan.shape[1])))
 
     matrix = blocks[0, 0]
-    row_top, col_top = first_max(jnp.stack([rows_of, cols_of]), matrix)
+    row_top, col_top, matrix = first_max(jnp.stack([rows_of, cols_of]), matrix)
     row_top, col_top = exchange_max(row_top, col_top)
     row_scale = 1.0 / jnp.sqrt(row_top + epsilon)
     col_scale = 1.0 / jnp.sqrt(col_top + epsilon)
     for sweep in range(1, PASSES):
         row_top, col_top = row_col_max(rows_of, cols_of, matrix, row_scale, col_scale)
+        if sweep == PASSES - 1:
+            row_top, need = lax.optimization_barrier((row_top, need))
         row_top, col_top = exchange_max(row_top, col_top, sweep == PASSES - 1)
         row_scale = row_scale / jnp.sqrt(row_top + epsilon)
         col_scale = col_scale / jnp.sqrt(col_top + epsilon)
 
-    primal_rest = dual_rest = None
-    terms = ()
+    primal_rest = terms = ()
     for k in range(ITERS):
         last = k == ITERS - 1
         primal, ext, drift, weight, *more = primal_update(
-            obj, cap, col_scale, strides[k], agains[k], weight, primal_rest, terms, last
+            k, obj, cap, col_scale, plan, primal_rest, terms
         )
-        if k == 0:
-            row_scale, need = lax.optimization_barrier((row_scale, need))
-        pieces = [ext] + [swap(ext, "rows", o) for o in range(1, row_groups)]
+        pieces = [swap(ext, "rows", o) for o in offsets(row_groups)]
         if k == 0:
             matrix = scale_matrix(rows_of, cols_of, matrix, row_scale, col_scale)
             dual_rest = [need] + [swap(need, "cols", 2 * o) for o in range(1, chips)]
             pieces, dual_rest = lax.optimization_barrier((pieces, dual_rest))
+            dual_rest = [row_scale] + dual_rest
         keep, send = forward(rows_of, cols_of, matrix, drift, pieces)
         terms = sum_columns(keep, send)
-        outs = dual_update(
-            strides[k],
-            agains[k],
-            weight,
-            dual_rest,
-            terms,
-            need.shape[1],
-            row_scale=row_scale if k == 0 else None,
-            last=last,
-        )
+        outs = dual_update(k, plan, weight, dual_rest, terms, need.shape[1])
         if last:
-            dual, packed = outs
+            dual, packed, weight = outs
             break
         if k == 0:
             demands, outs = outs[0], outs[1:]
         dual, dual_sums, dual_anchors, totals, packed, drift = outs
-        primal_rest = (agains[k], totals, primal, *more)
+        primal_rest = (weight, totals, primal, *more)
         dual_rest = (demands, totals, dual, dual_sums, dual_anchors)
         sent = backward(rows_of, cols_of, matrix, packed, swap(packed, "cols", 1), drift)
-        terms = [sent[0]] + [swap(sent[o], "rows", o) for o in range(1, row_groups)]
+        terms = [swap(value, "rows", o) for value, o in zip(sent, offsets(row_groups))]
 
     other = swap(packed, "cols", 1)
-    lane = lax.broadcasted_iota(jnp.int32, packed.shape, 1)
-    total = packed + jnp.where(lane == 0, other, 0.0)
+    row = lax.broadcasted_iota(jnp.int32, packed.shape, 0)
+    total = packed + jnp.where(row == 0, other, 0.0)
     step = 1
     while step < row_groups:
         total = total + swap(total, "rows", step)
         step *= 2
-    final = next_weight(weight[:, 0], restart[-1], total[:, 0], total[:, 1])
-    return (primal.T, dual.T, final)
+    weight, drift_dual, drift_primal = (
+        value[:scenarios] for value in (weight[0], total[0], total[1])
+    )
+    final = next_weight(weight, restart[-1], drift_dual, drift_primal)
+    return (hand_over(primal).T, hand_over(dual).T, final)
 
 
 def solution(mesh):

time: 167 us -> 161 us (0.964)
  waiting for transfers between devices: 73.4 us -> 66.5 us
  local copies, waits for them, and re-layouts: 2.91 us -> 4.61 us
    ppermute x53, waiting for transfers between devices: 73.4 us -> 66.5 us  [swap(): return lax.ppermute(value, axis, [(i, i ^ offset) for i in range(count)])]
    unnamed x20 -> x21, local copies, waits for them, and re-layouts: 2.23 us -> 4.43 us
    pallas_call x6 -> x8, Pallas kernels: 3.29 us -> 3.72 us  [the longest x3 1.41 us: dual_update(): pl.pallas_call(functools.partial(dual_kernel, iteration, chips), out_shap...]
where the time goes in v3:
time: 161 us
  waiting for transfers between devices  66.5 us (41%)
  starting transfers between devices  63.7 us (40%)
  Pallas kernels  24.1 us (15%)
  local copies, waits for them, and re-layouts  4.61 us (3%)
    ppermute x53, waiting for transfers between devices, swap(): return lax.ppermute(value, axis, [(i, i ^ offset) for i in range(count)])  66.5 us
    ppermute x53, starting transfers between devices, swap(): return lax.ppermute(value, axis, [(i, i ^ offset) for i in range(count)])  63.7 us
    pallas_call x2, Pallas kernels, row_col_max(): pl.pallas_call(max_kernel, out_shape=(jax.ShapeDtypeStruct((RB, BLK), F32...  7.15 us
    pallas_call x3, Pallas kernels, forward(): pl.pallas_call(functools.partial(forward_kernel, len(pieces)), out_shape=...  5.99 us
    unnamed x21, local copies, waits for them, and re-layouts  4.43 us
  transfers between devices with their start and end apart: 53, of which 35 were waited for; matrix products, arithmetic and copies ran while one was open for 0% of the time, Pallas kernels for 2%

profile of v3, /device:TPU:0, one launch (start us, length us, event | category | flops | bytes accessed | tf_op | source)
XLA Modules:
  0.0 161.0 jit_solution(5420642779449503029)
XLA Ops:
  0.7 2.2 %copy.19 = bf16[1,1,32,256,256]{4,3,2,1,0:T(8,128)(2,1)S(1)} copy(bf16[1,1,32,256,256]{4,3,2,1,0:T(8,128)(2,1)} %param.9) | data formatting | bytes 8388608
  5.2 2.7 %collective-permute-start = (f32[16,256]{1,0:T(8,128)S(1)}, f32[16,256]{1,0:T(8,128)S(1)}, u32[]{:S(2)}, u32[]{:S(2)}) collective-permute-start(f32[16,256]{1,0:T(8,128)S(1)} %get-tuple-element.68), channel_id=1, source_target_pairs={{0,8},{8,0},{16,24},{24,16},{1,9},{9,1},{17,25},{25,17},{2,10},{10... | collective-permute-start | bytes 49160 | tf_op jit(solution)/shard_map/ppermute | solution.py:33
  9.6 3.0 %collective-permute-start.1 = (f32[16,256]{1,0:T(8,128)S(1)}, f32[16,256]{1,0:T(8,128)S(1)}, u32[]{:S(2)}, u32[]{:S(2)}) collective-permute-start(f32[16,256]{1,0:T(8,128)S(1)} %max.45), channel_id=1, source_target_pairs={{0,16},{8,24},{16,0},{24,8},{1,17},{9,25},{17,1},{25,9},{2,18},{10... | collective-permute-start | bytes 49160 | tf_op jit(solution)/shard_map/ppermute | solution.py:33
  16.5 3.6 %row_col_max.2 = (f32[16,256]{1,0:T(8,128)S(1)}, f32[16,256]{1,0:T(8,128)S(1)}) custom-call(s32[32]{0:T(128)S(1)} %bitcast.43, s32[32]{0:T(128)S(1)} %bitcast.34, bf16[32,256,256]{2,1,0:T(8,128)(2,1)S(1)} %get-tuple-element.69.a, f32[16,256]{1,0:T(8,128)S(1)} %add_rsqrt_fusion.r_ref, f32[16,256]{1,0:T(8,128)S(1)} %add_rsqrt_fusion.1.c_ref), custom_call_target="tpu_custom_call" | custom-call | tf_op jit(solution)/shard_map/row_col_max/pallas_call | solution.py:197
  29.4 3.6 %row_col_max.3 = (f32[16,256]{1,0:T(8,128)S(1)}, f32[16,256]{1,0:T(8,128)S(1)}) custom-call(s32[32]{0:T(128)S(1)} %bitcast.44, s32[32]{0:T(128)S(1)} %bitcast.35, bf16[32,256,256]{2,1,0:T(8,128)(2,1)S(1)} %get-tuple-element.69.a, f32[16,256]{1,0:T(8,128)S(1)} %rsqrt_multiply_fusion.2.r_ref, f32[16,256]{1,0:T(8,128)S(1)} %rsqrt_multiply_fusion.3.c_ref), custom_call_target="tpu_custom_call" | custom-call | tf_op jit(solution)/shard_map/row_col_max/pallas_call | solution.py:197
  34.1 2.7 %collective-permute-done.12 = f32[16,256]{1,0:T(8,128)S(1)} collective-permute-done((f32[16,256]{1,0:T(8,128)S(1)}, f32[16,256]{1,0:T(8,128)S(1)}, u32[]{:S(2)}, u32[]{:S(2)}) %collective-permute-start.12) | collective-permute-done | bytes 16416 | tf_op jit(solution)/shard_map/ppermute | solution.py:33
  50.7 2.2 %copy-done.1 = bf16[32,256,256]{2,1,0:T(8,128)(2,1)S(1)} copy-done((bf16[32,256,256]{2,1,0:T(8,128)(2,1)S(1)}, bf16[32,256,256]{2,1,0:T(8,128)(2,1)}, u32[]{:S(2)}) %copy-start.1) | copy-done | bytes 4194328
  52.8 2.5 %scale_matrix.1.refs_2_ = bf16[32,256,256]{2,1,0:T(8,128)(2,1)S(1)} custom-call(s32[32]{0:T(128)S(1)} %bitcast.45, s32[32]{0:T(128)S(1)} %bitcast.36, bf16[32,256,256]{2,1,0:T(8,128)(2,1)S(1)} %copy-done.1, f32[16,256]{1,0:T(8,128)S(1)} %rsqrt_multiply_fusion.r_ref.refs_2_, f32[16,256]{1,0:T(8,128)S(1)} %rsqrt_multiply_fusion.1.refs_2_.c_ref), custom_call_target="tpu_custom_call" | custom-call | tf_op jit(solution)/shard_map/scale_matrix/pallas_call | solution.py:256
  61.3 2.9 %collective-permute-done.24 = bf16[400,128]{1,0:T(8,128)(2,1)S(1)} collective-permute-done((bf16[400,128]{1,0:T(8,128)(2,1)S(1)}, bf16[400,128]{1,0:T(8,128)(2,1)S(1)}, u32[]{:S(2)}, u32[]{:S(2)}) %collective-permute-start.24) | collective-permute-done | bytes 102432 | tf_op jit(solution)/shard_map/ppermute | solution.py:33
  66.4 3.4 %collective-permute-done.23.refs_8_ = bf16[384,128]{1,0:T(8,128)(2,1)S(1)} collective-permute-done((bf16[384,128]{1,0:T(8,128)(2,1)S(1)}, bf16[384,128]{1,0:T(8,128)(2,1)S(1)}, u32[]{:S(2)}, u32[]{:S(2)}) %collective-permute-start.23) | collective-permute-done | bytes 98336 | tf_op jit(solution)/shard_map/ppermute | solution.py:33
  73.6 2.5 %collective-permute-start.28 = (bf16[400,128]{1,0:T(8,128)(2,1)S(1)}, bf16[400,128]{1,0:T(8,128)(2,1)S(1)}, u32[]{:S(2)}, u32[]{:S(2)}) collective-permute-start(bf16[400,128]{1,0:T(8,128)(2,1)S(1)} %get-tuple-element.100), channel_id=1, source_target_pairs={{0,8},{8,0},{16,24},{24,16},{1,9},{9,1},{17,25},{25,17},{2,10},{10... | collective-permute-start | bytes 307208 | tf_op jit(solution)/shard_map/ppermute | solution.py:33
  77.7 5.5 %collective-permute-done.27.refs_10_ = bf16[400,128]{1,0:T(8,128)(2,1)S(1)} collective-permute-done((bf16[400,128]{1,0:T(8,128)(2,1)S(1)}, bf16[400,128]{1,0:T(8,128)(2,1)S(1)}, u32[]{:S(2)}, u32[]{:S(2)}) %collective-permute-start.27) | collective-permute-done | bytes 102432 | tf_op jit(solution)/shard_map/ppermute | solution.py:33
  83.8 2.8 %collective-permute-start.30 = (bf16[384,128]{1,0:T(8,128)(2,1)S(1)}, bf16[384,128]{1,0:T(8,128)(2,1)S(1)}, u32[]{:S(2)}, u32[]{:S(2)}) collective-permute-start(bf16[384,128]{1,0:T(8,128)(2,1)S(1)} %get-tuple-element.108.refs_4_), channel_id=1, source_target_pairs={{0,16},{8,24},{16,0},{24,8},{1,17},{9,25},{17,1},{25,9},{2,18},{10... | collective-permute-start | bytes 294920 | tf_op jit(solution)/shard_map/ppermute | solution.py:33
  88.7 2.4 %collective-permute-done.30.refs_5_ = bf16[384,128]{1,0:T(8,128)(2,1)S(1)} collective-permute-done((bf16[384,128]{1,0:T(8,128)(2,1)S(1)}, bf16[384,128]{1,0:T(8,128)(2,1)S(1)}, u32[]{:S(2)}, u32[]{:S(2)}) %collective-permute-start.30) | collective-permute-done | bytes 98336 | tf_op jit(solution)/shard_map/ppermute | solution.py:33
  91.9 3.8 %collective-permute-done.32.refs_7_ = bf16[384,128]{1,0:T(8,128)(2,1)S(1)} collective-permute-done((bf16[384,128]{1,0:T(8,128)(2,1)S(1)}, bf16[384,128]{1,0:T(8,128)(2,1)S(1)}, u32[]{:S(2)}, u32[]{:S(2)}) %collective-permute-start.32) | collective-permute-done | bytes 98336 | tf_op jit(solution)/shard_map/ppermute | solution.py:33
  101.8 2.5 %collective-permute-done.36 = bf16[400,128]{1,0:T(8,128)(2,1)S(1)} collective-permute-done((bf16[400,128]{1,0:T(8,128)(2,1)S(1)}, bf16[400,128]{1,0:T(8,128)(2,1)S(1)}, u32[]{:S(2)}, u32[]{:S(2)}) %collective-permute-start.36) | collective-permute-done | bytes 102432 | tf_op jit(solution)/shard_map/ppermute | solution.py:33
  106.9 3.5 %collective-permute-done.35.refs_8_ = bf16[384,128]{1,0:T(8,128)(2,1)S(1)} collective-permute-done((bf16[384,128]{1,0:T(8,128)(2,1)S(1)}, bf16[384,128]{1,0:T(8,128)(2,1)S(1)}, u32[]{:S(2)}, u32[]{:S(2)}) %collective-permute-start.35) | collective-permute-done | bytes 98336 | tf_op jit(solution)/shard_map/ppermute | solution.py:33
  116.2 2.2 %collective-permute-start.41 = (bf16[400,128]{1,0:T(8,128)(2,1)S(1)}, bf16[400,128]{1,0:T(8,128)(2,1)S(1)}, u32[]{:S(2)}, u32[]{:S(2)}) collective-permute-start(bf16[400,128]{1,0:T(8,128)(2,1)S(1)} %get-tuple-element.120), channel_id=1, source_target_pairs={{0,24},{8,16},{16,8},{24,0},{1,25},{9,17},{17,9},{25,1},{2,26},{10... | collective-permute-start | bytes 307208 | tf_op jit(solution)/shard_map/ppermute | solution.py:33
  118.3 4.7 %collective-permute-done.39.refs_10_ = bf16[400,128]{1,0:T(8,128)(2,1)S(1)} collective-permute-done((bf16[400,128]{1,0:T(8,128)(2,1)S(1)}, bf16[400,128]{1,0:T(8,128)(2,1)S(1)}, u32[]{:S(2)}, u32[]{:S(2)}) %collective-permute-start.39) | collective-permute-done | bytes 102432 | tf_op jit(solution)/shard_map/ppermute | solution.py:33
  124.8 2.7 %collective-permute-start.42 = (bf16[384,128]{1,0:T(8,128)(2,1)S(1)}, bf16[384,128]{1,0:T(8,128)(2,1)S(1)}, u32[]{:S(2)}, u32[]{:S(2)}) collective-permute-start(bf16[384,128]{1,0:T(8,128)(2,1)S(1)} %get-tuple-element.127.refs_4_), channel_id=1, source_target_pairs={{0,16},{8,24},{16,0},{24,8},{1,17},{9,25},{17,1},{25,9},{2,18},{10... | collective-permute-start | bytes 294920 | tf_op jit(solution)/shard_map/ppermute | solution.py:33
  132.5 4.1 %collective-permute-done.44.refs_7_ = bf16[384,128]{1,0:T(8,128)(2,1)S(1)} collective-permute-done((bf16[384,128]{1,0:T(8,128)(2,1)S(1)}, bf16[384,128]{1,0:T(8,128)(2,1)S(1)}, u32[]{:S(2)}, u32[]{:S(2)}) %collective-permute-start.44) | collective-permute-done | bytes 98336 | tf_op jit(solution)/shard_map/ppermute | solution.py:33
  142.3 2.9 %collective-permute-done.48 = bf16[400,128]{1,0:T(8,128)(2,1)S(1)} collective-permute-done((bf16[400,128]{1,0:T(8,128)(2,1)S(1)}, bf16[400,128]{1,0:T(8,128)(2,1)S(1)}, u32[]{:S(2)}, u32[]{:S(2)}) %collective-permute-start.48) | collective-permute-done | bytes 102432 | tf_op jit(solution)/shard_map/ppermute | solution.py:33
  147.3 3.4 %collective-permute-done.47.refs_8_ = bf16[384,128]{1,0:T(8,128)(2,1)S(1)} collective-permute-done((bf16[384,128]{1,0:T(8,128)(2,1)S(1)}, bf16[384,128]{1,0:T(8,128)(2,1)S(1)}, u32[]{:S(2)}, u32[]{:S(2)}) %collective-permute-start.47) | collective-permute-done | bytes 98336 | tf_op jit(solution)/shard_map/ppermute | solution.py:33
  153.1 2.9 %collective-permute-done.51 = f32[8,128]{1,0:T(8,128)S(1)} collective-permute-done((f32[8,128]{1,0:T(8,128)S(1)}, f32[8,128]{1,0:T(8,128)S(1)}, u32[]{:S(2)}, u32[]{:S(2)}) %collective-permute-start.51) | collective-permute-done | bytes 4128 | tf_op jit(solution)/shard_map/ppermute | solution.py:33
  (161 shorter events, 85.5 us)
Async XLA Ops:
  36.8 6.6 %collective-permute-start.13 = (f32[16,256]{1,0:T(8,128)S(1)}, f32[16,256]{1,0:T(8,128)S(1)}, u32[]{:S(2)}, u32[]{:S(2)}) collective-permute-start(f32[16,256]{1,0:T(8,128)S(1)} %max.57), channel_id=1, source_target_pairs={{0,16},{8,24},{16,0},{24,8},{1,17},{9,25},{17,1},{25,9},{2,18},{10... | collective-permute-start | bytes 49160 | tf_op jit(solution)/shard_map/ppermute | solution.py:33
  38.1 5.2 %collective-permute-start.11 = (f32[16,256]{1,0:T(8,128)S(1)}, f32[16,256]{1,0:T(8,128)S(1)}, u32[]{:S(2)}, u32[]{:S(2)}) collective-permute-start(f32[16,256]{1,0:T(8,128)S(1)} %max.55), channel_id=1, source_target_pairs={{0,2},{1,3},{2,0},{3,1},{4,6},{5,7},{6,4},{7,5},{8,10},{9,11},{10,... | collective-permute-start | bytes 49160 | tf_op jit(solution)/shard_map/ppermute | solution.py:33
  39.8 9.4 %collective-permute-start.18 = (f32[48,512]{1,0:T(8,128)S(1)}, f32[48,512]{1,0:T(8,128)S(1)}, u32[]{:S(2)}, u32[]{:S(2)}) collective-permute-start(f32[48,512]{1,0:T(8,128)S(1)} %bitcast.29), channel_id=1, source_target_pairs={{0,2},{1,3},{2,0},{3,1},{4,6},{5,7},{6,4},{7,5},{8,10},{9,11},{10,... | collective-permute-start | bytes 294920 | tf_op jit(solution)/shard_map/ppermute | solution.py:33
  40.4 14.9 %collective-permute-start.19 = (f32[48,512]{1,0:T(8,128)S(1)}, f32[48,512]{1,0:T(8,128)S(1)}, u32[]{:S(2)}, u32[]{:S(2)}) collective-permute-start(f32[48,512]{1,0:T(8,128)S(1)} %bitcast.30), channel_id=1, source_target_pairs={{0,4},{1,5},{2,6},{3,7},{4,0},{5,1},{6,2},{7,3},{8,12},{9,13},{10,... | collective-permute-start | bytes 294920 | tf_op jit(solution)/shard_map/ppermute | solution.py:33
  41.9 13.4 %collective-permute-start.20 = (f32[48,512]{1,0:T(8,128)S(1)}, f32[48,512]{1,0:T(8,128)S(1)}, u32[]{:S(2)}, u32[]{:S(2)}) collective-permute-start(f32[48,512]{1,0:T(8,128)S(1)} %bitcast.31), channel_id=1, source_target_pairs={{0,6},{1,7},{2,4},{3,5},{4,2},{5,3},{6,0},{7,1},{8,14},{9,15},{10,... | collective-permute-start | bytes 294920 | tf_op jit(solution)/shard_map/ppermute | solution.py:33
  45.2 10.2 %collective-permute-start.15 = (bf16[384,128]{1,0:T(8,128)(2,1)S(1)}, bf16[384,128]{1,0:T(8,128)(2,1)S(1)}, u32[]{:S(2)}, u32[]{:S(2)}) collective-permute-start(bf16[384,128]{1,0:T(8,128)(2,1)S(1)} %get-tuple-element.86.refs_4_), channel_id=1, source_target_pairs={{0,16},{8,24},{16,0},{24,8},{1,17},{9,25},{17,1},{25,9},{2,18},{10... | collective-permute-start | bytes 294920 | tf_op jit(solution)/shard_map/ppermute | solution.py:33
  47.6 7.8 %collective-permute-start.16 = (bf16[384,128]{1,0:T(8,128)(2,1)S(1)}, bf16[384,128]{1,0:T(8,128)(2,1)S(1)}, u32[]{:S(2)}, u32[]{:S(2)}) collective-permute-start(bf16[384,128]{1,0:T(8,128)(2,1)S(1)} %get-tuple-element.86.refs_4_), channel_id=1, source_target_pairs={{0,8},{8,0},{16,24},{24,16},{1,9},{9,1},{17,25},{25,17},{2,10},{10... | collective-permute-start | bytes 294920 | tf_op jit(solution)/shard_map/ppermute | solution.py:33
  49.2 6.4 %collective-permute-start.17 = (bf16[384,128]{1,0:T(8,128)(2,1)S(1)}, bf16[384,128]{1,0:T(8,128)(2,1)S(1)}, u32[]{:S(2)}, u32[]{:S(2)}) collective-permute-start(bf16[384,128]{1,0:T(8,128)(2,1)S(1)} %get-tuple-element.86.refs_4_), channel_id=1, source_target_pairs={{0,24},{8,16},{16,8},{24,0},{1,25},{9,17},{17,9},{25,1},{2,26},{10... | collective-permute-start | bytes 294920 | tf_op jit(solution)/shard_map/ppermute | solution.py:33
  59.2 5.0 %collective-permute-start.24 = (bf16[400,128]{1,0:T(8,128)(2,1)S(1)}, bf16[400,128]{1,0:T(8,128)(2,1)S(1)}, u32[]{:S(2)}, u32[]{:S(2)}) collective-permute-start(bf16[400,128]{1,0:T(8,128)(2,1)S(1)} %slice.76), channel_id=1, source_target_pairs={{0,4},{1,5},{2,6},{3,7},{4,0},{5,1},{6,2},{7,3},{8,12},{9,13},{10,... | collective-permute-start | bytes 307208 | tf_op jit(solution)/shard_map/ppermute | solution.py:33
  64.2 5.6 %collective-permute-start.25 = (bf16[400,128]{1,0:T(8,128)(2,1)S(1)}, bf16[400,128]{1,0:T(8,128)(2,1)S(1)}, u32[]{:S(2)}, u32[]{:S(2)}) collective-permute-start(bf16[400,128]{1,0:T(8,128)(2,1)S(1)} %get-tuple-element.141), channel_id=1, source_target_pairs={{0,2},{1,3},{2,0},{3,1},{4,6},{5,7},{6,4},{7,5},{8,10},{9,11},{10,... | collective-permute-start | bytes 307208 | tf_op jit(solution)/shard_map/ppermute | solution.py:33
  73.3 10.0 %collective-permute-start.27 = (bf16[400,128]{1,0:T(8,128)(2,1)S(1)}, bf16[400,128]{1,0:T(8,128)(2,1)S(1)}, u32[]{:S(2)}, u32[]{:S(2)}) collective-permute-start(bf16[400,128]{1,0:T(8,128)(2,1)S(1)} %get-tuple-element.99), channel_id=1, source_target_pairs={{0,16},{8,24},{16,0},{24,8},{1,17},{9,25},{17,1},{25,9},{2,18},{10... | collective-permute-start | bytes 307208 | tf_op jit(solution)/shard_map/ppermute | solution.py:33
  73.6 9.8 %collective-permute-start.28 = (bf16[400,128]{1,0:T(8,128)(2,1)S(1)}, bf16[400,128]{1,0:T(8,128)(2,1)S(1)}, u32[]{:S(2)}, u32[]{:S(2)}) collective-permute-start(bf16[400,128]{1,0:T(8,128)(2,1)S(1)} %get-tuple-element.100), channel_id=1, source_target_pairs={{0,8},{8,0},{16,24},{24,16},{1,9},{9,1},{17,25},{25,17},{2,10},{10... | collective-permute-start | bytes 307208 | tf_op jit(solution)/shard_map/ppermute | solution.py:33
  76.1 7.3 %collective-permute-start.29 = (bf16[400,128]{1,0:T(8,128)(2,1)S(1)}, bf16[400,128]{1,0:T(8,128)(2,1)S(1)}, u32[]{:S(2)}, u32[]{:S(2)}) collective-permute-start(bf16[400,128]{1,0:T(8,128)(2,1)S(1)} %get-tuple-element.101), channel_id=1, source_target_pairs={{0,24},{8,16},{16,8},{24,0},{1,25},{9,17},{17,9},{25,1},{2,26},{10... | collective-permute-start | bytes 307208 | tf_op jit(solution)/shard_map/ppermute | solution.py:33
  83.8 7.3 %collective-permute-start.30 = (bf16[384,128]{1,0:T(8,128)(2,1)S(1)}, bf16[384,128]{1,0:T(8,128)(2,1)S(1)}, u32[]{:S(2)}, u32[]{:S(2)}) collective-permute-start(bf16[384,128]{1,0:T(8,128)(2,1)S(1)} %get-tuple-element.108.refs_4_), channel_id=1, source_target_pairs={{0,16},{8,24},{16,0},{24,8},{1,17},{9,25},{17,1},{25,9},{2,18},{10... | collective-permute-start | bytes 294920 | tf_op jit(solution)/shard_map/ppermute | solution.py:33
  86.6 5.3 %collective-permute-start.31 = (bf16[384,128]{1,0:T(8,128)(2,1)S(1)}, bf16[384,128]{1,0:T(8,128)(2,1)S(1)}, u32[]{:S(2)}, u32[]{:S(2)}) collective-permute-start(bf16[384,128]{1,0:T(8,128)(2,1)S(1)} %get-tuple-element.108.refs_4_), channel_id=1, source_target_pairs={{0,8},{8,0},{16,24},{24,16},{1,9},{9,1},{17,25},{25,17},{2,10},{10... | collective-permute-start | bytes 294920 | tf_op jit(solution)/shard_map/ppermute | solution.py:33
  86.6 9.2 %collective-permute-start.32 = (bf16[384,128]{1,0:T(8,128)(2,1)S(1)}, bf16[384,128]{1,0:T(8,128)(2,1)S(1)}, u32[]{:S(2)}, u32[]{:S(2)}) collective-permute-start(bf16[384,128]{1,0:T(8,128)(2,1)S(1)} %get-tuple-element.108.refs_4_), channel_id=1, source_target_pairs={{0,24},{8,16},{16,8},{24,0},{1,25},{9,17},{17,9},{25,1},{2,26},{10... | collective-permute-start | bytes 294920 | tf_op jit(solution)/shard_map/ppermute | solution.py:33
  100.6 5.0 %collective-permute-start.34 = (bf16[384,128]{1,0:T(8,128)(2,1)S(1)}, bf16[384,128]{1,0:T(8,128)(2,1)S(1)}, u32[]{:S(2)}, u32[]{:S(2)}) collective-permute-start(bf16[384,128]{1,0:T(8,128)(2,1)S(1)} %slice.78), channel_id=1, source_target_pairs={{0,2},{1,3},{2,0},{3,1},{4,6},{5,7},{6,4},{7,5},{8,10},{9,11},{10,... | collective-permute-start | bytes 294920 | tf_op jit(solution)/shard_map/ppermute | solution.py:33
  104.3 6.1 %collective-permute-start.37 = (bf16[400,128]{1,0:T(8,128)(2,1)S(1)}, bf16[400,128]{1,0:T(8,128)(2,1)S(1)}, u32[]{:S(2)}, u32[]{:S(2)}) collective-permute-start(bf16[400,128]{1,0:T(8,128)(2,1)S(1)} %get-tuple-element.137), channel_id=1, source_target_pairs={{0,2},{1,3},{2,0},{3,1},{4,6},{5,7},{6,4},{7,5},{8,10},{9,11},{10,... | collective-permute-start | bytes 307208 | tf_op jit(solution)/shard_map/ppermute | solution.py:33
  113.9 9.1 %collective-permute-start.39 = (bf16[400,128]{1,0:T(8,128)(2,1)S(1)}, bf16[400,128]{1,0:T(8,128)(2,1)S(1)}, u32[]{:S(2)}, u32[]{:S(2)}) collective-permute-start(bf16[400,128]{1,0:T(8,128)(2,1)S(1)} %get-tuple-element.118), channel_id=1, source_target_pairs={{0,16},{8,24},{16,0},{24,8},{1,17},{9,25},{17,1},{25,9},{2,18},{10... | collective-permute-start | bytes 307208 | tf_op jit(solution)/shard_map/ppermute | solution.py:33
  115.3 7.7 %collective-permute-start.40 = (bf16[400,128]{1,0:T(8,128)(2,1)S(1)}, bf16[400,128]{1,0:T(8,128)(2,1)S(1)}, u32[]{:S(2)}, u32[]{:S(2)}) collective-permute-start(bf16[400,128]{1,0:T(8,128)(2,1)S(1)} %get-tuple-element.119), channel_id=1, source_target_pairs={{0,8},{8,0},{16,24},{24,16},{1,9},{9,1},{17,25},{25,17},{2,10},{10... | collective-permute-start | bytes 307208 | tf_op jit(solution)/shard_map/ppermute | solution.py:33
  116.2 8.3 %collective-permute-start.41 = (bf16[400,128]{1,0:T(8,128)(2,1)S(1)}, bf16[400,128]{1,0:T(8,128)(2,1)S(1)}, u32[]{:S(2)}, u32[]{:S(2)}) collective-permute-start(bf16[400,128]{1,0:T(8,128)(2,1)S(1)} %get-tuple-element.120), channel_id=1, source_target_pairs={{0,24},{8,16},{16,8},{24,0},{1,25},{9,17},{17,9},{25,1},{2,26},{10... | collective-permute-start | bytes 307208 | tf_op jit(solution)/shard_map/ppermute | solution.py:33
  124.8 7.1 %collective-permute-start.42 = (bf16[384,128]{1,0:T(8,128)(2,1)S(1)}, bf16[384,128]{1,0:T(8,128)(2,1)S(1)}, u32[]{:S(2)}, u32[]{:S(2)}) collective-permute-start(bf16[384,128]{1,0:T(8,128)(2,1)S(1)} %get-tuple-element.127.refs_4_), channel_id=1, source_target_pairs={{0,16},{8,24},{16,0},{24,8},{1,17},{9,25},{17,1},{25,9},{2,18},{10... | collective-permute-start | bytes 294920 | tf_op jit(solution)/shard_map/ppermute | solution.py:33
  127.6 9.0 %collective-permute-start.44 = (bf16[384,128]{1,0:T(8,128)(2,1)S(1)}, bf16[384,128]{1,0:T(8,128)(2,1)S(1)}, u32[]{:S(2)}, u32[]{:S(2)}) collective-permute-start(bf16[384,128]{1,0:T(8,128)(2,1)S(1)} %get-tuple-element.127.refs_4_), channel_id=1, source_target_pairs={{0,24},{8,16},{16,8},{24,0},{1,25},{9,17},{17,9},{25,1},{2,26},{10... | collective-permute-start | bytes 294920 | tf_op jit(solution)/shard_map/ppermute | solution.py:33
  145.2 5.5 %collective-permute-start.49 = (bf16[400,128]{1,0:T(8,128)(2,1)S(1)}, bf16[400,128]{1,0:T(8,128)(2,1)S(1)}, u32[]{:S(2)}, u32[]{:S(2)}) collective-permute-start(bf16[400,128]{1,0:T(8,128)(2,1)S(1)} %get-tuple-element.133), channel_id=1, source_target_pairs={{0,2},{1,3},{2,0},{3,1},{4,6},{5,7},{6,4},{7,5},{8,10},{9,11},{10,... | collective-permute-start | bytes 307208 | tf_op jit(solution)/shard_map/ppermute | solution.py:33
  (39 other events, 285.1 us)

commit v4 on v3

--- a/solution.py
+++ b/solution.py
@@ -212,22 +212,23 @@
     )(rows_of, cols_of, matrix, row_scale, col_scale)
 
 
-def exchange_max(row_part, col_part, last=False):
+def exchange_max(row_part, col_part):
     row_step, col_step = 1, 1
-    while row_step < lax.axis_size("cols") or col_step < lax.axis_size("rows"):
-        row_next = col_next = None
-        if row_step < lax.axis_size("cols"):
-            row_next = swap(row_part, "cols", row_step)
-        if col_step < lax.axis_size("rows"):
-            col_next = swap(col_part, "rows", col_step)
-        if row_next is not None:
-            row_part = jnp.maximum(row_part, row_next)
-        if col_next is not None:
-            col_part = jnp.maximum(col_part, col_next)
-        if last and col_step * 2 == lax.axis_size("rows"):
-            row_part, col_part = lax.optimization_barrier((row_part, col_part))
+    while col_step < lax.axis_size("rows"):
+        row_next = swap(row_part, "cols", row_step)
+        col_next = swap(col_part, "rows", col_step)
+        row_part = jnp.maximum(row_part, row_next)
+        col_part = jnp.maximum(col_part, col_next)
         row_step, col_step = 2 * row_step, 2 * col_step
-    return row_part, col_part
+
+    def rest(part):
+        step = row_step
+        while step < lax.axis_size("cols"):
+            part = jnp.maximum(part, swap(part, "cols", step))
+            step *= 2
+        return part
+
+    return row_part, col_part, rest
 
 
 def fetch_units(ref, first, count):
@@ -392,6 +393,27 @@
         jnp.where(again, mean, anchor),
         move * move,
     )
+
+
+def plan_kernel(steps, restarts, weight, out, square):
+    square[...] = jnp.zeros_like(square)
+    count, scenarios = steps.shape
+    square[:count, :scenarios] = steps[...]
+    square[count : 2 * count, :scenarios] = restarts[...].astype(F32)
+    square[2 * count : 2 * count + 1, :scenarios] = weight[...]
+    out[...] = square[...].T[:scenarios]
+
+
+def make_plan(steps, restarts, weight):
+    return pl.pallas_call(
+        plan_kernel,
+        out_shape=jax.ShapeDtypeStruct((steps.shape[1], LANES), F32),
+        in_specs=[VMEM] * 3,
+        out_specs=VMEM,
+        scratch_shapes=[pltpu.VMEM((LANES, LANES), F32)],
+        compiler_params=PARAMS,
+        name="make_plan",
+    )(steps, restarts, weight)
 
 
 def column(ref, lane):
@@ -599,20 +621,22 @@
     row_groups = lax.axis_size("rows")
     scenarios = objective.shape[1]
     obj, cap, need = objective.T, capacity.T, demand.T
-    plan = jnp.concatenate([step_size, restart.astype(F32), primal_weight[None]]).T
-    plan = jnp.pad(plan, ((0, 0), (0, LANES - plan.shape[1])))
+    plan = make_plan(step_size, restart, primal_weight[None])
 
     matrix = blocks[0, 0]
     row_top, col_top, matrix = first_max(jnp.stack([rows_of, cols_of]), matrix)
-    row_top, col_top = exchange_max(row_top, col_top)
-    row_scale = 1.0 / jnp.sqrt(row_top + epsilon)
+    row_part, col_top, rest = exchange_max(row_top, col_top)
+    row_scale = 1.0 / jnp.sqrt(rest(row_part) + epsilon)
     col_scale = 1.0 / jnp.sqrt(col_top + epsilon)
     for sweep in range(1, PASSES):
         row_top, col_top = row_col_max(rows_of, cols_of, matrix, row_scale, col_scale)
         if sweep == PASSES - 1:
             row_top, need = lax.optimization_barrier((row_top, need))
-        row_top, col_top = exchange_max(row_top, col_top, sweep == PASSES - 1)
-        row_scale = row_scale / jnp.sqrt(row_top + epsilon)
+        row_part, col_top, rest = exchange_max(row_top, col_top)
+        if sweep == PASSES - 1:
+            row_part, col_top = lax.optimization_barrier((row_part, col_top))
+        else:
+            row_scale = row_scale / jnp.sqrt(rest(row_part) + epsilon)
         col_scale = col_scale / jnp.sqrt(col_top + epsilon)
 
     primal_rest = terms = ()
@@ -621,11 +645,13 @@
         primal, ext, drift, weight, *more = primal_update(
             k, obj, cap, col_scale, plan, primal_rest, terms
         )
+        if k == 0:
+            row_scale = row_scale / jnp.sqrt(rest(row_part) + epsilon)
         pieces = [swap(ext, "rows", o) for o in offsets(row_groups)]
         if k == 0:
             matrix = scale_matrix(rows_of, cols_of, matrix, row_scale, col_scale)
             dual_rest = [need] + [swap(need, "cols", 2 * o) for o in range(1, chips)]
-            pieces, dual_rest = lax.optimization_barrier((pieces, dual_rest))
+            dual_rest, pieces = lax.optimization_barrier((dual_rest, pieces))
             dual_rest = [row_scale] + dual_rest
         keep, send = forward(rows_of, cols_of, matrix, drift, pieces)
         terms = sum_columns(keep, send)

time: 161 us -> 160 us (level)
  local copies, waits for them, and re-layouts: 4.61 us -> 2.32 us
    unnamed x21 -> x17, local copies, waits for them, and re-layouts: 4.43 us -> 2.25 us
  transfers between devices with their start and end apart: 53 -> 53, of which waited for: 35 -> 33; matrix products, arithmetic and copies ran while one was open for 0% -> 0% of each run, Pallas kernels for 2% -> 3%
where the time goes in v4:
time: 160 us
  waiting for transfers between devices  66.6 us (42%)
  starting transfers between devices  64.6 us (40%)
  Pallas kernels  24 us (15%)
  local copies, waits for them, and re-layouts  2.32 us (1%)
    ppermute x53, waiting for transfers between devices, swap(): return lax.ppermute(value, axis, [(i, i ^ offset) for i in range(count)])  66.6 us
    ppermute x53, starting transfers between devices, swap(): return lax.ppermute(value, axis, [(i, i ^ offset) for i in range(count)])  64.6 us
    pallas_call x2, Pallas kernels, row_col_max(): pl.pallas_call(max_kernel, out_shape=(jax.ShapeDtypeStruct((RB, BLK), F32...  7.04 us
    pallas_call x3, Pallas kernels, forward(): pl.pallas_call(functools.partial(forward_kernel, len(pieces)), out_shape=...  5.98 us
  transfers between devices with their start and end apart: 53, of which 33 were waited for; matrix products, arithmetic and copies ran while one was open for 0% of the time, Pallas kernels for 3%

profile of v4, /device:TPU:0, one launch (start us, length us, event | category | flops | bytes accessed | tf_op | source)
XLA Modules:
  0.0 159.6 jit_solution(10069891859857143504)
XLA Ops:
  0.7 2.2 %copy.15 = bf16[1,1,32,256,256]{4,3,2,1,0:T(8,128)(2,1)S(1)} copy(bf16[1,1,32,256,256]{4,3,2,1,0:T(8,128)(2,1)} %param.9) | data formatting | bytes 8388608
  5.2 2.6 %collective-permute-start = (f32[16,256]{1,0:T(8,128)S(1)}, f32[16,256]{1,0:T(8,128)S(1)}, u32[]{:S(2)}, u32[]{:S(2)}) collective-permute-start(f32[16,256]{1,0:T(8,128)S(1)} %get-tuple-element.68), channel_id=1, source_target_pairs={{0,8},{8,0},{16,24},{24,16},{1,9},{9,1},{17,25},{25,17},{2,10},{10... | collective-permute-start | bytes 49160 | tf_op jit(solution)/shard_map/ppermute | solution.py:33
  9.5 3.0 %collective-permute-start.1 = (f32[16,256]{1,0:T(8,128)S(1)}, f32[16,256]{1,0:T(8,128)S(1)}, u32[]{:S(2)}, u32[]{:S(2)}) collective-permute-start(f32[16,256]{1,0:T(8,128)S(1)} %max.45), channel_id=1, source_target_pairs={{0,16},{8,24},{16,0},{24,8},{1,17},{9,25},{17,1},{25,9},{2,18},{10... | collective-permute-start | bytes 49160 | tf_op jit(solution)/shard_map/ppermute | solution.py:33
  16.5 3.5 %row_col_max.2 = (f32[16,256]{1,0:T(8,128)S(1)}, f32[16,256]{1,0:T(8,128)S(1)}) custom-call(s32[32]{0:T(128)S(1)} %bitcast.42, s32[32]{0:T(128)S(1)} %bitcast.33, bf16[32,256,256]{2,1,0:T(8,128)(2,1)S(1)} %get-tuple-element.69.a, f32[16,256]{1,0:T(8,128)S(1)} %add_rsqrt_fusion.r_ref, f32[16,256]{1,0:T(8,128)S(1)} %add_rsqrt_fusion.1.c_ref), custom_call_target="tpu_custom_call" | custom-call | tf_op jit(solution)/shard_map/row_col_max/pallas_call | solution.py:197
  29.3 3.5 %row_col_max.3 = (f32[16,256]{1,0:T(8,128)S(1)}, f32[16,256]{1,0:T(8,128)S(1)}) custom-call(s32[32]{0:T(128)S(1)} %bitcast.43, s32[32]{0:T(128)S(1)} %bitcast.34, bf16[32,256,256]{2,1,0:T(8,128)(2,1)S(1)} %get-tuple-element.69.a, f32[16,256]{1,0:T(8,128)S(1)} %rsqrt_multiply_fusion.2.r_ref, f32[16,256]{1,0:T(8,128)S(1)} %rsqrt_multiply_fusion.3.c_ref), custom_call_target="tpu_custom_call" | custom-call | tf_op jit(solution)/shard_map/row_col_max/pallas_call | solution.py:197
  33.9 2.7 %collective-permute-done.12 = f32[16,256]{1,0:T(8,128)S(1)} collective-permute-done((f32[16,256]{1,0:T(8,128)S(1)}, f32[16,256]{1,0:T(8,128)S(1)}, u32[]{:S(2)}, u32[]{:S(2)}) %collective-permute-start.12) | collective-permute-done | bytes 16416 | tf_op jit(solution)/shard_map/ppermute | solution.py:33
  50.5 2.5 %scale_matrix.1.refs_2_ = bf16[32,256,256]{2,1,0:T(8,128)(2,1)S(1)} custom-call(s32[32]{0:T(128)S(1)} %bitcast.44, s32[32]{0:T(128)S(1)} %bitcast.35, bf16[32,256,256]{2,1,0:T(8,128)(2,1)S(1)} %get-tuple-element.69.a, f32[16,256]{1,0:T(8,128)S(1)} %rsqrt_multiply_fusion.r_ref.refs_2_, f32[16,256]{1,0:T(8,128)S(1)} %rsqrt_multiply_fusion.1.refs_2_.c_ref), custom_call_target="tpu_custom_call" | custom-call | tf_op jit(solution)/shard_map/scale_matrix/pallas_call | solution.py:257
  53.0 2.4 %collective-permute-done.20.refs_7_ = bf16[384,128]{1,0:T(8,128)(2,1)S(1)} collective-permute-done((bf16[384,128]{1,0:T(8,128)(2,1)S(1)}, bf16[384,128]{1,0:T(8,128)(2,1)S(1)}, u32[]{:S(2)}, u32[]{:S(2)}) %collective-permute-start.20) | collective-permute-done | bytes 98336 | tf_op jit(solution)/shard_map/ppermute | solution.py:33
  61.1 2.8 %collective-permute-done.24 = bf16[400,128]{1,0:T(8,128)(2,1)S(1)} collective-permute-done((bf16[400,128]{1,0:T(8,128)(2,1)S(1)}, bf16[400,128]{1,0:T(8,128)(2,1)S(1)}, u32[]{:S(2)}, u32[]{:S(2)}) %collective-permute-start.24) | collective-permute-done | bytes 102432 | tf_op jit(solution)/shard_map/ppermute | solution.py:33
  66.2 3.4 %collective-permute-done.23.refs_8_ = bf16[384,128]{1,0:T(8,128)(2,1)S(1)} collective-permute-done((bf16[384,128]{1,0:T(8,128)(2,1)S(1)}, bf16[384,128]{1,0:T(8,128)(2,1)S(1)}, u32[]{:S(2)}, u32[]{:S(2)}) %collective-permute-start.23) | collective-permute-done | bytes 98336 | tf_op jit(solution)/shard_map/ppermute | solution.py:33
  75.1 2.4 %collective-permute-start.29 = (bf16[400,128]{1,0:T(8,128)(2,1)S(1)}, bf16[400,128]{1,0:T(8,128)(2,1)S(1)}, u32[]{:S(2)}, u32[]{:S(2)}) collective-permute-start(bf16[400,128]{1,0:T(8,128)(2,1)S(1)} %get-tuple-element.101), channel_id=1, source_target_pairs={{0,24},{8,16},{16,8},{24,0},{1,25},{9,17},{17,9},{25,1},{2,26},{10... | collective-permute-start | bytes 307208 | tf_op jit(solution)/shard_map/ppermute | solution.py:33
  77.5 3.5 %collective-permute-done.27.refs_10_ = bf16[400,128]{1,0:T(8,128)(2,1)S(1)} collective-permute-done((bf16[400,128]{1,0:T(8,128)(2,1)S(1)}, bf16[400,128]{1,0:T(8,128)(2,1)S(1)}, u32[]{:S(2)}, u32[]{:S(2)}) %collective-permute-start.27) | collective-permute-done | bytes 102432 | tf_op jit(solution)/shard_map/ppermute | solution.py:33
  82.9 3.4 %collective-permute-start.30 = (bf16[384,128]{1,0:T(8,128)(2,1)S(1)}, bf16[384,128]{1,0:T(8,128)(2,1)S(1)}, u32[]{:S(2)}, u32[]{:S(2)}) collective-permute-start(bf16[384,128]{1,0:T(8,128)(2,1)S(1)} %get-tuple-element.108.refs_4_), channel_id=1, source_target_pairs={{0,16},{8,24},{16,0},{24,8},{1,17},{9,25},{17,1},{25,9},{2,18},{10... | collective-permute-start | bytes 294920 | tf_op jit(solution)/shard_map/ppermute | solution.py:33
  87.9 4.5 %collective-permute-done.30.refs_5_ = bf16[384,128]{1,0:T(8,128)(2,1)S(1)} collective-permute-done((bf16[384,128]{1,0:T(8,128)(2,1)S(1)}, bf16[384,128]{1,0:T(8,128)(2,1)S(1)}, u32[]{:S(2)}, u32[]{:S(2)}) %collective-permute-start.30) | collective-permute-done | bytes 98336 | tf_op jit(solution)/shard_map/ppermute | solution.py:33
  92.3 2.5 %collective-permute-done.32.refs_7_ = bf16[384,128]{1,0:T(8,128)(2,1)S(1)} collective-permute-done((bf16[384,128]{1,0:T(8,128)(2,1)S(1)}, bf16[384,128]{1,0:T(8,128)(2,1)S(1)}, u32[]{:S(2)}, u32[]{:S(2)}) %collective-permute-start.32) | collective-permute-done | bytes 98336 | tf_op jit(solution)/shard_map/ppermute | solution.py:33
  100.9 2.5 %collective-permute-done.36 = bf16[400,128]{1,0:T(8,128)(2,1)S(1)} collective-permute-done((bf16[400,128]{1,0:T(8,128)(2,1)S(1)}, bf16[400,128]{1,0:T(8,128)(2,1)S(1)}, u32[]{:S(2)}, u32[]{:S(2)}) %collective-permute-start.36) | collective-permute-done | bytes 102432 | tf_op jit(solution)/shard_map/ppermute | solution.py:33
  106.0 3.5 %collective-permute-done.35.refs_8_ = bf16[384,128]{1,0:T(8,128)(2,1)S(1)} collective-permute-done((bf16[384,128]{1,0:T(8,128)(2,1)S(1)}, bf16[384,128]{1,0:T(8,128)(2,1)S(1)}, u32[]{:S(2)}, u32[]{:S(2)}) %collective-permute-start.35) | collective-permute-done | bytes 98336 | tf_op jit(solution)/shard_map/ppermute | solution.py:33
  113.6 2.3 %collective-permute-start.40 = (bf16[400,128]{1,0:T(8,128)(2,1)S(1)}, bf16[400,128]{1,0:T(8,128)(2,1)S(1)}, u32[]{:S(2)}, u32[]{:S(2)}) collective-permute-start(bf16[400,128]{1,0:T(8,128)(2,1)S(1)} %get-tuple-element.119), channel_id=1, source_target_pairs={{0,8},{8,0},{16,24},{24,16},{1,9},{9,1},{17,25},{25,17},{2,10},{10... | collective-permute-start | bytes 307208 | tf_op jit(solution)/shard_map/ppermute | solution.py:33
  117.4 5.2 %collective-permute-done.39.refs_10_ = bf16[400,128]{1,0:T(8,128)(2,1)S(1)} collective-permute-done((bf16[400,128]{1,0:T(8,128)(2,1)S(1)}, bf16[400,128]{1,0:T(8,128)(2,1)S(1)}, u32[]{:S(2)}, u32[]{:S(2)}) %collective-permute-start.39) | collective-permute-done | bytes 102432 | tf_op jit(solution)/shard_map/ppermute | solution.py:33
  126.8 2.2 %collective-permute-start.44 = (bf16[384,128]{1,0:T(8,128)(2,1)S(1)}, bf16[384,128]{1,0:T(8,128)(2,1)S(1)}, u32[]{:S(2)}, u32[]{:S(2)}) collective-permute-start(bf16[384,128]{1,0:T(8,128)(2,1)S(1)} %get-tuple-element.127.refs_4_), channel_id=1, source_target_pairs={{0,24},{8,16},{16,8},{24,0},{1,25},{9,17},{17,9},{25,1},{2,26},{10... | collective-permute-start | bytes 294920 | tf_op jit(solution)/shard_map/ppermute | solution.py:33
  129.0 4.6 %collective-permute-done.42.refs_5_ = bf16[384,128]{1,0:T(8,128)(2,1)S(1)} collective-permute-done((bf16[384,128]{1,0:T(8,128)(2,1)S(1)}, bf16[384,128]{1,0:T(8,128)(2,1)S(1)}, u32[]{:S(2)}, u32[]{:S(2)}) %collective-permute-start.42) | collective-permute-done | bytes 98336 | tf_op jit(solution)/shard_map/ppermute | solution.py:33
  140.8 2.9 %collective-permute-done.48 = bf16[400,128]{1,0:T(8,128)(2,1)S(1)} collective-permute-done((bf16[400,128]{1,0:T(8,128)(2,1)S(1)}, bf16[400,128]{1,0:T(8,128)(2,1)S(1)}, u32[]{:S(2)}, u32[]{:S(2)}) %collective-permute-start.48) | collective-permute-done | bytes 102432 | tf_op jit(solution)/shard_map/ppermute | solution.py:33
  145.9 3.4 %collective-permute-done.47.refs_8_ = bf16[384,128]{1,0:T(8,128)(2,1)S(1)} collective-permute-done((bf16[384,128]{1,0:T(8,128)(2,1)S(1)}, bf16[384,128]{1,0:T(8,128)(2,1)S(1)}, u32[]{:S(2)}, u32[]{:S(2)}) %collective-permute-start.47) | collective-permute-done | bytes 98336 | tf_op jit(solution)/shard_map/ppermute | solution.py:33
  152.4 2.1 %collective-permute-done.51 = f32[8,128]{1,0:T(8,128)S(1)} collective-permute-done((f32[8,128]{1,0:T(8,128)S(1)}, f32[8,128]{1,0:T(8,128)S(1)}, u32[]{:S(2)}, u32[]{:S(2)}) %collective-permute-start.51) | collective-permute-done | bytes 4128 | tf_op jit(solution)/shard_map/ppermute | solution.py:33
  (154 shorter events, 84.9 us)
Async XLA Ops:
  36.6 6.5 %collective-permute-start.13 = (f32[16,256]{1,0:T(8,128)S(1)}, f32[16,256]{1,0:T(8,128)S(1)}, u32[]{:S(2)}, u32[]{:S(2)}) collective-permute-start(f32[16,256]{1,0:T(8,128)S(1)} %max.57), channel_id=1, source_target_pairs={{0,16},{8,24},{16,0},{24,8},{1,17},{9,25},{17,1},{25,9},{2,18},{10... | collective-permute-start | bytes 49160 | tf_op jit(solution)/shard_map/ppermute | solution.py:33
  38.0 5.2 %collective-permute-start.11 = (f32[16,256]{1,0:T(8,128)S(1)}, f32[16,256]{1,0:T(8,128)S(1)}, u32[]{:S(2)}, u32[]{:S(2)}) collective-permute-start(f32[16,256]{1,0:T(8,128)S(1)} %max.55), channel_id=1, source_target_pairs={{0,2},{1,3},{2,0},{3,1},{4,6},{5,7},{6,4},{7,5},{8,10},{9,11},{10,... | collective-permute-start | bytes 49160 | tf_op jit(solution)/shard_map/ppermute | solution.py:33
  39.6 9.4 %collective-permute-start.15 = (f32[48,512]{1,0:T(8,128)S(1)}, f32[48,512]{1,0:T(8,128)S(1)}, u32[]{:S(2)}, u32[]{:S(2)}) collective-permute-start(f32[48,512]{1,0:T(8,128)S(1)} %bitcast.28), channel_id=1, source_target_pairs={{0,2},{1,3},{2,0},{3,1},{4,6},{5,7},{6,4},{7,5},{8,10},{9,11},{10,... | collective-permute-start | bytes 294920 | tf_op jit(solution)/shard_map/ppermute | solution.py:33
  40.2 12.8 %collective-permute-start.16 = (f32[48,512]{1,0:T(8,128)S(1)}, f32[48,512]{1,0:T(8,128)S(1)}, u32[]{:S(2)}, u32[]{:S(2)}) collective-permute-start(f32[48,512]{1,0:T(8,128)S(1)} %bitcast.29), channel_id=1, source_target_pairs={{0,4},{1,5},{2,6},{3,7},{4,0},{5,1},{6,2},{7,3},{8,12},{9,13},{10,... | collective-permute-start | bytes 294920 | tf_op jit(solution)/shard_map/ppermute | solution.py:33
  41.7 11.2 %collective-permute-start.17 = (f32[48,512]{1,0:T(8,128)S(1)}, f32[48,512]{1,0:T(8,128)S(1)}, u32[]{:S(2)}, u32[]{:S(2)}) collective-permute-start(f32[48,512]{1,0:T(8,128)S(1)} %bitcast.30), channel_id=1, source_target_pairs={{0,6},{1,7},{2,4},{3,5},{4,2},{5,3},{6,0},{7,1},{8,14},{9,15},{10,... | collective-permute-start | bytes 294920 | tf_op jit(solution)/shard_map/ppermute | solution.py:33
  45.0 8.0 %collective-permute-start.18 = (bf16[384,128]{1,0:T(8,128)(2,1)S(1)}, bf16[384,128]{1,0:T(8,128)(2,1)S(1)}, u32[]{:S(2)}, u32[]{:S(2)}) collective-permute-start(bf16[384,128]{1,0:T(8,128)(2,1)S(1)} %get-tuple-element.86.refs_4_), channel_id=1, source_target_pairs={{0,16},{8,24},{16,0},{24,8},{1,17},{9,25},{17,1},{25,9},{2,18},{10... | collective-permute-start | bytes 294920 | tf_op jit(solution)/shard_map/ppermute | solution.py:33
  47.4 5.6 %collective-permute-start.19 = (bf16[384,128]{1,0:T(8,128)(2,1)S(1)}, bf16[384,128]{1,0:T(8,128)(2,1)S(1)}, u32[]{:S(2)}, u32[]{:S(2)}) collective-permute-start(bf16[384,128]{1,0:T(8,128)(2,1)S(1)} %get-tuple-element.86.refs_4_), channel_id=1, source_target_pairs={{0,8},{8,0},{16,24},{24,16},{1,9},{9,1},{17,25},{25,17},{2,10},{10... | collective-permute-start | bytes 294920 | tf_op jit(solution)/shard_map/ppermute | solution.py:33
  49.0 6.4 %collective-permute-start.20 = (bf16[384,128]{1,0:T(8,128)(2,1)S(1)}, bf16[384,128]{1,0:T(8,128)(2,1)S(1)}, u32[]{:S(2)}, u32[]{:S(2)}) collective-permute-start(bf16[384,128]{1,0:T(8,128)(2,1)S(1)} %get-tuple-element.86.refs_4_), channel_id=1, source_target_pairs={{0,24},{8,16},{16,8},{24,0},{1,25},{9,17},{17,9},{25,1},{2,26},{10... | collective-permute-start | bytes 294920 | tf_op jit(solution)/shard_map/ppermute | solution.py:33
  64.0 5.5 %collective-permute-start.25 = (bf16[400,128]{1,0:T(8,128)(2,1)S(1)}, bf16[400,128]{1,0:T(8,128)(2,1)S(1)}, u32[]{:S(2)}, u32[]{:S(2)}) collective-permute-start(bf16[400,128]{1,0:T(8,128)(2,1)S(1)} %get-tuple-element.141), channel_id=1, source_target_pairs={{0,2},{1,3},{2,0},{3,1},{4,6},{5,7},{6,4},{7,5},{8,10},{9,11},{10,... | collective-permute-start | bytes 307208 | tf_op jit(solution)/shard_map/ppermute | solution.py:33
  73.0 8.0 %collective-permute-start.27 = (bf16[400,128]{1,0:T(8,128)(2,1)S(1)}, bf16[400,128]{1,0:T(8,128)(2,1)S(1)}, u32[]{:S(2)}, u32[]{:S(2)}) collective-permute-start(bf16[400,128]{1,0:T(8,128)(2,1)S(1)} %get-tuple-element.99), channel_id=1, source_target_pairs={{0,16},{8,24},{16,0},{24,8},{1,17},{9,25},{17,1},{25,9},{2,18},{10... | collective-permute-start | bytes 307208 | tf_op jit(solution)/shard_map/ppermute | solution.py:33
  73.1 9.4 %collective-permute-start.28 = (bf16[400,128]{1,0:T(8,128)(2,1)S(1)}, bf16[400,128]{1,0:T(8,128)(2,1)S(1)}, u32[]{:S(2)}, u32[]{:S(2)}) collective-permute-start(bf16[400,128]{1,0:T(8,128)(2,1)S(1)} %get-tuple-element.100), channel_id=1, source_target_pairs={{0,8},{8,0},{16,24},{24,16},{1,9},{9,1},{17,25},{25,17},{2,10},{10... | collective-permute-start | bytes 307208 | tf_op jit(solution)/shard_map/ppermute | solution.py:33
  75.1 7.4 %collective-permute-start.29 = (bf16[400,128]{1,0:T(8,128)(2,1)S(1)}, bf16[400,128]{1,0:T(8,128)(2,1)S(1)}, u32[]{:S(2)}, u32[]{:S(2)}) collective-permute-start(bf16[400,128]{1,0:T(8,128)(2,1)S(1)} %get-tuple-element.101), channel_id=1, source_target_pairs={{0,24},{8,16},{16,8},{24,0},{1,25},{9,17},{17,9},{25,1},{2,26},{10... | collective-permute-start | bytes 307208 | tf_op jit(solution)/shard_map/ppermute | solution.py:33
  82.9 9.4 %collective-permute-start.30 = (bf16[384,128]{1,0:T(8,128)(2,1)S(1)}, bf16[384,128]{1,0:T(8,128)(2,1)S(1)}, u32[]{:S(2)}, u32[]{:S(2)}) collective-permute-start(bf16[384,128]{1,0:T(8,128)(2,1)S(1)} %get-tuple-element.108.refs_4_), channel_id=1, source_target_pairs={{0,16},{8,24},{16,0},{24,8},{1,17},{9,25},{17,1},{25,9},{2,18},{10... | collective-permute-start | bytes 294920 | tf_op jit(solution)/shard_map/ppermute | solution.py:33
  86.3 6.0 %collective-permute-start.31 = (bf16[384,128]{1,0:T(8,128)(2,1)S(1)}, bf16[384,128]{1,0:T(8,128)(2,1)S(1)}, u32[]{:S(2)}, u32[]{:S(2)}) collective-permute-start(bf16[384,128]{1,0:T(8,128)(2,1)S(1)} %get-tuple-element.108.refs_4_), channel_id=1, source_target_pairs={{0,8},{8,0},{16,24},{24,16},{1,9},{9,1},{17,25},{25,17},{2,10},{10... | collective-permute-start | bytes 294920 | tf_op jit(solution)/shard_map/ppermute | solution.py:33
  86.3 8.5 %collective-permute-start.32 = (bf16[384,128]{1,0:T(8,128)(2,1)S(1)}, bf16[384,128]{1,0:T(8,128)(2,1)S(1)}, u32[]{:S(2)}, u32[]{:S(2)}) collective-permute-start(bf16[384,128]{1,0:T(8,128)(2,1)S(1)} %get-tuple-element.108.refs_4_), channel_id=1, source_target_pairs={{0,24},{8,16},{16,8},{24,0},{1,25},{9,17},{17,9},{25,1},{2,26},{10... | collective-permute-start | bytes 294920 | tf_op jit(solution)/shard_map/ppermute | solution.py:33
  99.7 5.0 %collective-permute-start.34 = (bf16[384,128]{1,0:T(8,128)(2,1)S(1)}, bf16[384,128]{1,0:T(8,128)(2,1)S(1)}, u32[]{:S(2)}, u32[]{:S(2)}) collective-permute-start(bf16[384,128]{1,0:T(8,128)(2,1)S(1)} %slice.78), channel_id=1, source_target_pairs={{0,2},{1,3},{2,0},{3,1},{4,6},{5,7},{6,4},{7,5},{8,10},{9,11},{10,... | collective-permute-start | bytes 294920 | tf_op jit(solution)/shard_map/ppermute | solution.py:33
  103.4 6.1 %collective-permute-start.37 = (bf16[400,128]{1,0:T(8,128)(2,1)S(1)}, bf16[400,128]{1,0:T(8,128)(2,1)S(1)}, u32[]{:S(2)}, u32[]{:S(2)}) collective-permute-start(bf16[400,128]{1,0:T(8,128)(2,1)S(1)} %get-tuple-element.137), channel_id=1, source_target_pairs={{0,2},{1,3},{2,0},{3,1},{4,6},{5,7},{6,4},{7,5},{8,10},{9,11},{10,... | collective-permute-start | bytes 307208 | tf_op jit(solution)/shard_map/ppermute | solution.py:33
  112.9 9.6 %collective-permute-start.39 = (bf16[400,128]{1,0:T(8,128)(2,1)S(1)}, bf16[400,128]{1,0:T(8,128)(2,1)S(1)}, u32[]{:S(2)}, u32[]{:S(2)}) collective-permute-start(bf16[400,128]{1,0:T(8,128)(2,1)S(1)} %get-tuple-element.118), channel_id=1, source_target_pairs={{0,16},{8,24},{16,0},{24,8},{1,17},{9,25},{17,1},{25,9},{2,18},{10... | collective-permute-start | bytes 307208 | tf_op jit(solution)/shard_map/ppermute | solution.py:33
  113.6 9.0 %collective-permute-start.40 = (bf16[400,128]{1,0:T(8,128)(2,1)S(1)}, bf16[400,128]{1,0:T(8,128)(2,1)S(1)}, u32[]{:S(2)}, u32[]{:S(2)}) collective-permute-start(bf16[400,128]{1,0:T(8,128)(2,1)S(1)} %get-tuple-element.119), channel_id=1, source_target_pairs={{0,8},{8,0},{16,24},{24,16},{1,9},{9,1},{17,25},{25,17},{2,10},{10... | collective-permute-start | bytes 307208 | tf_op jit(solution)/shard_map/ppermute | solution.py:33
  115.9 8.3 %collective-permute-start.41 = (bf16[400,128]{1,0:T(8,128)(2,1)S(1)}, bf16[400,128]{1,0:T(8,128)(2,1)S(1)}, u32[]{:S(2)}, u32[]{:S(2)}) collective-permute-start(bf16[400,128]{1,0:T(8,128)(2,1)S(1)} %get-tuple-element.120), channel_id=1, source_target_pairs={{0,24},{8,16},{16,8},{24,0},{1,25},{9,17},{17,9},{25,1},{2,26},{10... | collective-permute-start | bytes 307208 | tf_op jit(solution)/shard_map/ppermute | solution.py:33
  124.6 9.1 %collective-permute-start.42 = (bf16[384,128]{1,0:T(8,128)(2,1)S(1)}, bf16[384,128]{1,0:T(8,128)(2,1)S(1)}, u32[]{:S(2)}, u32[]{:S(2)}) collective-permute-start(bf16[384,128]{1,0:T(8,128)(2,1)S(1)} %get-tuple-element.127.refs_4_), channel_id=1, source_target_pairs={{0,16},{8,24},{16,0},{24,8},{1,17},{9,25},{17,1},{25,9},{2,18},{10... | collective-permute-start | bytes 294920 | tf_op jit(solution)/shard_map/ppermute | solution.py:33
  126.5 7.2 %collective-permute-start.43 = (bf16[384,128]{1,0:T(8,128)(2,1)S(1)}, bf16[384,128]{1,0:T(8,128)(2,1)S(1)}, u32[]{:S(2)}, u32[]{:S(2)}) collective-permute-start(bf16[384,128]{1,0:T(8,128)(2,1)S(1)} %get-tuple-element.127.refs_4_), channel_id=1, source_target_pairs={{0,8},{8,0},{16,24},{24,16},{1,9},{9,1},{17,25},{25,17},{2,10},{10... | collective-permute-start | bytes 294920 | tf_op jit(solution)/shard_map/ppermute | solution.py:33
  126.8 8.4 %collective-permute-start.44 = (bf16[384,128]{1,0:T(8,128)(2,1)S(1)}, bf16[384,128]{1,0:T(8,128)(2,1)S(1)}, u32[]{:S(2)}, u32[]{:S(2)}) collective-permute-start(bf16[384,128]{1,0:T(8,128)(2,1)S(1)} %get-tuple-element.127.refs_4_), channel_id=1, source_target_pairs={{0,24},{8,16},{16,8},{24,0},{1,25},{9,17},{17,9},{25,1},{2,26},{10... | collective-permute-start | bytes 294920 | tf_op jit(solution)/shard_map/ppermute | solution.py:33
  143.7 5.6 %collective-permute-start.49 = (bf16[400,128]{1,0:T(8,128)(2,1)S(1)}, bf16[400,128]{1,0:T(8,128)(2,1)S(1)}, u32[]{:S(2)}, u32[]{:S(2)}) collective-permute-start(bf16[400,128]{1,0:T(8,128)(2,1)S(1)} %get-tuple-element.133), channel_id=1, source_target_pairs={{0,2},{1,3},{2,0},{3,1},{4,6},{5,7},{6,4},{7,5},{8,10},{9,11},{10,... | collective-permute-start | bytes 307208 | tf_op jit(solution)/shard_map/ppermute | solution.py:33
  (37 other events, 259.4 us)

commit v5 on v4

--- a/solution.py
+++ b/solution.py
@@ -212,10 +212,14 @@
     )(rows_of, cols_of, matrix, row_scale, col_scale)
 
 
-def exchange_max(row_part, col_part):
+def unlike(step, last=False):
+    return step if step == 1 or last else step + 1
+
+
+def exchange_max(row_part, col_part, last=False):
     row_step, col_step = 1, 1
     while col_step < lax.axis_size("rows"):
-        row_next = swap(row_part, "cols", row_step)
+        row_next = swap(row_part, "cols", unlike(row_step, last))
         col_next = swap(col_part, "rows", col_step)
         row_part = jnp.maximum(row_part, row_next)
         col_part = jnp.maximum(col_part, col_next)
@@ -224,7 +228,7 @@
     def rest(part):
         step = row_step
         while step < lax.axis_size("cols"):
-            part = jnp.maximum(part, swap(part, "cols", step))
+            part = jnp.maximum(part, swap(part, "cols", unlike(step, last)))
             step *= 2
         return part
 
@@ -235,7 +239,7 @@
     return jnp.concatenate([ref[first + k] for k in range(count)], axis=1)
 
 
-def scale_kernel(rows_ref, cols_ref, a, r_ref, c_ref, m, rb):
+def scale_kernel(rows_ref, cols_ref, a, r_ref, c_ref, m, flipped, rb):
     spread_rows(r_ref, rb)
 
     def block(n):
@@ -249,6 +253,7 @@
                 lanes = slice(half * LANES, (half + 1) * LANES)
                 scaled = raw[:, lanes] * tall * factor[:, lanes]
                 m[n, part, pl.ds(half * LANES, LANES)] = scaled.astype(BF16)
+        flipped[n] = m[n].T
 
     for_each_block(m.shape[0], 2, lambda ns: [block(n) for n in ns])
 
@@ -256,9 +261,9 @@
 def scale_matrix(rows_of, cols_of, matrix, row_scale, col_scale):
     return pl.pallas_call(
         scale_kernel,
-        out_shape=jax.ShapeDtypeStruct(matrix.shape, BF16),
+        out_shape=[jax.ShapeDtypeStruct(matrix.shape, BF16)] * 2,
         in_specs=[SMEM, SMEM, VMEM, VMEM, VMEM],
-        out_specs=VMEM,
+        out_specs=[VMEM] * 2,
         scratch_shapes=[pltpu.VMEM((RB, BLK, LANES), F32)],
         compiler_params=PARAMS,
         name="scale_matrix",
@@ -297,7 +302,7 @@
             x[(me ^ o) * units + k] = piece[k * scenarios : (k + 1) * scenarios, :]
     acc[...] = jnp.zeros_like(acc)
     count = m.shape[0]
-    dims = (((1,), (1,)), ((), ()))
+    dims = (((1,), (0,)), ((), ()))
     for_each_block(
         count, count, lambda ns: block_products(ns, cols_ref, rows_ref, x, m, acc, dims)
     )
@@ -632,7 +637,7 @@
         row_top, col_top = row_col_max(rows_of, cols_of, matrix, row_scale, col_scale)
         if sweep == PASSES - 1:
             row_top, need = lax.optimization_barrier((row_top, need))
-        row_part, col_top, rest = exchange_max(row_top, col_top)
+        row_part, col_top, rest = exchange_max(row_top, col_top, sweep == PASSES - 1)
         if sweep == PASSES - 1:
             row_part, col_top = lax.optimization_barrier((row_part, col_top))
         else:
@@ -649,11 +654,11 @@
             row_scale = row_scale / jnp.sqrt(rest(row_part) + epsilon)
         pieces = [swap(ext, "rows", o) for o in offsets(row_groups)]
         if k == 0:
-            matrix = scale_matrix(rows_of, cols_of, matrix, row_scale, col_scale)
+            matrix, flipped = scale_matrix(rows_of, cols_of, matrix, row_scale, col_scale)
             dual_rest = [need] + [swap(need, "cols", 2 * o) for o in range(1, chips)]
             dual_rest, pieces = lax.optimization_barrier((dual_rest, pieces))
             dual_rest = [row_scale] + dual_rest
-        keep, send = forward(rows_of, cols_of, matrix, drift, pieces)
+        keep, send = forward(rows_of, cols_of, flipped, drift, pieces)
         terms = sum_columns(keep, send)
         outs = dual_update(k, plan, weight, dual_rest, terms, need.shape[1])
         if last:

time: 160 us -> 158 us (0.988)
  transfers between devices with their start and end apart: 53 -> 53, of which waited for: 33 -> 32; matrix products, arithmetic and copies ran while one was open for 0% -> 0% of each run, Pallas kernels for 3% -> 3%
where the time goes in v5:
time: 158 us; the launch traced here: 157 us
  waiting for transfers between devices  65.5 us (41%)
  starting transfers between devices  63.5 us (40%)
  Pallas kernels  24 us (15%)
  local copies, waits for them, and re-layouts  2.32 us (1%)
    ppermute x53, waiting for transfers between devices, swap(): return lax.ppermute(value, axis, [(i, i ^ offset) for i in range(count)])  65.5 us
    ppermute x53, starting transfers between devices, swap(): return lax.ppermute(value, axis, [(i, i ^ offset) for i in range(count)])  63.5 us
    pallas_call x2, Pallas kernels, row_col_max(): pl.pallas_call(max_kernel, out_shape=(jax.ShapeDtypeStruct((RB, BLK), F32...  7.15 us
    pallas_call x3, Pallas kernels, forward(): pl.pallas_call(functools.partial(forward_kernel, len(pieces)), out_shape=...  4.47 us
    pallas_call x1, Pallas kernels, scale_matrix(): pl.pallas_call(scale_kernel, out_shape=[jax.ShapeDtypeStruct(matrix.shape...  3.9 us
  transfers between devices with their start and end apart: 53, of which 32 were waited for; matrix products, arithmetic and copies ran while one was open for 0% of the time, Pallas kernels for 3%

profile of v5, /device:TPU:0, one launch (start us, length us, event | category | flops | bytes accessed | tf_op | source)
XLA Modules:
  0.0 157.4 jit_solution(6519282693847456208)
XLA Ops:
  0.7 2.2 %copy.15 = bf16[1,1,32,256,256]{4,3,2,1,0:T(8,128)(2,1)S(1)} copy(bf16[1,1,32,256,256]{4,3,2,1,0:T(8,128)(2,1)} %param.9) | data formatting | bytes 8388608
  5.2 2.7 %collective-permute-start = (f32[16,256]{1,0:T(8,128)S(1)}, f32[16,256]{1,0:T(8,128)S(1)}, u32[]{:S(2)}, u32[]{:S(2)}) collective-permute-start(f32[16,256]{1,0:T(8,128)S(1)} %get-tuple-element.70), channel_id=1, source_target_pairs={{0,8},{8,0},{16,24},{24,16},{1,9},{9,1},{17,25},{25,17},{2,10},{10... | collective-permute-start | bytes 49160 | tf_op jit(solution)/shard_map/ppermute | solution.py:33
  9.6 3.0 %collective-permute-start.1 = (f32[16,256]{1,0:T(8,128)S(1)}, f32[16,256]{1,0:T(8,128)S(1)}, u32[]{:S(2)}, u32[]{:S(2)}) collective-permute-start(f32[16,256]{1,0:T(8,128)S(1)} %max.45), channel_id=1, source_target_pairs={{0,16},{8,24},{16,0},{24,8},{1,17},{9,25},{17,1},{25,9},{2,18},{10... | collective-permute-start | bytes 49160 | tf_op jit(solution)/shard_map/ppermute | solution.py:33
  16.0 3.6 %row_col_max.2 = (f32[16,256]{1,0:T(8,128)S(1)}, f32[16,256]{1,0:T(8,128)S(1)}) custom-call(s32[32]{0:T(128)S(1)} %bitcast.42, s32[32]{0:T(128)S(1)} %bitcast.33, bf16[32,256,256]{2,1,0:T(8,128)(2,1)S(1)} %get-tuple-element.71.a, f32[16,256]{1,0:T(8,128)S(1)} %add_rsqrt_fusion.r_ref, f32[16,256]{1,0:T(8,128)S(1)} %add_rsqrt_fusion.1.c_ref), custom_call_target="tpu_custom_call" | custom-call | tf_op jit(solution)/shard_map/row_col_max/pallas_call | solution.py:197
  25.7 2.4 %collective-permute-done.6 = f32[16,256]{1,0:T(8,128)S(1)} collective-permute-done((f32[16,256]{1,0:T(8,128)S(1)}, f32[16,256]{1,0:T(8,128)S(1)}, u32[]{:S(2)}, u32[]{:S(2)}) %collective-permute-start.6) | collective-permute-done | bytes 16416 | tf_op jit(solution)/shard_map/ppermute | solution.py:33
  28.2 3.6 %row_col_max.3 = (f32[16,256]{1,0:T(8,128)S(1)}, f32[16,256]{1,0:T(8,128)S(1)}) custom-call(s32[32]{0:T(128)S(1)} %bitcast.43, s32[32]{0:T(128)S(1)} %bitcast.34, bf16[32,256,256]{2,1,0:T(8,128)(2,1)S(1)} %get-tuple-element.71.a, f32[16,256]{1,0:T(8,128)S(1)} %rsqrt_multiply_fusion.2.r_ref, f32[16,256]{1,0:T(8,128)S(1)} %rsqrt_multiply_fusion.3.c_ref), custom_call_target="tpu_custom_call" | custom-call | tf_op jit(solution)/shard_map/row_col_max/pallas_call | solution.py:197
  33.4 2.2 %collective-permute-done.12 = f32[16,256]{1,0:T(8,128)S(1)} collective-permute-done((f32[16,256]{1,0:T(8,128)S(1)}, f32[16,256]{1,0:T(8,128)S(1)}, u32[]{:S(2)}, u32[]{:S(2)}) %collective-permute-start.12) | collective-permute-done | bytes 16416 | tf_op jit(solution)/shard_map/ppermute | solution.py:33
  49.4 3.9 %scale_matrix.1 = (bf16[32,256,256]{2,1,0:T(8,128)(2,1)S(1)}, bf16[32,256,256]{2,1,0:T(8,128)(2,1)S(1)}) custom-call(s32[32]{0:T(128)S(1)} %bitcast.44, s32[32]{0:T(128)S(1)} %bitcast.35, bf16[32,256,256]{2,1,0:T(8,128)(2,1)S(1)} %get-tuple-element.71.a, f32[16,256]{1,0:T(8,128)S(1)} %rsqrt_multiply_fusion.r_ref.refs_2_, ...), custom_call_target="tpu_custom_call" | custom-call | tf_op jit(solution)/shard_map/scale_matrix/pallas_call | solution.py:262
  59.9 2.6 %collective-permute-done.24 = bf16[400,128]{1,0:T(8,128)(2,1)S(1)} collective-permute-done((bf16[400,128]{1,0:T(8,128)(2,1)S(1)}, bf16[400,128]{1,0:T(8,128)(2,1)S(1)}, u32[]{:S(2)}, u32[]{:S(2)}) %collective-permute-start.24) | collective-permute-done | bytes 102432 | tf_op jit(solution)/shard_map/ppermute | solution.py:33
  64.9 3.1 %collective-permute-done.23.refs_8_ = bf16[384,128]{1,0:T(8,128)(2,1)S(1)} collective-permute-done((bf16[384,128]{1,0:T(8,128)(2,1)S(1)}, bf16[384,128]{1,0:T(8,128)(2,1)S(1)}, u32[]{:S(2)}, u32[]{:S(2)}) %collective-permute-start.23) | collective-permute-done | bytes 98336 | tf_op jit(solution)/shard_map/ppermute | solution.py:33
  73.7 2.3 %collective-permute-start.29 = (bf16[400,128]{1,0:T(8,128)(2,1)S(1)}, bf16[400,128]{1,0:T(8,128)(2,1)S(1)}, u32[]{:S(2)}, u32[]{:S(2)}) collective-permute-start(bf16[400,128]{1,0:T(8,128)(2,1)S(1)} %get-tuple-element.105), channel_id=1, source_target_pairs={{0,24},{8,16},{16,8},{24,0},{1,25},{9,17},{17,9},{25,1},{2,26},{10... | collective-permute-start | bytes 307208 | tf_op jit(solution)/shard_map/ppermute | solution.py:33
  76.0 5.0 %collective-permute-done.27.refs_10_ = bf16[400,128]{1,0:T(8,128)(2,1)S(1)} collective-permute-done((bf16[400,128]{1,0:T(8,128)(2,1)S(1)}, bf16[400,128]{1,0:T(8,128)(2,1)S(1)}, u32[]{:S(2)}, u32[]{:S(2)}) %collective-permute-start.27) | collective-permute-done | bytes 102432 | tf_op jit(solution)/shard_map/ppermute | solution.py:33
  81.8 3.3 %collective-permute-start.30 = (bf16[384,128]{1,0:T(8,128)(2,1)S(1)}, bf16[384,128]{1,0:T(8,128)(2,1)S(1)}, u32[]{:S(2)}, u32[]{:S(2)}) collective-permute-start(bf16[384,128]{1,0:T(8,128)(2,1)S(1)} %get-tuple-element.112.refs_4_), channel_id=1, source_target_pairs={{0,16},{8,24},{16,0},{24,8},{1,17},{9,25},{17,1},{25,9},{2,18},{10... | collective-permute-start | bytes 294920 | tf_op jit(solution)/shard_map/ppermute | solution.py:33
  86.6 4.5 %collective-permute-done.30.refs_5_ = bf16[384,128]{1,0:T(8,128)(2,1)S(1)} collective-permute-done((bf16[384,128]{1,0:T(8,128)(2,1)S(1)}, bf16[384,128]{1,0:T(8,128)(2,1)S(1)}, u32[]{:S(2)}, u32[]{:S(2)}) %collective-permute-start.30) | collective-permute-done | bytes 98336 | tf_op jit(solution)/shard_map/ppermute | solution.py:33
  91.1 2.4 %collective-permute-done.32.refs_7_ = bf16[384,128]{1,0:T(8,128)(2,1)S(1)} collective-permute-done((bf16[384,128]{1,0:T(8,128)(2,1)S(1)}, bf16[384,128]{1,0:T(8,128)(2,1)S(1)}, u32[]{:S(2)}, u32[]{:S(2)}) %collective-permute-start.32) | collective-permute-done | bytes 98336 | tf_op jit(solution)/shard_map/ppermute | solution.py:33
  99.1 2.5 %collective-permute-done.36 = bf16[400,128]{1,0:T(8,128)(2,1)S(1)} collective-permute-done((bf16[400,128]{1,0:T(8,128)(2,1)S(1)}, bf16[400,128]{1,0:T(8,128)(2,1)S(1)}, u32[]{:S(2)}, u32[]{:S(2)}) %collective-permute-start.36) | collective-permute-done | bytes 102432 | tf_op jit(solution)/shard_map/ppermute | solution.py:33
  104.2 3.5 %collective-permute-done.35.refs_8_ = bf16[384,128]{1,0:T(8,128)(2,1)S(1)} collective-permute-done((bf16[384,128]{1,0:T(8,128)(2,1)S(1)}, bf16[384,128]{1,0:T(8,128)(2,1)S(1)}, u32[]{:S(2)}, u32[]{:S(2)}) %collective-permute-start.35) | collective-permute-done | bytes 98336 | tf_op jit(solution)/shard_map/ppermute | solution.py:33
  115.6 5.2 %collective-permute-done.39.refs_10_ = bf16[400,128]{1,0:T(8,128)(2,1)S(1)} collective-permute-done((bf16[400,128]{1,0:T(8,128)(2,1)S(1)}, bf16[400,128]{1,0:T(8,128)(2,1)S(1)}, u32[]{:S(2)}, u32[]{:S(2)}) %collective-permute-start.39) | collective-permute-done | bytes 102432 | tf_op jit(solution)/shard_map/ppermute | solution.py:33
  122.7 2.7 %collective-permute-start.42 = (bf16[384,128]{1,0:T(8,128)(2,1)S(1)}, bf16[384,128]{1,0:T(8,128)(2,1)S(1)}, u32[]{:S(2)}, u32[]{:S(2)}) collective-permute-start(bf16[384,128]{1,0:T(8,128)(2,1)S(1)} %get-tuple-element.131.refs_4_), channel_id=1, source_target_pairs={{0,16},{8,24},{16,0},{24,8},{1,17},{9,25},{17,1},{25,9},{2,18},{10... | collective-permute-start | bytes 294920 | tf_op jit(solution)/shard_map/ppermute | solution.py:33
  127.1 4.8 %collective-permute-done.42.refs_5_ = bf16[384,128]{1,0:T(8,128)(2,1)S(1)} collective-permute-done((bf16[384,128]{1,0:T(8,128)(2,1)S(1)}, bf16[384,128]{1,0:T(8,128)(2,1)S(1)}, u32[]{:S(2)}, u32[]{:S(2)}) %collective-permute-start.42) | collective-permute-done | bytes 98336 | tf_op jit(solution)/shard_map/ppermute | solution.py:33
  138.7 2.8 %collective-permute-done.48 = bf16[400,128]{1,0:T(8,128)(2,1)S(1)} collective-permute-done((bf16[400,128]{1,0:T(8,128)(2,1)S(1)}, bf16[400,128]{1,0:T(8,128)(2,1)S(1)}, u32[]{:S(2)}, u32[]{:S(2)}) %collective-permute-start.48) | collective-permute-done | bytes 102432 | tf_op jit(solution)/shard_map/ppermute | solution.py:33
  143.7 3.3 %collective-permute-done.47.refs_8_ = bf16[384,128]{1,0:T(8,128)(2,1)S(1)} collective-permute-done((bf16[384,128]{1,0:T(8,128)(2,1)S(1)}, bf16[384,128]{1,0:T(8,128)(2,1)S(1)}, u32[]{:S(2)}, u32[]{:S(2)}) %collective-permute-start.47) | collective-permute-done | bytes 98336 | tf_op jit(solution)/shard_map/ppermute | solution.py:33
  150.5 1.8 %collective-permute-done.51 = f32[8,128]{1,0:T(8,128)S(1)} collective-permute-done((f32[8,128]{1,0:T(8,128)S(1)}, f32[8,128]{1,0:T(8,128)S(1)}, u32[]{:S(2)}, u32[]{:S(2)}) %collective-permute-start.51) | collective-permute-done | bytes 4128 | tf_op jit(solution)/shard_map/ppermute | solution.py:33
  152.3 2.0 %collective-permute-start.52 = (f32[8,128]{1,0:T(8,128)S(1)}, f32[8,128]{1,0:T(8,128)S(1)}, u32[]{:S(2)}, u32[]{:S(2)}) collective-permute-start(f32[8,128]{1,0:T(8,128)S(1)} %add.78), channel_id=1, source_target_pairs={{0,16},{8,24},{16,0},{24,8},{1,17},{9,25},{17,1},{25,9},{2,18},{10... | collective-permute-start | bytes 12296 | tf_op jit(solution)/shard_map/ppermute | solution.py:33
  (154 shorter events, 80.8 us)
Async XLA Ops:
  35.6 6.8 %collective-permute-start.13 = (f32[16,256]{1,0:T(8,128)S(1)}, f32[16,256]{1,0:T(8,128)S(1)}, u32[]{:S(2)}, u32[]{:S(2)}) collective-permute-start(f32[16,256]{1,0:T(8,128)S(1)} %max.57), channel_id=1, source_target_pairs={{0,16},{8,24},{16,0},{24,8},{1,17},{9,25},{17,1},{25,9},{2,18},{10... | collective-permute-start | bytes 49160 | tf_op jit(solution)/shard_map/ppermute | solution.py:33
  37.2 5.2 %collective-permute-start.11 = (f32[16,256]{1,0:T(8,128)S(1)}, f32[16,256]{1,0:T(8,128)S(1)}, u32[]{:S(2)}, u32[]{:S(2)}) collective-permute-start(f32[16,256]{1,0:T(8,128)S(1)} %max.55), channel_id=1, source_target_pairs={{0,2},{1,3},{2,0},{3,1},{4,6},{5,7},{6,4},{7,5},{8,10},{9,11},{10,... | collective-permute-start | bytes 49160 | tf_op jit(solution)/shard_map/ppermute | solution.py:33
  38.8 9.1 %collective-permute-start.15 = (f32[48,512]{1,0:T(8,128)S(1)}, f32[48,512]{1,0:T(8,128)S(1)}, u32[]{:S(2)}, u32[]{:S(2)}) collective-permute-start(f32[48,512]{1,0:T(8,128)S(1)} %bitcast.28), channel_id=1, source_target_pairs={{0,2},{1,3},{2,0},{3,1},{4,6},{5,7},{6,4},{7,5},{8,10},{9,11},{10,... | collective-permute-start | bytes 294920 | tf_op jit(solution)/shard_map/ppermute | solution.py:33
  39.4 13.9 %collective-permute-start.16 = (f32[48,512]{1,0:T(8,128)S(1)}, f32[48,512]{1,0:T(8,128)S(1)}, u32[]{:S(2)}, u32[]{:S(2)}) collective-permute-start(f32[48,512]{1,0:T(8,128)S(1)} %bitcast.29), channel_id=1, source_target_pairs={{0,4},{1,5},{2,6},{3,7},{4,0},{5,1},{6,2},{7,3},{8,12},{9,13},{10,... | collective-permute-start | bytes 294920 | tf_op jit(solution)/shard_map/ppermute | solution.py:33
  40.8 12.5 %collective-permute-start.17 = (f32[48,512]{1,0:T(8,128)S(1)}, f32[48,512]{1,0:T(8,128)S(1)}, u32[]{:S(2)}, u32[]{:S(2)}) collective-permute-start(f32[48,512]{1,0:T(8,128)S(1)} %bitcast.30), channel_id=1, source_target_pairs={{0,6},{1,7},{2,4},{3,5},{4,2},{5,3},{6,0},{7,1},{8,14},{9,15},{10,... | collective-permute-start | bytes 294920 | tf_op jit(solution)/shard_map/ppermute | solution.py:33
  44.1 9.2 %collective-permute-start.18 = (bf16[384,128]{1,0:T(8,128)(2,1)S(1)}, bf16[384,128]{1,0:T(8,128)(2,1)S(1)}, u32[]{:S(2)}, u32[]{:S(2)}) collective-permute-start(bf16[384,128]{1,0:T(8,128)(2,1)S(1)} %get-tuple-element.89.refs_4_), channel_id=1, source_target_pairs={{0,16},{8,24},{16,0},{24,8},{1,17},{9,25},{17,1},{25,9},{2,18},{10... | collective-permute-start | bytes 294920 | tf_op jit(solution)/shard_map/ppermute | solution.py:33
  46.5 6.9 %collective-permute-start.19 = (bf16[384,128]{1,0:T(8,128)(2,1)S(1)}, bf16[384,128]{1,0:T(8,128)(2,1)S(1)}, u32[]{:S(2)}, u32[]{:S(2)}) collective-permute-start(bf16[384,128]{1,0:T(8,128)(2,1)S(1)} %get-tuple-element.89.refs_4_), channel_id=1, source_target_pairs={{0,8},{8,0},{16,24},{24,16},{1,9},{9,1},{17,25},{25,17},{2,10},{10... | collective-permute-start | bytes 294920 | tf_op jit(solution)/shard_map/ppermute | solution.py:33
  48.0 6.4 %collective-permute-start.20 = (bf16[384,128]{1,0:T(8,128)(2,1)S(1)}, bf16[384,128]{1,0:T(8,128)(2,1)S(1)}, u32[]{:S(2)}, u32[]{:S(2)}) collective-permute-start(bf16[384,128]{1,0:T(8,128)(2,1)S(1)} %get-tuple-element.89.refs_4_), channel_id=1, source_target_pairs={{0,24},{8,16},{16,8},{24,0},{1,25},{9,17},{17,9},{25,1},{2,26},{10... | collective-permute-start | bytes 294920 | tf_op jit(solution)/shard_map/ppermute | solution.py:33
  57.5 5.0 %collective-permute-start.24 = (bf16[400,128]{1,0:T(8,128)(2,1)S(1)}, bf16[400,128]{1,0:T(8,128)(2,1)S(1)}, u32[]{:S(2)}, u32[]{:S(2)}) collective-permute-start(bf16[400,128]{1,0:T(8,128)(2,1)S(1)} %slice.76), channel_id=1, source_target_pairs={{0,4},{1,5},{2,6},{3,7},{4,0},{5,1},{6,2},{7,3},{8,12},{9,13},{10,... | collective-permute-start | bytes 307208 | tf_op jit(solution)/shard_map/ppermute | solution.py:33
  62.5 5.5 %collective-permute-start.25 = (bf16[400,128]{1,0:T(8,128)(2,1)S(1)}, bf16[400,128]{1,0:T(8,128)(2,1)S(1)}, u32[]{:S(2)}, u32[]{:S(2)}) collective-permute-start(bf16[400,128]{1,0:T(8,128)(2,1)S(1)} %get-tuple-element.145), channel_id=1, source_target_pairs={{0,2},{1,3},{2,0},{3,1},{4,6},{5,7},{6,4},{7,5},{8,10},{9,11},{10,... | collective-permute-start | bytes 307208 | tf_op jit(solution)/shard_map/ppermute | solution.py:33
  71.5 9.5 %collective-permute-start.27 = (bf16[400,128]{1,0:T(8,128)(2,1)S(1)}, bf16[400,128]{1,0:T(8,128)(2,1)S(1)}, u32[]{:S(2)}, u32[]{:S(2)}) collective-permute-start(bf16[400,128]{1,0:T(8,128)(2,1)S(1)} %get-tuple-element.103), channel_id=1, source_target_pairs={{0,16},{8,24},{16,0},{24,8},{1,17},{9,25},{17,1},{25,9},{2,18},{10... | collective-permute-start | bytes 307208 | tf_op jit(solution)/shard_map/ppermute | solution.py:33
  72.3 9.0 %collective-permute-start.28 = (bf16[400,128]{1,0:T(8,128)(2,1)S(1)}, bf16[400,128]{1,0:T(8,128)(2,1)S(1)}, u32[]{:S(2)}, u32[]{:S(2)}) collective-permute-start(bf16[400,128]{1,0:T(8,128)(2,1)S(1)} %get-tuple-element.104), channel_id=1, source_target_pairs={{0,8},{8,0},{16,24},{24,16},{1,9},{9,1},{17,25},{25,17},{2,10},{10... | collective-permute-start | bytes 307208 | tf_op jit(solution)/shard_map/ppermute | solution.py:33
  73.7 7.7 %collective-permute-start.29 = (bf16[400,128]{1,0:T(8,128)(2,1)S(1)}, bf16[400,128]{1,0:T(8,128)(2,1)S(1)}, u32[]{:S(2)}, u32[]{:S(2)}) collective-permute-start(bf16[400,128]{1,0:T(8,128)(2,1)S(1)} %get-tuple-element.105), channel_id=1, source_target_pairs={{0,24},{8,16},{16,8},{24,0},{1,25},{9,17},{17,9},{25,1},{2,26},{10... | collective-permute-start | bytes 307208 | tf_op jit(solution)/shard_map/ppermute | solution.py:33
  81.8 9.3 %collective-permute-start.30 = (bf16[384,128]{1,0:T(8,128)(2,1)S(1)}, bf16[384,128]{1,0:T(8,128)(2,1)S(1)}, u32[]{:S(2)}, u32[]{:S(2)}) collective-permute-start(bf16[384,128]{1,0:T(8,128)(2,1)S(1)} %get-tuple-element.112.refs_4_), channel_id=1, source_target_pairs={{0,16},{8,24},{16,0},{24,8},{1,17},{9,25},{17,1},{25,9},{2,18},{10... | collective-permute-start | bytes 294920 | tf_op jit(solution)/shard_map/ppermute | solution.py:33
  85.1 6.0 %collective-permute-start.31 = (bf16[384,128]{1,0:T(8,128)(2,1)S(1)}, bf16[384,128]{1,0:T(8,128)(2,1)S(1)}, u32[]{:S(2)}, u32[]{:S(2)}) collective-permute-start(bf16[384,128]{1,0:T(8,128)(2,1)S(1)} %get-tuple-element.112.refs_4_), channel_id=1, source_target_pairs={{0,8},{8,0},{16,24},{24,16},{1,9},{9,1},{17,25},{25,17},{2,10},{10... | collective-permute-start | bytes 294920 | tf_op jit(solution)/shard_map/ppermute | solution.py:33
  85.1 8.4 %collective-permute-start.32 = (bf16[384,128]{1,0:T(8,128)(2,1)S(1)}, bf16[384,128]{1,0:T(8,128)(2,1)S(1)}, u32[]{:S(2)}, u32[]{:S(2)}) collective-permute-start(bf16[384,128]{1,0:T(8,128)(2,1)S(1)} %get-tuple-element.112.refs_4_), channel_id=1, source_target_pairs={{0,24},{8,16},{16,8},{24,0},{1,25},{9,17},{17,9},{25,1},{2,26},{10... | collective-permute-start | bytes 294920 | tf_op jit(solution)/shard_map/ppermute | solution.py:33
  101.6 6.1 %collective-permute-start.37 = (bf16[400,128]{1,0:T(8,128)(2,1)S(1)}, bf16[400,128]{1,0:T(8,128)(2,1)S(1)}, u32[]{:S(2)}, u32[]{:S(2)}) collective-permute-start(bf16[400,128]{1,0:T(8,128)(2,1)S(1)} %get-tuple-element.141), channel_id=1, source_target_pairs={{0,2},{1,3},{2,0},{3,1},{4,6},{5,7},{6,4},{7,5},{8,10},{9,11},{10,... | collective-permute-start | bytes 307208 | tf_op jit(solution)/shard_map/ppermute | solution.py:33
  111.2 9.7 %collective-permute-start.39 = (bf16[400,128]{1,0:T(8,128)(2,1)S(1)}, bf16[400,128]{1,0:T(8,128)(2,1)S(1)}, u32[]{:S(2)}, u32[]{:S(2)}) collective-permute-start(bf16[400,128]{1,0:T(8,128)(2,1)S(1)} %get-tuple-element.122), channel_id=1, source_target_pairs={{0,16},{8,24},{16,0},{24,8},{1,17},{9,25},{17,1},{25,9},{2,18},{10... | collective-permute-start | bytes 307208 | tf_op jit(solution)/shard_map/ppermute | solution.py:33
  112.7 8.1 %collective-permute-start.40 = (bf16[400,128]{1,0:T(8,128)(2,1)S(1)}, bf16[400,128]{1,0:T(8,128)(2,1)S(1)}, u32[]{:S(2)}, u32[]{:S(2)}) collective-permute-start(bf16[400,128]{1,0:T(8,128)(2,1)S(1)} %get-tuple-element.123), channel_id=1, source_target_pairs={{0,8},{8,0},{16,24},{24,16},{1,9},{9,1},{17,25},{25,17},{2,10},{10... | collective-permute-start | bytes 307208 | tf_op jit(solution)/shard_map/ppermute | solution.py:33
  114.0 8.3 %collective-permute-start.41 = (bf16[400,128]{1,0:T(8,128)(2,1)S(1)}, bf16[400,128]{1,0:T(8,128)(2,1)S(1)}, u32[]{:S(2)}, u32[]{:S(2)}) collective-permute-start(bf16[400,128]{1,0:T(8,128)(2,1)S(1)} %get-tuple-element.124), channel_id=1, source_target_pairs={{0,24},{8,16},{16,8},{24,0},{1,25},{9,17},{17,9},{25,1},{2,26},{10... | collective-permute-start | bytes 307208 | tf_op jit(solution)/shard_map/ppermute | solution.py:33
  122.7 9.3 %collective-permute-start.42 = (bf16[384,128]{1,0:T(8,128)(2,1)S(1)}, bf16[384,128]{1,0:T(8,128)(2,1)S(1)}, u32[]{:S(2)}, u32[]{:S(2)}) collective-permute-start(bf16[384,128]{1,0:T(8,128)(2,1)S(1)} %get-tuple-element.131.refs_4_), channel_id=1, source_target_pairs={{0,16},{8,24},{16,0},{24,8},{1,17},{9,25},{17,1},{25,9},{2,18},{10... | collective-permute-start | bytes 294920 | tf_op jit(solution)/shard_map/ppermute | solution.py:33
  125.4 6.6 %collective-permute-start.43 = (bf16[384,128]{1,0:T(8,128)(2,1)S(1)}, bf16[384,128]{1,0:T(8,128)(2,1)S(1)}, u32[]{:S(2)}, u32[]{:S(2)}) collective-permute-start(bf16[384,128]{1,0:T(8,128)(2,1)S(1)} %get-tuple-element.131.refs_4_), channel_id=1, source_target_pairs={{0,8},{8,0},{16,24},{24,16},{1,9},{9,1},{17,25},{25,17},{2,10},{10... | collective-permute-start | bytes 294920 | tf_op jit(solution)/shard_map/ppermute | solution.py:33
  125.4 8.0 %collective-permute-start.44 = (bf16[384,128]{1,0:T(8,128)(2,1)S(1)}, bf16[384,128]{1,0:T(8,128)(2,1)S(1)}, u32[]{:S(2)}, u32[]{:S(2)}) collective-permute-start(bf16[384,128]{1,0:T(8,128)(2,1)S(1)} %get-tuple-element.131.refs_4_), channel_id=1, source_target_pairs={{0,24},{8,16},{16,8},{24,0},{1,25},{9,17},{17,9},{25,1},{2,26},{10... | collective-permute-start | bytes 294920 | tf_op jit(solution)/shard_map/ppermute | solution.py:33
  141.5 5.5 %collective-permute-start.49 = (bf16[400,128]{1,0:T(8,128)(2,1)S(1)}, bf16[400,128]{1,0:T(8,128)(2,1)S(1)}, u32[]{:S(2)}, u32[]{:S(2)}) collective-permute-start(bf16[400,128]{1,0:T(8,128)(2,1)S(1)} %get-tuple-element.137), channel_id=1, source_target_pairs={{0,2},{1,3},{2,0},{3,1},{4,6},{5,7},{6,4},{7,5},{8,10},{9,11},{10,... | collective-permute-start | bytes 307208 | tf_op jit(solution)/shard_map/ppermute | solution.py:33
  (37 other events, 255.6 us)
